TPU v7x, 512 devices: a whole 4x4x16 slice. The times are simulated.
512 devices in a mesh: dp: 32 (over z, core), ctx: 16 (over y, x).
Axes of the slice: x: 4, y: 4, z: 16, core: 2. Of those that a mesh axis runs over, the one named last changes fastest.
Arguments:
- features: bfloat16 [64, 1024, 768], P('dp', 'ctx'), may hold values from -75 to 75, as said below
- query_weight: bfloat16 [768, 256], replicated, may hold values from -0.21875 to 0.21875
- key_weight: bfloat16 [768, 256], replicated, may hold values from -0.21875 to 0.21875
- value_weight: bfloat16 [768, 768], replicated, may hold values from -0.21875 to 0.21875
- output_weight: bfloat16 [768, 768], replicated, may hold values from -0.875 to 0.875
- dilated_weight: bfloat16 [768, 1152], P('ctx'), may hold values from -0.125 to 0.125
- mixing_weight: bfloat16 [384, 768], replicated, may hold values from -0.3125 to 0.3125
- cotangent: bfloat16 [64, 1024, 768], P('dp', 'ctx'), may hold values from -0.0625 to 0.0625
Outputs:
- track_out: bfloat16 [64, 1024, 768], P('dp', 'ctx')
- dilated_grad: float32 [768, 1152], P('ctx')
Inputs may be any that keep to these rules, and one draw needn't show every extreme that they name: `features`: Real-valued activations of varying scale over bins and channels.
All inputs are finite; a program needn't handle non-finite values.
Results may differ from a plain program's by a relative error of at most 0.019.
Values may be sent and summed in bfloat16 or wider, within the bound.
No kernel may reach another device: no remote copies, remote signals or barrier semaphores. Data moves between devices by JAX's collectives and lax.ppermute only.
A program may use at most 64 MiB of HBM per device.

v0:
```python
import math

import jax
import jax.numpy as jnp
from jax import lax
from jax.sharding import PartitionSpec as P

HEADS = 4


def from_behind(value, axis, steps):
    count = lax.axis_size(axis)
    initial, last = (max(0, -steps), min(count, count - steps))
    return lax.ppermute(value, axis, [(source, source + steps) for source in range(initial, last)])


def layer_norm(values):
    center = values - jnp.mean(values, axis=-1, keepdims=True)
    spread = jnp.mean(center * center, axis=-1, keepdims=True)
    return center * lax.rsqrt(spread + 1e-05)


def head_norm(values, heads):
    shaped = values.reshape(values.shape[:-1] + (heads, values.shape[-1] // heads))
    shaped = shaped * lax.rsqrt(jnp.mean(shaped * shaped, axis=-1, keepdims=True) + 1e-06)
    return shaped.reshape(values.shape)


def gelu_exact(values):
    return jax.nn.gelu(values, approximate=False)


def gelu_slope(values):
    normal_cdf = 0.5 * (1.0 + lax.erf(values / math.sqrt(2.0)))
    normal_pdf = jnp.exp(-0.5 * values * values) / math.sqrt(2.0 * math.pi)
    return normal_cdf + values * normal_pdf


def jump(values, offset):
    return from_behind(values, "ctx", offset)


def shards(
    features,
    query_weight,
    key_weight,
    value_weight,
    output_weight,
    dilated_weight,
    mixing_weight,
    cotangent,
):
    seq_count, bin_count, channels = features.shape
    key_size = query_weight.shape[1] // HEADS
    value_size = value_weight.shape[1] // HEADS
    filter_width = dilated_weight.shape[1] // 3
    row_total = seq_count * bin_count
    token_rows = features.reshape(row_total, channels)
    normed = layer_norm(token_rows.astype(jnp.float32)).astype(jnp.bfloat16)
    queries = head_norm(
        jnp.dot(normed, query_weight, preferred_element_type=jnp.float32), HEADS
    ).astype(jnp.bfloat16)
    keys = head_norm(jnp.dot(normed, key_weight, preferred_element_type=jnp.float32), HEADS).astype(
        jnp.bfloat16
    )
    values = jnp.dot(normed, value_weight, preferred_element_type=jnp.float32).astype(jnp.bfloat16)
    query_heads = queries.reshape(seq_count, bin_count, HEADS, key_size)
    keys = keys.reshape(seq_count, bin_count, HEADS * key_size)
    values = values.reshape(seq_count, bin_count, HEADS * value_size)
    key_piece = lax.all_gather(keys, "ctx", axis=1, tiled=True)
    value_piece = lax.all_gather(values, "ctx", axis=1, tiled=True)
    amount = key_piece.shape[1]
    key_heads = key_piece.reshape(seq_count, amount, HEADS, key_size)
    value_heads = value_piece.reshape(seq_count, amount, HEADS, value_size)
    scores = (
        jnp.einsum("sqhd,skhd->shqk", query_heads, key_heads, preferred_element_type=jnp.float32)
        * 0.25
    )
    weights = jnp.exp(scores)
    total = jnp.sum(weights, axis=-1)
    summed = jnp.einsum(
        "shqk,skhv->sqhv",
        weights.astype(jnp.bfloat16),
        value_heads,
        preferred_element_type=jnp.float32,
    )
    summed, total = (summed, total)
    mixed = (
        (summed / jnp.transpose(total, (0, 2, 1))[..., None])
        .astype(jnp.bfloat16)
        .reshape(row_total, HEADS * value_size)
    )
    attended = (
        token_rows.astype(jnp.float32)
        + jnp.dot(mixed, output_weight, preferred_element_type=jnp.float32)
    ).astype(jnp.bfloat16)
    raised_input = gelu_exact(layer_norm(attended.astype(jnp.float32))).astype(jnp.bfloat16)
    lifted_seq = raised_input.reshape(seq_count, bin_count, channels)
    lower_neighbour = jump(lifted_seq, 2)
    upper_neighbour = jump(lifted_seq, -2)
    sources = (
        lower_neighbour.reshape(row_total, channels),
        raised_input,
        upper_neighbour.reshape(row_total, channels),
    )
    complete_filters = lax.all_gather(dilated_weight, "ctx", axis=0, tiled=True)
    hidden = jnp.zeros((row_total, filter_width), jnp.float32)
    for tap_index in range(3):
        hidden = hidden + jnp.dot(
            sources[tap_index],
            complete_filters[:, tap_index * filter_width : (tap_index + 1) * filter_width],
            preferred_element_type=jnp.float32,
        )
    gated = gelu_exact(hidden).astype(jnp.bfloat16)
    track_out = (
        attended.astype(jnp.float32)
        + jnp.dot(gated, mixing_weight, preferred_element_type=jnp.float32)
    ).astype(jnp.bfloat16)
    back = lax.dot_general(
        cotangent.reshape(row_total, channels),
        mixing_weight,
        (((1,), (1,)), ((), ())),
        preferred_element_type=jnp.float32,
    )
    slope = (back * gelu_slope(hidden)).astype(jnp.bfloat16)
    owned = channels // lax.axis_size("ctx")
    blocks = []
    for tap_index in range(3):
        inputs = sources[tap_index]
        blocks.append(
            lax.dot_general(
                inputs, slope, (((0,), (0,)), ((), ())), preferred_element_type=jnp.float32
            )
        )
    complete = lax.psum(jnp.concatenate(blocks, axis=1), ("dp", "ctx"))
    dilated_grad = lax.dynamic_slice_in_dim(complete, lax.axis_index("ctx") * owned, owned, 0)
    return (track_out.reshape(seq_count, bin_count, channels), dilated_grad)


def solution(mesh):
    return jax.shard_map(
        shards,
        mesh=mesh,
        in_specs=(
            P("dp", "ctx", None),
            P(),
            P(),
            P(),
            P(),
            P("ctx", None),
            P(),
            P("dp", "ctx", None),
        ),
        out_specs=(P("dp", "ctx", None), P("ctx", None)),
        check_vma=False,
    )
```

profile of v0, /device:TPU:1, one launch (start us, length us, event | category | flops | bytes accessed | tf_op | source)
XLA Modules:
  0.0 707.2 jit_solution(5632362071871800323)
XLA Ops:
  7.2 0.0 copy-start
  7.2 0.0 copy-start.1
  7.2 0.0 copy-start.3
  7.2 0.0 all-gather.6.cloned.1.call-start
  7.2 1.2 convert_reduce_fusion
  8.4 1.1 multiply_reduce_fusion.1
  9.6 1.1 multiply_convert_fusion
  10.7 1.2 copy.18
  11.8 0.0 copy-start.4
  11.9 0.3 multiply_reduce_fusion.2
  12.2 0.1 reshape.140
  12.3 0.7 copy.24
  13.0 0.0 all-gather.6.cloned.1.call-update
  13.0 0.0 all-gather.4.cloned.1.call-start
  13.1 0.1 rsqrt.37
  13.2 0.1 div.39
  13.2 0.0 copy-done.1
  13.2 0.1 fusion.19
  13.4 0.0 copy-done.3
  13.4 1.0 convolution_convert_fusion
  14.4 0.0 all-gather.4.cloned.1.call-update
  14.4 0.0 all-gather.8.cloned.1.call-start
  14.5 0.7 all-gather.8.cloned.1.call-update
  15.2 0.0 all-reduce.2.cloned.1.call-start
  15.2 0.0 copy-done.4
  15.2 0.2 copy.17
  15.4 0.3 multiply_reduce_fusion.3
  15.7 0.1 convert_element_type.72
  15.8 59.2 %all-gather.6.cloned.1.call-done = bf16[2,1024,256]{2,1,0:T(8,128)(2,1)} async-done(((bf16[2,64,256]{2,1,0:T(8,128)(2,1)}), bf16[2,1024,256]{2,1,0:T(8,128)(2,1)}) %all-gather.6.cloned.1.call-update) | async-done | bytes 1048592 | tf_op jit(solution)/shard_map/all_gather | solution.py:70
  75.1 1.5 copy.20
  76.6 1.9 fusion
  78.4 0.0 copy-start.2
  78.4 64.0 %all-gather.4.cloned.1.call-done = bf16[2,1024,768]{2,1,0:T(8,128)(2,1)} async-done(((bf16[2,64,768]{2,1,0:T(8,128)(2,1)}), bf16[2,1024,768]{2,1,0:T(8,128)(2,1)}) %all-gather.4.cloned.1.call-update) | async-done | bytes 3145744 | tf_op jit(solution)/shard_map/all_gather | solution.py:71
  142.4 4.7 copy.16
  147.1 0.0 copy-done.2
  147.1 3.0 fusion.3
  150.1 0.2 copy.22
  150.3 0.2 reshape.132
  150.5 0.0 copy-done
  150.6 0.4 fusion.107
  151.0 0.2 multiply_reduce_fusion
  151.2 1.0 fusion.17
  152.2 0.0 copy-start.5
  152.2 0.0 copy-start.6
  152.2 1.4 collective-permute-start.1
  153.7 5.5 collective-permute-start
  159.2 44.2 %all-gather.8.cloned.1.call-done = bf16[768,1152]{1,0:T(8,128)(2,1)} async-done(((bf16[48,1152]{1,0:T(8,128)(2,1)}), bf16[768,1152]{1,0:T(8,128)(2,1)}) %all-gather.8.cloned.1.call-update) | async-done | bytes 1769488 | tf_op jit(solution)/shard_map/all_gather | solution.py:106
  203.3 1.3 fusion.12
  204.7 0.0 collective-permute-done.1
  204.7 1.3 fusion.10
  206.0 0.0 collective-permute-done
  206.0 1.3 fusion.7
  207.3 0.0 copy-done.5
  207.4 0.0 copy-done.6
  207.4 0.3 fusion.35
  207.7 0.4 fusion.110
  208.1 0.4 fusion.109
  208.4 0.4 fusion.108
  208.8 2.0 pad_maximum_fusion
  210.8 0.0 all-reduce.2.cloned.1.call-update
  210.9 1.3 fusion.6
  212.2 486.1 %all-reduce.2.cloned.1.call-done = f32[768,1152]{0,1:T(8,128)} async-done(((f32[768,1152]{0,1:T(8,128)}), f32[768,1152]{0,1:T(8,128)}) %all-reduce.2.cloned.1.call-update) | async-done | bytes 3538960 | tf_op jit(solution)/shard_map/psum | solution.py:135
  698.2 1.5 constant_dynamic-slice_fusion
  699.7 0.9 copy.23
  (8 shorter events, 0.1 us)
Async XLA Ops:
  7.2 143.4 %copy-start = (bf16[768,768]{1,0:T(8,128)(2,1)S(1)}, bf16[768,768]{1,0:T(8,128)(2,1)}, u32[]{:S(2)}) copy-start(bf16[768,768]{1,0:T(8,128)(2,1)} %param.12) | copy-start | bytes 3538948
  7.2 6.1 copy-start.1
  7.2 6.2 copy-start.3
  7.2 67.9 %all-gather.6.cloned.1.call-start = ((), (), s32[]{:S(2)}) async-start(), calls=%async_computation.1 | async-start | bytes 1114112 | tf_op jit(solution)/shard_map/all_gather | solution.py:70
  11.8 3.4 copy-start.4
  13.0 129.4 %all-gather.4.cloned.1.call-start = ((), (), s32[]{:S(2)}) async-start(), calls=%async_computation | async-start | bytes 3342336 | tf_op jit(solution)/shard_map/all_gather | solution.py:71
  14.4 188.9 %all-gather.8.cloned.1.call-start = ((), (), s32[]{:S(2)}) async-start(), calls=%async_computation.2 | async-start | bytes 1880064 | tf_op jit(solution)/shard_map/all_gather | solution.py:106
  15.2 683.1 %all-reduce.2.cloned.1.call-start = ((), (), s32[]{:S(2)}) async-start(), calls=%async_computation.3 | async-start | bytes 7077888 | tf_op jit(solution)/shard_map/psum | solution.py:135
  78.4 68.7 %copy-start.2 = (f32[2,4,64,1024]{3,2,1,0:T(8,128)S(1)}, f32[2,4,64,1024]{3,2,1,0:T(8,128)}, u32[]{:S(2)}) copy-start(f32[2,4,64,1024]{3,2,1,0:T(8,128)} %get-tuple-element.11) | copy-start | bytes 6291460
  152.2 55.2 %copy-start.5 = (bf16[384,768]{1,0:T(8,128)(2,1)S(1)}, bf16[384,768]{1,0:T(8,128)(2,1)}, u32[]{:S(2)}) copy-start(bf16[384,768]{1,0:T(8,128)(2,1)} %param.14) | copy-start | bytes 1769476
  152.2 55.2 %copy-start.6 = (bf16[2,64,768]{2,1,0:T(8,128)(2,1)S(1)}, bf16[2,64,768]{2,1,0:T(8,128)(2,1)}, u32[]{:S(2)}) copy-start(bf16[2,64,768]{2,1,0:T(8,128)(2,1)} %param.15) | copy-start | bytes 589828
  152.2 52.4 %collective-permute-start.1 = (bf16[2,64,768]{2,1,0:T(8,128)(2,1)S(1)}, bf16[2,64,768]{2,1,0:T(8,128)(2,1)S(1)}, u32[]{:S(2)}, u32[]{:S(2)}) collective-permute-start(bf16[2,64,768]{2,1,0:T(8,128)(2,1)S(1)} %bitcast.62), channel_id=1, source_target_pairs={{2,0},{3,1},{4,2},{5,3},{6,4},{7,5},{8,6},{9,7},{10,8},{11,9},{12,... | collective-permute-start | bytes 589832 | tf_op jit(solution)/shard_map/ppermute | solution.py:14
  153.7 52.4 %collective-permute-start = (bf16[2,64,768]{2,1,0:T(8,128)(2,1)S(1)}, bf16[2,64,768]{2,1,0:T(8,128)(2,1)S(1)}, u32[]{:S(2)}, u32[]{:S(2)}) collective-permute-start(bf16[2,64,768]{2,1,0:T(8,128)(2,1)S(1)} %bitcast.63), channel_id=1, source_target_pairs={{0,2},{1,3},{2,4},{3,5},{4,6},{5,7},{6,8},{7,9},{8,10},{9,11},{10,... | collective-permute-start | bytes 589832 | tf_op jit(solution)/shard_map/ppermute | solution.py:14
Sparse Core Ops, SparseCore 0:
  13.2 61.8 all-gather.5
  78.7 63.7 all-gather.3
  145.4 57.8 all-gather.7
  211.0 487.2 all-reduce.1
where the time goes:
time: 708 us; the launch traced here: 707 us
  waiting for transfers between devices  654 us (92%)
  between operations  14.1 us (2%)
  matrix products  13.6 us (2%)
  local copies, waits for them, and re-layouts  11.4 us (2%)
  starting transfers between devices  7.09 us (1%)
    psum x1, waiting for transfers between devices, shards(): complete = lax.psum(jnp.concatenate(blocks, axis=1), ('dp', 'ctx'))  486 us
    all_gather x1, waiting for transfers between devices, shards(): value_piece = lax.all_gather(values, 'ctx', axis=1, tiled=True)  64 us
    all_gather x1, waiting for transfers between devices, shards(): key_piece = lax.all_gather(keys, 'ctx', axis=1, tiled=True)  59.2 us
    all_gather x1, waiting for transfers between devices, shards(): complete_filters = lax.all_gather(dilated_weight, 'ctx', axis=0, tiled=True)  44.2 us
  transfers between devices with their start and end apart: 6, of which 4 were waited for; matrix products, arithmetic and copies ran while one was open for 3% of the time, Pallas kernels for 0%

commit v1 on v0

v1 whole, which is shorter than its diff:
```python
import math

import jax
import jax.numpy as jnp
from jax import lax
from jax.sharding import PartitionSpec as P

HEADS = 4
NEAR = [[2 * (4 * far + near) + core for near in range(4)] for core in range(2) for far in range(4)]
FAR = [[2 * (4 * far + near) + core for far in range(4)] for core in range(2) for near in range(4)]


def from_behind(value, axis, steps):
    count = lax.axis_size(axis)
    initial, last = (max(0, -steps), min(count, count - steps))
    return lax.ppermute(value, axis, [(source, source + steps) for source in range(initial, last)])


def other_core(value):
    return lax.ppermute(value, "dp", [(source, source ^ 1) for source in range(32)])


def layer_norm(values):
    center = values - jnp.mean(values, axis=-1, keepdims=True)
    spread = jnp.mean(center * center, axis=-1, keepdims=True)
    return center * lax.rsqrt(spread + 1e-05)


def head_norm(values, heads):
    shaped = values.reshape(values.shape[:-1] + (heads, values.shape[-1] // heads))
    shaped = shaped * lax.rsqrt(jnp.mean(shaped * shaped, axis=-1, keepdims=True) + 1e-06)
    return shaped.reshape(values.shape)


def gelu_exact(values):
    return jax.nn.gelu(values, approximate=False)


def gelu_slope(values):
    normal_cdf = 0.5 * (1.0 + lax.erf(values / math.sqrt(2.0)))
    normal_pdf = jnp.exp(-0.5 * values * values) / math.sqrt(2.0 * math.pi)
    return normal_cdf + values * normal_pdf


def summed_over(value, groups):
    copies = jnp.broadcast_to(value[None], (4,) + value.shape)
    got = lax.all_to_all(copies, "dp", 0, 0, axis_index_groups=groups)
    return jnp.sum(got.astype(jnp.float32), axis=0).astype(jnp.bfloat16)


def shards(
    features,
    query_weight,
    key_weight,
    value_weight,
    output_weight,
    dilated_weight,
    mixing_weight,
    cotangent,
):
    f32, bf16 = jnp.float32, jnp.bfloat16
    complete_filters = lax.all_gather(dilated_weight, "ctx", axis=0, tiled=True)
    token_rows = features.reshape(128, 768)
    normed = layer_norm(token_rows.astype(f32)).astype(bf16)
    queries = head_norm(jnp.dot(normed, query_weight, preferred_element_type=f32), HEADS)
    queries = queries.astype(bf16)
    keys = head_norm(jnp.dot(normed, key_weight, preferred_element_type=f32), HEADS).astype(bf16)
    values = jnp.dot(normed, value_weight, preferred_element_type=f32).astype(bf16)
    q = queries.reshape(2, 2, 2, 16, 4, 64).transpose(0, 4, 1, 3, 2, 5).reshape(16, 16, 128)
    k = keys.reshape(2, 64, 4, 64).transpose(0, 2, 1, 3)
    v = values.reshape(2, 64, 4, 192).transpose(0, 2, 1, 3)
    kv = jnp.concatenate([k, v], axis=-1)
    kv = jnp.concatenate([kv[..., :128], kv[..., 128:]], axis=2)
    kv = jnp.broadcast_to(kv[:, :, None], (2, 4, 2, 128, 128)).reshape(16, 128, 128)
    got = lax.all_to_all(jnp.concatenate([kv, q], axis=1), "ctx", 0, 0)
    low, high = got[:, :64].reshape(1024, 128), got[:, 64:128].reshape(1024, 128)
    query = got[:, 128:].reshape(256, 128)
    query = jnp.concatenate([query[:, :64], query[:, 64:]], axis=0)
    key = low[:, :64]
    value = jnp.concatenate([low[:, 64:], high], axis=1)
    scores = 0.25 * lax.dot_general(
        query, key, (((1,), (1,)), ((), ())), preferred_element_type=f32
    )
    weights = jnp.exp(scores)
    total = jnp.sum(weights, axis=-1, keepdims=True)
    summed = jnp.dot(weights.astype(bf16), value, preferred_element_type=f32)
    mixed = (summed / total).astype(bf16)
    mixed = mixed.reshape(2, 16, 16, 192).transpose(1, 2, 0, 3).reshape(16, 16, 384)
    mixed = lax.all_to_all(mixed, "ctx", 0, 0)
    mixed = mixed.reshape(2, 4, 2, 16, 2, 192).transpose(0, 2, 4, 3, 1, 5).reshape(128, 768)
    attended = (
        token_rows.astype(f32) + jnp.dot(mixed, output_weight, preferred_element_type=f32)
    ).astype(bf16)
    raised_input = gelu_exact(layer_norm(attended.astype(f32))).astype(bf16)
    lifted_seq = raised_input.reshape(2, 64, 768)
    sources = (
        from_behind(lifted_seq, "ctx", 2).reshape(128, 768),
        raised_input,
        from_behind(lifted_seq, "ctx", -2).reshape(128, 768),
    )
    hidden = jnp.zeros((128, 384), f32)
    for tap in (1, 0, 2):
        hidden = hidden + jnp.dot(
            sources[tap],
            complete_filters[:, tap * 384 : (tap + 1) * 384],
            preferred_element_type=f32,
        )
    gated = gelu_exact(hidden).astype(bf16)
    track_out = (
        attended.astype(f32) + jnp.dot(gated, mixing_weight, preferred_element_type=f32)
    ).astype(bf16)
    back = lax.dot_general(
        cotangent.reshape(128, 768),
        mixing_weight,
        (((1,), (1,)), ((), ())),
        preferred_element_type=f32,
    )
    slope = (back * gelu_slope(hidden)).astype(bf16)
    core = lax.axis_index("dp") % 2
    parts = []
    for tap in range(3):
        parts.append(
            lax.dot_general(
                sources[tap], slope, (((0,), (0,)), ((), ())), preferred_element_type=f32
            )
        )
    grad = jnp.concatenate(parts, axis=1).astype(bf16).reshape(16, 2, 24, 1152)
    mine = lax.dynamic_index_in_dim(grad, core, 1, keepdims=False)
    theirs = lax.dynamic_index_in_dim(grad, 1 - core, 1, keepdims=False)
    grad = (mine.astype(f32) + other_core(theirs).astype(f32)).astype(bf16)
    grad = lax.all_to_all(grad, "ctx", 0, 0)
    grad = jnp.sum(grad.astype(f32), axis=0).astype(bf16)
    grad = summed_over(summed_over(grad, NEAR), FAR)
    rest = other_core(grad)
    first, second = jnp.where(core == 0, grad, rest), jnp.where(core == 0, rest, grad)
    dilated_grad = jnp.concatenate([first, second], axis=0).astype(f32)
    return (track_out.reshape(2, 64, 768), dilated_grad)


def solution(mesh):
    return jax.shard_map(
        shards,
        mesh=mesh,
        in_specs=(
            P("dp", "ctx", None),
            P(),
            P(),
            P(),
            P(),
            P("ctx", None),
            P(),
            P("dp", "ctx", None),
        ),
        out_specs=(P("dp", "ctx", None), P("ctx", None)),
        check_vma=False,
    )
```

time: 708 us -> 162 us (0.23)
  waiting for transfers between devices: 654 us -> 36.7 us
  blocking collectives: 0 us -> 58 us
  starting transfers between devices: 7.09 us -> 28.2 us
    psum x1 -> x0, waiting for transfers between devices: 486 us -> none  [shards(): complete = lax.psum(jnp.concatenate(blocks, axis=1), ('dp', 'ctx'))]
    all_gather x2 -> x0, waiting for transfers between devices: 123 us -> none  [the longest x1 64 us: shards(): value_piece = lax.all_gather(values, 'ctx', axis=1, tiled=True)]
    all_to_all x0 -> x4, blocking collectives: none -> 58 us  [the longest x1 19.4 us: shards(): grad = lax.all_to_all(grad, 'ctx', 0, 0)]
    all_gather x1, waiting for transfers between devices: 44.2 us -> 16.2 us  [shards(): complete_filters = lax.all_gather(dilated_weight, 'ctx', axis=0, tiled=True)]
    all_to_all x0 -> x1, waiting for transfers between devices: none -> 15.1 us  [summed_over(): got = lax.all_to_all(copies, 'dp', 0, 0, axis_index_groups=groups)]
    all_to_all x0 -> x1, starting transfers between devices: none -> 11 us  [summed_over(): got = lax.all_to_all(copies, 'dp', 0, 0, axis_index_groups=groups)]
    ppermute x0 -> x2, starting transfers between devices: none -> 10.3 us  [other_core(): lax.ppermute(value, 'dp', [(source, source ^ 1) for source in range(32)])]
  transfers between devices with their start and end apart: 6 -> 6, of which waited for: 4 -> 5; matrix products, arithmetic and copies ran while one was open for 3% -> 9% of each run, Pallas kernels for 0% -> 0%
where the time goes in v1:
time: 162 us; the launch traced here: 161 us
  blocking collectives  58 us (36%)
  waiting for transfers between devices  36.7 us (23%)
  starting transfers between devices  28.2 us (17%)
  between operations  14.5 us (9%)
  matrix products  9.24 us (6%)
  other arithmetic  7.38 us (5%)
  local copies, waits for them, and re-layouts  7.13 us (4%)
    all_to_all x1, blocking collectives, shards(): grad = lax.all_to_all(grad, 'ctx', 0, 0)  19.4 us
    all_to_all x1, blocking collectives, shards(): got = lax.all_to_all(jnp.concatenate([kv, q], axis=1), 'ctx', 0, 0)  17.6 us
    all_gather x1, waiting for transfers between devices, shards(): complete_filters = lax.all_gather(dilated_weight, 'ctx', axis=0, tiled=True)  16.2 us
    all_to_all x1, waiting for transfers between devices, summed_over(): got = lax.all_to_all(copies, 'dp', 0, 0, axis_index_groups=groups)  15.1 us
    all_to_all x1, starting transfers between devices, summed_over(): got = lax.all_to_all(copies, 'dp', 0, 0, axis_index_groups=groups)  11 us
    all_to_all x1, blocking collectives, shards(): mixed = lax.all_to_all(mixed, 'ctx', 0, 0)  10.8 us
    ppermute x2, starting transfers between devices, other_core(): lax.ppermute(value, 'dp', [(source, source ^ 1) for source in range(32)])  10.3 us
    all_to_all x1, blocking collectives, summed_over(): got = lax.all_to_all(copies, 'dp', 0, 0, axis_index_groups=groups)  10.2 us
  transfers between devices with their start and end apart: 6, of which 5 were waited for; matrix products, arithmetic and copies ran while one was open for 9% of the time, Pallas kernels for 0%

profile of v1, /device:TPU:1, one launch (start us, length us, event | category | flops | bytes accessed | tf_op | source)
XLA Modules:
  0.0 161.2 jit_solution(16007798112097170368)
XLA Ops:
  7.2 0.7 all-gather.2.cloned.1.call-update
  7.9 1.1 convert_reduce_fusion
  9.0 1.1 multiply_reduce_fusion.1
  10.1 1.1 multiply_convert_fusion
  11.2 0.1 rsqrt.38
  11.3 0.1 div.41
  11.4 1.2 copy.30
  12.6 0.3 multiply_reduce_fusion.2
  12.9 0.1 fusion.20
  13.0 0.3 convolution_convert_fusion.3
  13.3 0.2 reshape.159
  13.6 1.2 copy.27
  14.8 0.3 multiply_reduce_fusion.3
  15.1 0.1 convert_element_type.93
  15.2 0.2 copy.28
  15.3 0.1 slice.48
  15.5 0.2 fusion.30
  15.7 0.1 copy.31
  15.9 0.1 copy.32
  16.0 0.1 reshape.161
  16.2 0.1 broadcast_in_dim.6
  16.3 17.6 %all_to_all.25 = bf16[16,144,128]{2,1,0:T(8,128)(2,1)S(1)} all-to-all(bf16[16,144,128]{2,1,0:T(8,128)(2,1)S(1)} %pad_maximum_fusion.1), channel_id=1, replica_groups=mesh['dp'=32,'ctx'=16] {'ctx'}, dimensions={0} | all-to-all | bytes 1179648 | tf_op jit(solution)/shard_map/all_to_all | solution.py:75
  34.0 0.1 slice.54
  34.1 0.1 fusion.117
  34.2 0.5 fusion
  34.8 0.8 fusion.3
  35.5 0.1 copy.33
  35.7 0.3 copy.34
  36.0 0.2 reshape.166
  36.1 10.8 %all_to_all.26 = bf16[16,16,384]{2,1,0:T(8,128)(2,1)S(1)} all-to-all(bf16[16,16,384]{2,1,0:T(8,128)(2,1)S(1)} %reshape.166), channel_id=1, replica_groups=mesh['dp'=32,'ctx'=16] {'ctx'}, dimensions={0} | all-to-all | bytes 393216 | tf_op jit(solution)/shard_map/all_to_all | solution.py:89
  46.9 0.2 reshape.167
  47.1 0.2 copy.40
  47.3 0.2 reshape.168
  47.5 0.4 fusion.118
  48.0 0.2 multiply_reduce_fusion
  48.2 1.0 fusion.18
  49.2 1.3 collective-permute-start.1
  50.5 5.5 %collective-permute-start = (bf16[2,64,768]{2,1,0:T(8,128)(2,1)S(1)}, bf16[2,64,768]{2,1,0:T(8,128)(2,1)S(1)}, u32[]{:S(2)}, u32[]{:S(2)}) collective-permute-start(bf16[2,64,768]{2,1,0:T(8,128)(2,1)S(1)} %bitcast.81), channel_id=1, source_target_pairs={{0,2},{1,3},{2,4},{3,5},{4,6},{5,7},{6,8},{7,9},{8,10},{9,11},{10,... | collective-permute-start | bytes 589832 | tf_op jit(solution)/shard_map/ppermute | solution.py:16
  56.0 1.1 collective-permute-done.1
  57.1 0.2 copy.37
  57.3 1.3 collective-permute-done
  58.6 0.2 copy.36
  58.8 16.2 %all-gather.2.cloned.1.call-done = bf16[768,1152]{1,0:T(8,128)(2,1)} async-done(((bf16[48,1152]{1,0:T(8,128)(2,1)}), bf16[768,1152]{1,0:T(8,128)(2,1)}) %all-gather.2.cloned.1.call-update) | async-done | bytes 1769488 | tf_op jit(solution)/shard_map/all_gather | solution.py:62
  74.9 1.3 fusion.11
  76.2 1.3 convolution_add_fusion.3
  77.6 1.3 convolution_add_fusion.2
  79.0 0.3 fusion.39
  79.3 0.3 convolution_convert_fusion.1
  79.6 0.3 convolution_convert_fusion
  80.0 0.4 convolution_convert_fusion.2
  80.3 0.2 pad_maximum_fusion
  80.5 1.0 dynamic-slice_bitcast_fusion
  81.5 3.9 %collective-permute-start.2 = (bf16[16,24,1152]{2,1,0:T(8,128)(2,1)}, bf16[16,24,1152]{2,1,0:T(8,128)(2,1)}, u32[]{:S(2)}, u32[]{:S(2)}) collective-permute-start(bf16[16,24,1152]{2,1,0:T(8,128)(2,1)} %dynamic-slice_bitcast_fusion), channel_id=1, source_target_pairs={{0,16},{16,0},{32,48},{48,32},{64,80},{80,64},{96,112},{112,96},{1... | collective-permute-start | bytes 2654216 | tf_op jit(solution)/shard_map/ppermute | solution.py:20
  85.4 2.4 %collective-permute-done.2 = bf16[16,24,1152]{2,1,0:T(8,128)(2,1)} collective-permute-done((bf16[16,24,1152]{2,1,0:T(8,128)(2,1)}, bf16[16,24,1152]{2,1,0:T(8,128)(2,1)}, u32[]{:S(2)}, u32[]{:S(2)}) %collective-permute-start.2) | collective-permute-done | bytes 884768 | tf_op jit(solution)/shard_map/ppermute | solution.py:20
  87.8 1.4 fusion.2
  89.2 19.4 %all_to_all.27 = bf16[16,24,1152]{2,1,0:T(8,128)(2,1)S(1)} all-to-all(bf16[16,24,1152]{2,1,0:T(8,128)(2,1)S(1)} %fusion.2), channel_id=1, replica_groups=mesh['dp'=32,'ctx'=16] {'ctx'}, dimensions={0} | all-to-all | bytes 1769472 | tf_op jit(solution)/shard_map/all_to_all | solution.py:131
  108.6 0.1 reduce_sum.106
  108.7 10.2 %all_to_all.28 = bf16[4,24,1152]{2,1,0:T(8,128)(2,1)S(1)} all-to-all(bf16[4,24,1152]{2,1,0:T(8,128)(2,1)S(1)} %broadcast_in_dim.7), channel_id=1, replica_groups={{0,32,64,96},{128,160,192,224},{256,288,320,352},{384,416,448,480},{16,..., dimensions={0} | all-to-all | bytes 442368 | tf_op jit(solution)/shard_map/all_to_all | solution.py:47
  118.9 0.7 broadcast_in_dim.8
  119.6 11.0 %all-to-all-start.4 = ((bf16[4,24,1152]{2,1,0:T(8,128)(2,1)}), bf16[4,24,1152]{2,1,0:T(8,128)(2,1)S(1)}, u32[]{:S(2)}, u32[]{:S(2)}) async-start(bf16[4,24,1152]{2,1,0:T(8,128)(2,1)} %broadcast_in_dim.8), calls=%async_computation.4 | async-start | bytes 442368 | tf_op jit(solution)/shard_map/all_to_all | solution.py:47
  130.7 15.1 %all-to-all-done.4 = bf16[4,24,1152]{2,1,0:T(8,128)(2,1)S(1)} async-done(((bf16[4,24,1152]{2,1,0:T(8,128)(2,1)}), bf16[4,24,1152]{2,1,0:T(8,128)(2,1)S(1)}, u32[]{:S(2)}, u32[]{:S(2)}) %all-to-all-start.4) | async-done | bytes 221216 | tf_op jit(solution)/shard_map/all_to_all | solution.py:47
  145.8 6.5 %collective-permute-start.3 = (bf16[24,1152]{1,0:T(8,128)(2,1)S(1)}, bf16[24,1152]{1,0:T(8,128)(2,1)S(1)}, u32[]{:S(2)}, u32[]{:S(2)}) collective-permute-start(bf16[24,1152]{1,0:T(8,128)(2,1)S(1)} %reduce_sum.108), channel_id=1, source_target_pairs={{0,16},{16,0},{32,48},{48,32},{64,80},{80,64},{96,112},{112,96},{1... | collective-permute-start | bytes 165896 | tf_op jit(solution)/shard_map/ppermute | solution.py:20
  152.3 1.3 fusion.6
  153.7 0.7 maximum_convert_fusion
  (34 shorter events, 0.4 us)
Async XLA Ops:
  7.2 40.4 %copy-start = (bf16[768,768]{1,0:T(8,128)(2,1)S(1)}, bf16[768,768]{1,0:T(8,128)(2,1)}, u32[]{:S(2)}) copy-start(bf16[768,768]{1,0:T(8,128)(2,1)} %param.12) | copy-start | bytes 3538948
  7.2 5.7 %copy-start.1 = (bf16[2,64,768]{2,1,0:T(8,128)(2,1)S(1)}, bf16[2,64,768]{2,1,0:T(8,128)(2,1)}, u32[]{:S(2)}) copy-start(bf16[2,64,768]{2,1,0:T(8,128)(2,1)} %param.8) | copy-start | bytes 589828
  7.2 5.8 %copy-start.2 = (bf16[768,768]{1,0:T(8,128)(2,1)S(1)}, bf16[768,768]{1,0:T(8,128)(2,1)}, u32[]{:S(2)}) copy-start(bf16[768,768]{1,0:T(8,128)(2,1)} %param.11) | copy-start | bytes 3538948
  7.2 67.7 %all-gather.2.cloned.1.call-start = ((), (), s32[]{:S(2)}) async-start(), calls=%async_computation.5 | async-start | bytes 1880064 | tf_op jit(solution)/shard_map/all_gather | solution.py:62
  49.2 7.9 %collective-permute-start.1 = (bf16[2,64,768]{2,1,0:T(8,128)(2,1)S(1)}, bf16[2,64,768]{2,1,0:T(8,128)(2,1)S(1)}, u32[]{:S(2)}, u32[]{:S(2)}) collective-permute-start(bf16[2,64,768]{2,1,0:T(8,128)(2,1)S(1)} %bitcast.80), channel_id=1, source_target_pairs={{2,0},{3,1},{4,2},{5,3},{6,4},{7,5},{8,6},{9,7},{10,8},{11,9},{12,... | collective-permute-start | bytes 589832 | tf_op jit(solution)/shard_map/ppermute | solution.py:16
  50.5 8.1 %collective-permute-start = (bf16[2,64,768]{2,1,0:T(8,128)(2,1)S(1)}, bf16[2,64,768]{2,1,0:T(8,128)(2,1)S(1)}, u32[]{:S(2)}, u32[]{:S(2)}) collective-permute-start(bf16[2,64,768]{2,1,0:T(8,128)(2,1)S(1)} %bitcast.81), channel_id=1, source_target_pairs={{0,2},{1,3},{2,4},{3,5},{4,6},{5,7},{6,8},{7,9},{8,10},{9,11},{10,... | collective-permute-start | bytes 589832 | tf_op jit(solution)/shard_map/ppermute | solution.py:16
  58.7 20.2 %copy-start.5 = (bf16[384,768]{1,0:T(8,128)(2,1)S(1)}, bf16[384,768]{1,0:T(8,128)(2,1)}, u32[]{:S(2)}) copy-start(bf16[384,768]{1,0:T(8,128)(2,1)} %param.14) | copy-start | bytes 1769476
  58.8 20.2 %copy-start.7 = (bf16[2,64,768]{2,1,0:T(8,128)(2,1)S(1)}, bf16[2,64,768]{2,1,0:T(8,128)(2,1)}, u32[]{:S(2)}) copy-start(bf16[2,64,768]{2,1,0:T(8,128)(2,1)} %param.15) | copy-start | bytes 589828
  78.9 1.4 copy-start.3
  81.5 6.3 %collective-permute-start.2 = (bf16[16,24,1152]{2,1,0:T(8,128)(2,1)}, bf16[16,24,1152]{2,1,0:T(8,128)(2,1)}, u32[]{:S(2)}, u32[]{:S(2)}) collective-permute-start(bf16[16,24,1152]{2,1,0:T(8,128)(2,1)} %dynamic-slice_bitcast_fusion), channel_id=1, source_target_pairs={{0,16},{16,0},{32,48},{48,32},{64,80},{80,64},{96,112},{112,96},{1... | collective-permute-start | bytes 2654216 | tf_op jit(solution)/shard_map/ppermute | solution.py:20
  108.6 43.8 %copy-start.4 = (f32[128,384]{1,0:T(8,128)S(1)}, f32[128,384]{1,0:T(8,128)}, u32[]{:S(2)}) copy-start(f32[128,384]{1,0:T(8,128)} %copy-done.3) | copy-start | bytes 589828
  108.6 43.8 %copy-start.6 = (bf16[384,768]{1,0:T(8,128)(2,1)S(1)}, bf16[384,768]{1,0:T(8,128)(2,1)}, u32[]{:S(2)}) copy-start(bf16[384,768]{1,0:T(8,128)(2,1)} %param.14) | copy-start | bytes 1769476
  119.6 26.2 %all-to-all-start.4 = ((bf16[4,24,1152]{2,1,0:T(8,128)(2,1)}), bf16[4,24,1152]{2,1,0:T(8,128)(2,1)S(1)}, u32[]{:S(2)}, u32[]{:S(2)}) async-start(bf16[4,24,1152]{2,1,0:T(8,128)(2,1)} %broadcast_in_dim.8), calls=%async_computation.4 | async-start | bytes 442368 | tf_op jit(solution)/shard_map/all_to_all | solution.py:47
  145.8 7.8 %collective-permute-start.3 = (bf16[24,1152]{1,0:T(8,128)(2,1)S(1)}, bf16[24,1152]{1,0:T(8,128)(2,1)S(1)}, u32[]{:S(2)}, u32[]{:S(2)}) collective-permute-start(bf16[24,1152]{1,0:T(8,128)(2,1)S(1)} %reduce_sum.108), channel_id=1, source_target_pairs={{0,16},{16,0},{32,48},{48,32},{64,80},{80,64},{96,112},{112,96},{1... | collective-permute-start | bytes 165896 | tf_op jit(solution)/shard_map/ppermute | solution.py:20
Sparse Core Ops, SparseCore 0:
  11.1 63.8 all-gather.1

commit v2 on v1

v2 whole, which is shorter than its diff:
```python
import math

import jax
import jax.numpy as jnp
import numpy as np
from jax import lax
from jax.experimental import pallas as pl
from jax.experimental.pallas import tpu as pltpu
from jax.sharding import PartitionSpec as P


NEAR = [[2 * (4 * far + near) + core for near in range(4)] for core in range(2) for far in range(4)]
FAR = [[2 * (4 * far + near) + core for far in range(4)] for core in range(2) for near in range(4)]
F32, BF16 = jnp.float32, jnp.bfloat16
PARAMS = pltpu.CompilerParams(vmem_limit_bytes=50 * 1024 * 1024)
VMEM = pl.BlockSpec(memory_space=pltpu.VMEM)
SMEM = pl.BlockSpec(memory_space=pltpu.SMEM)


def dot(a, b, dims=((1,), (0,))):
    return lax.dot_general(a, b, (dims, ((), ())), preferred_element_type=F32)


def moves(count, source):
    row = lax.broadcasted_iota(jnp.int32, (count, count), 0)
    column = lax.broadcasted_iota(jnp.int32, (count, count), 1)
    return jnp.where(source(row, column), 1.0, 0.0).astype(BF16)


def layer_norm(values):
    center = values - jnp.mean(values, axis=-1, keepdims=True)
    spread = jnp.mean(center * center, axis=-1, keepdims=True)
    return center * lax.rsqrt(spread + 1e-05)


def head_norm(values):
    row = lax.broadcasted_iota(jnp.int32, (256, 256), 0)
    column = lax.broadcasted_iota(jnp.int32, (256, 256), 1)
    same = jnp.where((row >> 6) == (column >> 6), 1.0 / 64.0, 0.0).astype(F32)
    mean = lax.dot_general(
        values * values,
        same,
        (((1,), (0,)), ((), ())),
        precision=lax.Precision.HIGHEST,
        preferred_element_type=F32,
    )
    return values * lax.rsqrt(mean + 1e-06)


def normal_cdf(values):
    return 0.5 * (1.0 + lax.erf(values * (1.0 / math.sqrt(2.0))))


def swap(tile):
    return pltpu.roll(tile, 64, 1)


def lower_lanes(rows):
    return lax.broadcasted_iota(jnp.int32, (rows, 128), 1) < 64


def front(core, x, wq, wk, wv, wd, mix, cot, message):
    own = x[...]
    normed = layer_norm(own.astype(F32)).astype(BF16)
    q = head_norm(dot(normed, wq[...]))
    k = head_norm(dot(normed, wk[...]))
    v = dot(normed, wv[...])
    to_queries = moves(128, lambda r, c: c == ((r >> 6) * 64 + ((r >> 1) & 15) * 4 + ((r >> 5) & 1) * 2 + (r & 1)))
    q = dot(to_queries, q.astype(BF16))
    low16, low64 = lower_lanes(16), lower_lanes(64)
    for s in range(2):
        rows = slice(64 * s, 64 * s + 64)
        for pair in range(2):
            key = k[rows, 128 * pair : 128 * pair + 128]
            left, middle, right = (v[rows, 384 * pair + 128 * t : 384 * pair + 128 * t + 128] for t in range(3))
            for odd in range(2):
                first = jnp.where(low64, swap(key) if odd else key, middle if odd else swap(middle))
                block = jnp.concatenate([first, right if odd else left], axis=0).astype(BF16)
                for half in range(2):
                    message[8 * s + 4 * pair + 2 * odd + half, 0:128, :] = block
            for half in range(2):
                start = 64 * s + 32 * half
                a = q[start : start + 16, 128 * pair : 128 * pair + 128]
                b = q[start + 16 : start + 32, 128 * pair : 128 * pair + 128]
                message[8 * s + 4 * pair + half, 128:144, :] = jnp.where(low16, a, swap(b)).astype(BF16)
                message[8 * s + 4 * pair + 2 + half, 128:144, :] = jnp.where(low16, swap(a), b).astype(BF16)
    to_bins = moves(128, lambda r, c: c == (((r >> 2) & 1) * 64 + (r >> 3) * 4 + (r & 3)))
    sent = dot(to_bins, own)
    back = dot(dot(to_bins, cot[...]).astype(BF16), mix[...], ((1,), (1,)))
    filters = wd[...].astype(F32)
    filters = jnp.where(core[0] == 0, filters[0:24], filters[24:48])
    for j in range(16):
        rows = slice(8 * j, 8 * j + 8)
        slab = jnp.concatenate([sent[rows], back[rows]], axis=1)
        slab = jnp.concatenate([slab, filters], axis=0).astype(BF16)
        for t in range(9):
            message[j, 144 + 32 * t : 176 + 32 * t, :] = slab[:, 128 * t : 128 * t + 128]


def attention(got, out, filters, sent):
    low = got[:, 0:64, :].reshape(1024, 128)
    high = got[:, 64:128, :].reshape(1024, 128)
    value = jnp.concatenate([low, high], axis=1)
    query = got[:, 128:144, :].reshape(256, 128)
    by_bins = moves(256, lambda r, c: c == (((r >> 1) & 15) * 16 + (r >> 5) * 2 + (r & 1)))
    query = dot(by_bins, query) * 0.25
    is_low = lower_lanes(256)
    queries = (jnp.where(is_low, query, 0.0).astype(BF16), jnp.where(is_low, swap(query), 0.0).astype(BF16))
    low16 = lower_lanes(16)
    for block in range(4):
        rows = queries[block // 2][128 * (block % 2) : 128 * (block % 2) + 128]
        weights = jnp.exp(dot(rows, low, ((1,), (1,))))
        total = jnp.sum(weights, axis=-1, keepdims=True)
        mixed = dot(weights.astype(BF16), value) / total
        for j in range(4):
            part = mixed[32 * j : 32 * j + 32]
            first = jnp.where(low16, swap(part[16:32, 0:128]), part[0:16, 0:128])
            out[4 * block + j] = jnp.concatenate([first, part[:, 128:256]], axis=0).astype(BF16)
    to_groups = moves(128, lambda r, c: c == (((r >> 1) & 15) * 8 + (r >> 5) * 2 + (r & 1)))
    for t in range(9):
        lanes = slice(128 * t, 128 * t + 128)
        pieces = [got[i, 144 + 32 * t : 176 + 32 * t, :].astype(F32) for i in range(16)]
        filters[:, lanes] = jnp.concatenate([p[8:32] for p in pieces], axis=0).astype(BF16)
        rows = jnp.concatenate([p[0:8] for p in pieces], axis=0).astype(BF16)
        sent[:, lanes] = dot(to_groups, rows).astype(BF16)


def middle(core, got, sent, wo, filters, others, order, attended, gated, mine, theirs):
    low16 = lower_lanes(16)
    tiles = []
    for pair in range(2):
        groups = [[], [], []]
        for s in range(2):
            for half in range(2):
                even, odd = (got[8 * s + 4 * pair + 2 * o + half].astype(F32) for o in range(2))
                e, o = even[0:16], odd[0:16]
                groups[0].append(even[16:48])
                groups[1] += [jnp.where(low16, swap(e), o), jnp.where(low16, e, swap(o))]
                groups[2].append(odd[16:48])
        tiles += [jnp.concatenate(g, axis=0) for g in groups]
    mixed = jnp.concatenate(tiles, axis=1).astype(BF16)
    result = (sent[:, 0:768].astype(F32) + dot(mixed, wo[...])).astype(BF16)
    attended[...] = result
    normed = layer_norm(result.astype(F32))
    lifted = (normed * normal_cdf(normed)).astype(BF16)
    lifted = dot(lifted, order[...])
    first, second = lifted[:, 0:384], lifted[:, 384:768]
    lifted = (
        jnp.where(core[0] == 0, first, second).astype(BF16),
        jnp.where(core[0] == 0, second, first).astype(BF16),
    )
    from_below = moves(128, lambda r, c: (c == r - 4) & ((r & 31) >= 4))
    from_above = moves(128, lambda r, c: (c == r + 4) & ((r & 31) < 28))
    weights = (filters, others)
    hidden = jnp.zeros((128, 384), F32)
    for part in range(2):
        below = dot(from_below, lifted[part]).astype(BF16)
        above = dot(from_above, lifted[part]).astype(BF16)
        for tap, rows in enumerate((below, lifted[part], above)):
            hidden = hidden + dot(rows, weights[part][:, 384 * tap : 384 * tap + 384])
    cdf = normal_cdf(hidden)
    gated[...] = (hidden * cdf).astype(BF16)
    pdf = jnp.exp(-0.5 * hidden * hidden) * (1.0 / math.sqrt(2.0 * math.pi))
    slope = (sent[:, 768:1152].astype(F32) * (cdf + hidden * pdf)).astype(BF16)
    slopes = (dot(from_above, slope).astype(BF16), slope, dot(from_below, slope).astype(BF16))
    for part, target in ((1, theirs), (0, mine)):
        for tap in range(3):
            target[:, 384 * tap : 384 * tap + 384] = dot(lifted[part], slopes[tap], ((0,), (0,))).astype(BF16)


def mixing(attended, gated, mix, track):
    result = (attended[...].astype(F32) + dot(gated[...], mix[...])).astype(BF16)
    by_block = moves(128, lambda r, c: c == (((r >> 1) & 3) * 32 + (r >> 3) * 2 + (r & 1)))
    track[...] = dot(by_block, result).astype(BF16)


def joined(mine, came, track, message):
    blank = jnp.zeros((8, 384), F32)
    for d in range(16):
        rows = slice(24 * d, 24 * d + 24)
        grad = mine[rows].astype(F32) + came[rows].astype(F32)
        top = jnp.concatenate([track[8 * d : 8 * d + 8].astype(F32), blank], axis=1)
        message[d] = jnp.concatenate([top, grad], axis=0).astype(BF16)


def summed(got, grad, track):
    total = got[0].astype(F32)
    rows = [total[0:8, 0:768]]
    for d in range(1, 16):
        block = got[d].astype(F32)
        rows.append(block[0:8, 0:768])
        total = total + block
    total = total[8:32].astype(BF16)
    for copy in range(4):
        grad[copy] = total
    natural = moves(128, lambda r, c: c == (((r >> 2) & 15) * 8 + (r >> 6) * 4 + (r & 3)))
    result = dot(natural, jnp.concatenate(rows, axis=0).astype(BF16))
    track[...] = result.astype(BF16)


def summed_again(got, grad):
    total = got[0].astype(F32) + got[1].astype(F32) + got[2].astype(F32) + got[3].astype(F32)
    total = total.astype(BF16)
    if len(grad.shape) == 3:
        for copy in range(grad.shape[0]):
            grad[copy] = total
    else:
        grad[...] = total


def call(kernel, outs, *args):
    return pl.pallas_call(
        kernel,
        out_shape=[jax.ShapeDtypeStruct(shape, BF16) for shape in outs],
        in_specs=[SMEM if a.dtype == jnp.int32 else VMEM for a in args],
        out_specs=[VMEM] * len(outs),
        compiler_params=PARAMS,
    )(*args)


def other_core(value):
    return lax.ppermute(value, "dp", [(source, source ^ 1) for source in range(32)])


def column_order():
    order = np.zeros((768, 768), np.float32)
    target = np.arange(768)
    order[(target % 384) // 24 * 48 + target // 384 * 24 + target % 24, target] = 1.0
    return jnp.asarray(order, BF16)


def shards(
    features,
    query_weight,
    key_weight,
    value_weight,
    output_weight,
    dilated_weight,
    mixing_weight,
    cotangent,
):
    core = lax.axis_index("dp") % 2
    flag = core.astype(jnp.int32).reshape(1)
    (message,) = call(
        front,
        [(16, 432, 128)],
        flag,
        features.reshape(128, 768),
        query_weight,
        key_weight,
        value_weight,
        dilated_weight,
        mixing_weight,
        cotangent.reshape(128, 768),
    )
    got = lax.all_to_all(message, "ctx", 0, 0)
    mixed, filters, sent = call(attention, [(16, 48, 128), (384, 1152), (128, 1152)], got)
    others = other_core(filters)
    got = lax.all_to_all(mixed, "ctx", 0, 0)
    attended, gated, mine, theirs = call(
        middle,
        [(128, 768), (128, 384), (384, 1152), (384, 1152)],
        flag,
        got,
        sent,
        output_weight,
        filters,
        others,
        column_order(),
    )
    came = other_core(theirs)
    (track,) = call(mixing, [(128, 768)], attended, gated, mixing_weight)
    (message,) = call(joined, [(16, 32, 1152)], mine, came, track)
    got = lax.all_to_all(message, "ctx", 0, 0)
    grad, track = call(summed, [(4, 24, 1152), (128, 768)], got)
    got = lax.all_to_all(grad, "dp", 0, 0, axis_index_groups=NEAR)
    (grad,) = call(summed_again, [(4, 24, 1152)], got)
    got = lax.all_to_all(grad, "dp", 0, 0, axis_index_groups=FAR)
    (grad,) = call(summed_again, [(24, 1152)], got)
    rest = other_core(grad)
    first, second = jnp.where(core == 0, grad, rest), jnp.where(core == 0, rest, grad)
    dilated_grad = jnp.concatenate([first, second], axis=0).astype(F32)
    return (track.reshape(2, 64, 768), dilated_grad)


def solution(mesh):
    return jax.shard_map(
        shards,
        mesh=mesh,
        in_specs=(
            P("dp", "ctx", None),
            P(),
            P(),
            P(),
            P(),
            P("ctx", None),
            P(),
            P("dp", "ctx", None),
        ),
        out_specs=(P("dp", "ctx", None), P("ctx", None)),
        check_vma=False,
    )
```

time: 162 us -> 137 us (0.85)
  blocking collectives: 58 us -> 99.2 us
  waiting for transfers between devices: 36.7 us -> 2.46 us
  between operations: 14.5 us -> 0.72 us
  starting transfers between devices: 28.2 us -> 15.4 us
  Pallas kernels: 0 us -> 9.72 us
  matrix products: 9.24 us -> 0 us
  other arithmetic: 7.38 us -> 0.72 us
    all_to_all x4 -> x5, blocking collectives: 58 us -> 99.2 us  [the longest x2 50.4 us: shards(): got = lax.all_to_all(message, 'ctx', 0, 0)]
    all_gather x1 -> x0, waiting for transfers between devices: 16.2 us -> none  [shards(): complete_filters = lax.all_gather(dilated_weight, 'ctx', axis=0, tiled=True)]
    all_to_all x1 -> x0, waiting for transfers between devices: 15.1 us -> none  [summed_over(): got = lax.all_to_all(copies, 'dp', 0, 0, axis_index_groups=groups)]
    all_to_all x1 -> x0, starting transfers between devices: 11 us -> none  [summed_over(): got = lax.all_to_all(copies, 'dp', 0, 0, axis_index_groups=groups)]
    pallas_call x0 -> x8, Pallas kernels: none -> 9.72 us  [call(): pl.pallas_call(kernel, out_shape=[jax.ShapeDtypeStruct(shape, BF16) for s...]
    dot_general x14 -> x0, matrix products: 9.24 us -> none  [the longest x3 3.98 us: shards(): jnp.dot(sources[tap], complete_filters[:, tap * 384:(tap + 1) * 384], pre...]
    ppermute x2 -> x0, starting transfers between devices: 6.79 us -> none  [from_behind(): lax.ppermute(value, axis, [(source, source + steps) for source in range(i...]
    unnamed x18, local copies, waits for them, and re-layouts: 2.38 us -> 7.98 us
  transfers between devices with their start and end apart: 6 -> 3, of which waited for: 5 -> 2; matrix products, arithmetic and copies ran while one was open for 9% -> 0% of each run, Pallas kernels for 0% -> 0%
where the time goes in v2:
time: 137 us; the launch traced here: 136 us
  blocking collectives  99.2 us (72%)
  starting transfers between devices  15.4 us (11%)
  Pallas kernels  9.72 us (7%)
  local copies, waits for them, and re-layouts  7.98 us (6%)
  waiting for transfers between devices  2.46 us (2%)
    all_to_all x2, blocking collectives, shards(): got = lax.all_to_all(message, 'ctx', 0, 0)  50.4 us
    all_to_all x1, blocking collectives, shards(): got = lax.all_to_all(grad, 'dp', 0, 0, axis_index_groups=FAR)  27.3 us
    ppermute x3, starting transfers between devices, other_core(): lax.ppermute(value, 'dp', [(source, source ^ 1) for source in range(32)])  15.4 us
    all_to_all x1, blocking collectives, shards(): got = lax.all_to_all(grad, 'dp', 0, 0, axis_index_groups=NEAR)  11.1 us
    all_to_all x1, blocking collectives, shards(): got = lax.all_to_all(mixed, 'ctx', 0, 0)  10.5 us
    pallas_call x8, Pallas kernels, call(): pl.pallas_call(kernel, out_shape=[jax.ShapeDtypeStruct(shape, BF16) for s...  9.72 us
    unnamed x18, local copies, waits for them, and re-layouts  7.98 us
  transfers between devices with their start and end apart: 3, of which 2 were waited for; matrix products, arithmetic and copies ran while one was open for 0% of the time, Pallas kernels for 0%

profile of v2, /device:TPU:1, one launch (start us, length us, event | category | flops | bytes accessed | tf_op | source)
XLA Modules:
  0.0 136.2 jit_solution(9079404227493764546)
XLA Ops:
  0.6 0.0 copy-start
  0.7 1.1 copy-done
  1.7 0.0 copy-start.2
  1.7 1.3 copy-done.2
  3.0 0.0 copy-start.3
  3.0 1.0 copy-done.3
  4.0 0.0 copy-start.4
  4.0 1.0 copy-done.4
  5.0 0.0 copy-start.5
  5.0 0.9 copy-done.5
  5.9 0.0 copy-start.6
  5.9 0.9 copy-done.6
  6.8 0.0 copy-start.7
  6.8 0.9 copy-done.7
  7.7 2.6 %shard_map.104 = bf16[16,432,128]{2,1,0:T(8,128)(2,1)} custom-call(s32[1]{0:T(128)} %bitcast.core, bf16[128,768]{1,0:T(8,128)(2,1)S(1)} %bitcast.4, bf16[768,256]{1,0:T(8,128)(2,1)S(1)} %copy-done.3, bf16[768,256]{1,0:T(8,128)(2,1)S(1)} %copy-done.4, bf16[768,768]{1,0:T(8,128)(2,1)S(1)} %copy-done.2, bf16[48,1152]{1,0:T(8,128)(2,1)S(1)} %copy-done.7, ...), custom_call_target="tpu_custom_call" | custom-call | tf_op jit(solution)/shard_map/pallas_call | solution.py:212
  10.3 29.7 %all_to_all.25.got = bf16[16,432,128]{2,1,0:T(8,128)(2,1)S(1)} all-to-all(bf16[16,432,128]{2,1,0:T(8,128)(2,1)} %shard_map.104), channel_id=1, replica_groups=mesh['dp'=32,'ctx'=16] {'ctx'}, dimensions={0} | all-to-all | bytes 3538944 | tf_op jit(solution)/shard_map/all_to_all | solution.py:256
  40.0 1.1 shard_map.105
  41.0 5.7 %collective-permute-start = (bf16[384,1152]{1,0:T(8,128)(2,1)S(1)}, bf16[384,1152]{1,0:T(8,128)(2,1)S(1)}, u32[]{:S(2)}, u32[]{:S(2)}) collective-permute-start(bf16[384,1152]{1,0:T(8,128)(2,1)S(1)} %get-tuple-element.13.filters), channel_id=1, source_target_pairs={{0,16},{16,0},{32,48},{48,32},{64,80},{80,64},{96,112},{112,96},{1... | collective-permute-start | bytes 2654216 | tf_op jit(solution)/shard_map/ppermute | solution.py:222
  46.8 10.5 %all_to_all.26.got = bf16[16,48,128]{2,1,0:T(8,128)(2,1)S(1)} all-to-all(bf16[16,48,128]{2,1,0:T(8,128)(2,1)S(1)} %get-tuple-element.11), channel_id=1, replica_groups=mesh['dp'=32,'ctx'=16] {'ctx'}, dimensions={0} | all-to-all | bytes 393216 | tf_op jit(solution)/shard_map/all_to_all | solution.py:259
  57.3 0.0 collective-permute-done.others
  57.3 0.0 copy-start.8
  57.3 0.9 copy-done.8
  58.2 0.0 copy-start.1
  58.2 4.4 %shard_map.106 = (bf16[128,768]{1,0:T(8,128)(2,1)S(1)}, bf16[128,384]{1,0:T(8,128)(2,1)S(1)}, bf16[384,1152]{1,0:T(8,128)(2,1)S(1)}, bf16[384,1152]{1,0:T(8,128)(2,1)S(1)}) custom-call(s32[1]{0:T(128)} %bitcast.core, bf16[16,48,128]{2,1,0:T(8,128)(2,1)S(1)} %all_to_all.26.got, bf16[128,1152]{1,0:T(8,128)(2,1)S(1)} %get-tuple-element.12.sent, ...), custom_call_target="tpu_custom_call" | custom-call | tf_op jit(solution)/shard_map/pallas_call | solution.py:212
  62.6 3.1 %collective-permute-start.1 = (bf16[384,1152]{1,0:T(8,128)(2,1)S(1)}, bf16[384,1152]{1,0:T(8,128)(2,1)S(1)}, u32[]{:S(2)}, u32[]{:S(2)}) collective-permute-start(bf16[384,1152]{1,0:T(8,128)(2,1)S(1)} %get-tuple-element.15), channel_id=1, source_target_pairs={{0,16},{16,0},{32,48},{48,32},{64,80},{80,64},{96,112},{112,96},{1... | collective-permute-start | bytes 2654216 | tf_op jit(solution)/shard_map/ppermute | solution.py:222
  65.7 0.0 copy-done.1
  65.7 0.4 shard_map.107.track
  66.1 1.6 %collective-permute-done.1.came = bf16[384,1152]{1,0:T(8,128)(2,1)S(1)} collective-permute-done((bf16[384,1152]{1,0:T(8,128)(2,1)S(1)}, bf16[384,1152]{1,0:T(8,128)(2,1)S(1)}, u32[]{:S(2)}, u32[]{:S(2)}) %collective-permute-start.1) | collective-permute-done | bytes 884768 | tf_op jit(solution)/shard_map/ppermute | solution.py:222
  67.7 0.2 shard_map.108
  67.9 20.7 %all_to_all.27.got = bf16[16,32,1152]{2,1,0:T(8,128)(2,1)S(1)} all-to-all(bf16[16,32,1152]{2,1,0:T(8,128)(2,1)S(1)} %shard_map.108), channel_id=1, replica_groups=mesh['dp'=32,'ctx'=16] {'ctx'}, dimensions={0} | all-to-all | bytes 2359296 | tf_op jit(solution)/shard_map/all_to_all | solution.py:274
  88.6 1.0 shard_map.109
  89.6 11.1 %all_to_all.28.got = bf16[4,24,1152]{2,1,0:T(8,128)(2,1)S(1)} all-to-all(bf16[4,24,1152]{2,1,0:T(8,128)(2,1)S(1)} %get-tuple-element.19), channel_id=1, replica_groups={{0,32,64,96},{128,160,192,224},{256,288,320,352},{384,416,448,480},{16,..., dimensions={0} | all-to-all | bytes 442368 | tf_op jit(solution)/shard_map/all_to_all | solution.py:276
  100.7 27.3 %all_to_all.29.got = bf16[4,24,1152]{2,1,0:T(8,128)(2,1)S(1)} all-to-all(bf16[4,24,1152]{2,1,0:T(8,128)(2,1)S(1)} %shard_map.110), channel_id=1, replica_groups={{0,128,256,384},{32,160,288,416},{64,192,320,448},{96,224,352,480},{16,..., dimensions={0} | all-to-all | bytes 442368 | tf_op jit(solution)/shard_map/all_to_all | solution.py:278
  128.0 6.6 %collective-permute-start.2 = (bf16[24,1152]{1,0:T(8,128)(2,1)S(1)}, bf16[24,1152]{1,0:T(8,128)(2,1)S(1)}, u32[]{:S(2)}, u32[]{:S(2)}) collective-permute-start(bf16[24,1152]{1,0:T(8,128)(2,1)S(1)} %shard_map.111), channel_id=1, source_target_pairs={{0,16},{16,0},{32,48},{48,32},{64,80},{80,64},{96,112},{112,96},{1... | collective-permute-start | bytes 165896 | tf_op jit(solution)/shard_map/ppermute | solution.py:222
  134.6 0.9 collective-permute-done.2
  135.5 0.7 maximum_convert_fusion
  (3 shorter events, 0.1 us)
Async XLA Ops:
  0.6 1.1 copy-start
  1.7 1.3 copy-start.2
  3.0 1.0 copy-start.3
  4.0 1.0 copy-start.4
  5.0 0.9 copy-start.5
  5.9 0.9 copy-start.6
  6.8 0.9 copy-start.7
  41.0 16.3 %collective-permute-start = (bf16[384,1152]{1,0:T(8,128)(2,1)S(1)}, bf16[384,1152]{1,0:T(8,128)(2,1)S(1)}, u32[]{:S(2)}, u32[]{:S(2)}) collective-permute-start(bf16[384,1152]{1,0:T(8,128)(2,1)S(1)} %get-tuple-element.13.filters), channel_id=1, source_target_pairs={{0,16},{16,0},{32,48},{48,32},{64,80},{80,64},{96,112},{112,96},{1... | collective-permute-start | bytes 2654216 | tf_op jit(solution)/shard_map/ppermute | solution.py:222
  57.3 0.9 copy-start.8
  58.2 7.5 %copy-start.1 = (bf16[384,768]{1,0:T(8,128)(2,1)S(1)}, bf16[384,768]{1,0:T(8,128)(2,1)}, u32[]{:S(2)}) copy-start(bf16[384,768]{1,0:T(8,128)(2,1)} %mix.3) | copy-start | bytes 1769476
  62.6 5.1 %collective-permute-start.1 = (bf16[384,1152]{1,0:T(8,128)(2,1)S(1)}, bf16[384,1152]{1,0:T(8,128)(2,1)S(1)}, u32[]{:S(2)}, u32[]{:S(2)}) collective-permute-start(bf16[384,1152]{1,0:T(8,128)(2,1)S(1)} %get-tuple-element.15), channel_id=1, source_target_pairs={{0,16},{16,0},{32,48},{48,32},{64,80},{80,64},{96,112},{112,96},{1... | collective-permute-start | bytes 2654216 | tf_op jit(solution)/shard_map/ppermute | solution.py:222
  128.0 7.5 %collective-permute-start.2 = (bf16[24,1152]{1,0:T(8,128)(2,1)S(1)}, bf16[24,1152]{1,0:T(8,128)(2,1)S(1)}, u32[]{:S(2)}, u32[]{:S(2)}) collective-permute-start(bf16[24,1152]{1,0:T(8,128)(2,1)S(1)} %shard_map.111), channel_id=1, source_target_pairs={{0,16},{16,0},{32,48},{48,32},{64,80},{80,64},{96,112},{112,96},{1... | collective-permute-start | bytes 165896 | tf_op jit(solution)/shard_map/ppermute | solution.py:222

commit v3 on v2

--- a/solution.py
+++ b/solution.py
@@ -11,8 +11,8 @@
 
 NEAR = [[2 * (4 * far + near) + core for near in range(4)] for core in range(2) for far in range(4)]
 FAR = [[2 * (4 * far + near) + core for far in range(4)] for core in range(2) for near in range(4)]
+CLOSE = [[8 * far + member for member in range(8)] for far in range(4)]
 F32, BF16 = jnp.float32, jnp.bfloat16
-PARAMS = pltpu.CompilerParams(vmem_limit_bytes=50 * 1024 * 1024)
 VMEM = pl.BlockSpec(memory_space=pltpu.VMEM)
 SMEM = pl.BlockSpec(memory_space=pltpu.SMEM)
 
@@ -59,14 +59,48 @@
     return lax.broadcasted_iota(jnp.int32, (rows, 128), 1) < 64
 
 
-def front(core, x, wq, wk, wv, wd, mix, cot, message):
-    own = x[...]
-    normed = layer_norm(own.astype(F32)).astype(BF16)
-    q = head_norm(dot(normed, wq[...]))
-    k = head_norm(dot(normed, wk[...]))
-    v = dot(normed, wv[...])
+def fetch(pieces, semaphores):
+    copies = [pltpu.make_async_copy(a, b, semaphores.at[n]) for n, (a, b) in enumerate(pieces)]
+    for copy in copies:
+        copy.start()
+    return copies
+
+
+def front(core, x, wd, cot, mix, wq, wk, wv, message, carry, x_here, wd_here, cot_here, mix_here, wq_here, wk_here, wv_here, semaphores):
+    pieces = [(x, x_here), (wd, wd_here), (cot, cot_here)]
+    for weight, here in ((wq, wq_here), (wk, wk_here), (mix, mix_here), (wv, wv_here)):
+        step = weight.shape[0] // 4
+        pieces += [(weight.at[pl.ds(step * n, step)], here.at[pl.ds(step * n, step)]) for n in range(4)]
+    copies = fetch(pieces, semaphores)
     to_queries = moves(128, lambda r, c: c == ((r >> 6) * 64 + ((r >> 1) & 15) * 4 + ((r >> 5) & 1) * 2 + (r & 1)))
+    to_bins = moves(128, lambda r, c: c == (((r >> 2) & 1) * 64 + (r >> 3) * 4 + (r & 3)))
+    copies[0].wait()
+    normed = layer_norm(x_here[...].astype(F32)).astype(BF16)
+    sent = dot(to_bins, x_here[...])
+    copies[1].wait()
+    filters = wd_here[...].astype(F32)
+    filters = jnp.where(core[0] == 0, filters[0:24], filters[24:48]).astype(BF16)
+    for t in range(9):
+        tile = filters[:, 128 * t : 128 * t + 128]
+        for j in range(16):
+            message[j, 144 + 24 * t : 168 + 24 * t, :] = tile
+    for copy in copies[2:7]:
+        copy.wait()
+    moved = dot(to_bins, cot_here[...]).astype(BF16)
+    q = head_norm(dot(normed, wq_here[...]))
     q = dot(to_queries, q.astype(BF16))
+    for copy in copies[7:11]:
+        copy.wait()
+    k = head_norm(dot(normed, wk_here[...]))
+    for copy in copies[11:15]:
+        copy.wait()
+    back = dot(moved, mix_here[...], ((1,), (1,)))
+    for j in range(16):
+        rows = slice(8 * j, 8 * j + 8)
+        carry[j] = jnp.concatenate([sent[rows], back[rows]], axis=1).astype(BF16)
+    for copy in copies[15:19]:
+        copy.wait()
+    v = dot(normed, wv_here[...])
     low16, low64 = lower_lanes(16), lower_lanes(64)
     for s in range(2):
         rows = slice(64 * s, 64 * s + 64)
@@ -84,20 +118,9 @@
                 b = q[start + 16 : start + 32, 128 * pair : 128 * pair + 128]
                 message[8 * s + 4 * pair + half, 128:144, :] = jnp.where(low16, a, swap(b)).astype(BF16)
                 message[8 * s + 4 * pair + 2 + half, 128:144, :] = jnp.where(low16, swap(a), b).astype(BF16)
-    to_bins = moves(128, lambda r, c: c == (((r >> 2) & 1) * 64 + (r >> 3) * 4 + (r & 3)))
-    sent = dot(to_bins, own)
-    back = dot(dot(to_bins, cot[...]).astype(BF16), mix[...], ((1,), (1,)))
-    filters = wd[...].astype(F32)
-    filters = jnp.where(core[0] == 0, filters[0:24], filters[24:48])
-    for j in range(16):
-        rows = slice(8 * j, 8 * j + 8)
-        slab = jnp.concatenate([sent[rows], back[rows]], axis=1)
-        slab = jnp.concatenate([slab, filters], axis=0).astype(BF16)
-        for t in range(9):
-            message[j, 144 + 32 * t : 176 + 32 * t, :] = slab[:, 128 * t : 128 * t + 128]
-
-
-def attention(got, out, filters, sent):
+
+
+def attention(got, carry, out, filters):
     low = got[:, 0:64, :].reshape(1024, 128)
     high = got[:, 64:128, :].reshape(1024, 128)
     value = jnp.concatenate([low, high], axis=1)
@@ -115,31 +138,36 @@
         for j in range(4):
             part = mixed[32 * j : 32 * j + 32]
             first = jnp.where(low16, swap(part[16:32, 0:128]), part[0:16, 0:128])
-            out[4 * block + j] = jnp.concatenate([first, part[:, 128:256]], axis=0).astype(BF16)
-    to_groups = moves(128, lambda r, c: c == (((r >> 1) & 15) * 8 + (r >> 5) * 2 + (r & 1)))
+            out[4 * block + j, 0:48, :] = jnp.concatenate([first, part[:, 128:256]], axis=0).astype(BF16)
     for t in range(9):
         lanes = slice(128 * t, 128 * t + 128)
-        pieces = [got[i, 144 + 32 * t : 176 + 32 * t, :].astype(F32) for i in range(16)]
-        filters[:, lanes] = jnp.concatenate([p[8:32] for p in pieces], axis=0).astype(BF16)
-        rows = jnp.concatenate([p[0:8] for p in pieces], axis=0).astype(BF16)
-        sent[:, lanes] = dot(to_groups, rows).astype(BF16)
-
-
-def middle(core, got, sent, wo, filters, others, order, attended, gated, mine, theirs):
+        pieces = [got[i, 144 + 24 * t : 168 + 24 * t, :].astype(F32) for i in range(16)]
+        filters[:, lanes] = jnp.concatenate(pieces, axis=0).astype(BF16)
+        for j in range(16):
+            out[j, 48 + 8 * t : 56 + 8 * t, :] = carry[j, :, lanes]
+
+
+def middle(core, got, wo, filters, others, order, attended, gated, mine, theirs):
+    to_groups = moves(128, lambda r, c: c == (((r >> 1) & 15) * 8 + (r >> 5) * 2 + (r & 1)))
+    sent = []
+    for t in range(9):
+        rows = [got[i, 48 + 8 * t : 56 + 8 * t, :].astype(F32) for i in range(16)]
+        sent.append(jnp.concatenate(rows, axis=0).astype(BF16))
+    sent = dot(to_groups, jnp.concatenate(sent, axis=1))
     low16 = lower_lanes(16)
     tiles = []
     for pair in range(2):
         groups = [[], [], []]
         for s in range(2):
             for half in range(2):
-                even, odd = (got[8 * s + 4 * pair + 2 * o + half].astype(F32) for o in range(2))
+                even, odd = (got[8 * s + 4 * pair + 2 * o + half, 0:48, :].astype(F32) for o in range(2))
                 e, o = even[0:16], odd[0:16]
                 groups[0].append(even[16:48])
                 groups[1] += [jnp.where(low16, swap(e), o), jnp.where(low16, e, swap(o))]
                 groups[2].append(odd[16:48])
         tiles += [jnp.concatenate(g, axis=0) for g in groups]
     mixed = jnp.concatenate(tiles, axis=1).astype(BF16)
-    result = (sent[:, 0:768].astype(F32) + dot(mixed, wo[...])).astype(BF16)
+    result = (sent[:, 0:768] + dot(mixed, wo[...])).astype(BF16)
     attended[...] = result
     normed = layer_norm(result.astype(F32))
     lifted = (normed * normal_cdf(normed)).astype(BF16)
@@ -161,11 +189,16 @@
     cdf = normal_cdf(hidden)
     gated[...] = (hidden * cdf).astype(BF16)
     pdf = jnp.exp(-0.5 * hidden * hidden) * (1.0 / math.sqrt(2.0 * math.pi))
-    slope = (sent[:, 768:1152].astype(F32) * (cdf + hidden * pdf)).astype(BF16)
+    slope = (sent[:, 768:1152] * (cdf + hidden * pdf)).astype(BF16)
     slopes = (dot(from_above, slope).astype(BF16), slope, dot(from_below, slope).astype(BF16))
     for part, target in ((1, theirs), (0, mine)):
         for tap in range(3):
-            target[:, 384 * tap : 384 * tap + 384] = dot(lifted[part], slopes[tap], ((0,), (0,))).astype(BF16)
+            grad = dot(lifted[part], slopes[tap], ((0,), (0,)))
+            for d in range(16):
+                for t in range(3):
+                    start = 24 * (3 * tap + t)
+                    tile = grad[24 * d : 24 * d + 24, 128 * t : 128 * t + 128]
+                    target[d, start : start + 24, :] = tile.astype(BF16)
 
 
 def mixing(attended, gated, mix, track):
@@ -175,46 +208,54 @@
 
 
 def joined(mine, came, track, message):
-    blank = jnp.zeros((8, 384), F32)
     for d in range(16):
-        rows = slice(24 * d, 24 * d + 24)
-        grad = mine[rows].astype(F32) + came[rows].astype(F32)
-        top = jnp.concatenate([track[8 * d : 8 * d + 8].astype(F32), blank], axis=1)
-        message[d] = jnp.concatenate([top, grad], axis=0).astype(BF16)
+        for t in range(6):
+            message[d, 8 * t : 8 * t + 8, :] = track[8 * d : 8 * d + 8, 128 * t : 128 * t + 128]
+        message[d, 48:264, :] = (mine[d].astype(F32) + came[d].astype(F32)).astype(BF16)
 
 
 def summed(got, grad, track):
-    total = got[0].astype(F32)
-    rows = [total[0:8, 0:768]]
+    total = got[0, 48:264, :].astype(F32)
     for d in range(1, 16):
-        block = got[d].astype(F32)
-        rows.append(block[0:8, 0:768])
-        total = total + block
-    total = total[8:32].astype(BF16)
-    for copy in range(4):
-        grad[copy] = total
+        total = total + got[d, 48:264, :].astype(F32)
+    total = jnp.concatenate([total, jnp.zeros((8, 128), F32)], axis=0)
+    for near in range(4):
+        grad[near] = total[56 * near : 56 * near + 56].astype(BF16)
     natural = moves(128, lambda r, c: c == (((r >> 2) & 15) * 8 + (r >> 6) * 4 + (r & 3)))
-    result = dot(natural, jnp.concatenate(rows, axis=0).astype(BF16))
-    track[...] = result.astype(BF16)
+    for t in range(6):
+        rows = [got[d, 8 * t : 8 * t + 8, :].astype(F32) for d in range(16)]
+        rows = dot(natural, jnp.concatenate(rows, axis=0).astype(BF16))
+        track[:, 128 * t : 128 * t + 128] = rows.astype(BF16)
 
 
 def summed_again(got, grad):
     total = got[0].astype(F32) + got[1].astype(F32) + got[2].astype(F32) + got[3].astype(F32)
     total = total.astype(BF16)
-    if len(grad.shape) == 3:
-        for copy in range(grad.shape[0]):
-            grad[copy] = total
-    else:
-        grad[...] = total
-
-
-def call(kernel, outs, *args):
+    for copy in range(grad.shape[0]):
+        grad[copy] = total
+
+
+def ordered(got, grad):
+    for core in range(2):
+        rows = jnp.concatenate([got[2 * near + core].astype(F32) for near in range(4)], axis=0)
+        for t in range(9):
+            grad[24 * core : 24 * core + 24, 128 * t : 128 * t + 128] = rows[24 * t : 24 * t + 24]
+
+
+def call(kernel, outs, *args, dtype=BF16, fetched=()):
+    scratch = [pltpu.VMEM(shape, BF16) for shape in fetched]
+    if fetched:
+        scratch.append(pltpu.SemaphoreType.DMA((19,)))
     return pl.pallas_call(
         kernel,
-        out_shape=[jax.ShapeDtypeStruct(shape, BF16) for shape in outs],
-        in_specs=[SMEM if a.dtype == jnp.int32 else VMEM for a in args],
+        out_shape=[jax.ShapeDtypeStruct(shape, dtype) for shape in outs],
+        in_specs=[
+            SMEM if a.dtype == jnp.int32 else pl.BlockSpec(memory_space=pl.ANY) if fetched else VMEM
+            for a in args
+        ],
         out_specs=[VMEM] * len(outs),
-        compiler_params=PARAMS,
+        scratch_shapes=scratch,
+        compiler_params=pltpu.CompilerParams(vmem_limit_bytes=(56 if fetched else 32) * 1024 * 1024),
     )(*args)
 
 
@@ -241,28 +282,28 @@
 ):
     core = lax.axis_index("dp") % 2
     flag = core.astype(jnp.int32).reshape(1)
-    (message,) = call(
+    message, carry = call(
         front,
-        [(16, 432, 128)],
+        [(16, 360, 128), (16, 8, 1152)],
         flag,
         features.reshape(128, 768),
+        dilated_weight,
+        cotangent.reshape(128, 768),
+        mixing_weight,
         query_weight,
         key_weight,
         value_weight,
-        dilated_weight,
-        mixing_weight,
-        cotangent.reshape(128, 768),
+        fetched=((128, 768), (48, 1152), (128, 768), (384, 768), (768, 256), (768, 256), (768, 768)),
     )
     got = lax.all_to_all(message, "ctx", 0, 0)
-    mixed, filters, sent = call(attention, [(16, 48, 128), (384, 1152), (128, 1152)], got)
+    mixed, filters = call(attention, [(16, 120, 128), (384, 1152)], got, carry)
     others = other_core(filters)
     got = lax.all_to_all(mixed, "ctx", 0, 0)
     attended, gated, mine, theirs = call(
         middle,
-        [(128, 768), (128, 384), (384, 1152), (384, 1152)],
+        [(128, 768), (128, 384), (16, 216, 128), (16, 216, 128)],
         flag,
         got,
-        sent,
         output_weight,
         filters,
         others,
@@ -270,16 +311,15 @@
     )
     came = other_core(theirs)
     (track,) = call(mixing, [(128, 768)], attended, gated, mixing_weight)
-    (message,) = call(joined, [(16, 32, 1152)], mine, came, track)
+    (message,) = call(joined, [(16, 264, 128)], mine, came, track)
     got = lax.all_to_all(message, "ctx", 0, 0)
-    grad, track = call(summed, [(4, 24, 1152), (128, 768)], got)
+    grad, track = call(summed, [(4, 56, 128), (128, 768)], got)
     got = lax.all_to_all(grad, "dp", 0, 0, axis_index_groups=NEAR)
-    (grad,) = call(summed_again, [(4, 24, 1152)], got)
+    (grad,) = call(summed_again, [(4, 56, 128)], got)
     got = lax.all_to_all(grad, "dp", 0, 0, axis_index_groups=FAR)
-    (grad,) = call(summed_again, [(24, 1152)], got)
-    rest = other_core(grad)
-    first, second = jnp.where(core == 0, grad, rest), jnp.where(core == 0, rest, grad)
-    dilated_grad = jnp.concatenate([first, second], axis=0).astype(F32)
+    (grad,) = call(summed_again, [(8, 56, 128)], got)
+    got = lax.all_to_all(grad, "dp", 0, 0, axis_index_groups=CLOSE)
+    (dilated_grad,) = call(ordered, [(48, 1152)], got, dtype=F32)
     return (track.reshape(2, 64, 768), dilated_grad)
 
 

time: 137 us -> 128 us (0.934)
  local copies, waits for them, and re-layouts: 7.98 us -> 0.02 us
  blocking collectives: 99.2 us -> 106 us
  starting transfers between devices: 15.4 us -> 9.22 us
    all_to_all x0 -> x1, blocking collectives: none -> 12.8 us  [shards(): got = lax.all_to_all(grad, 'dp', 0, 0, axis_index_groups=CLOSE)]
    unnamed x18 -> x8, local copies, waits for them, and re-layouts: 7.98 us -> 0.02 us
    ppermute x3 -> x2, starting transfers between devices: 15.4 us -> 9.22 us  [other_core(): lax.ppermute(value, 'dp', [(source, source ^ 1) for source in range(32)])]
    all_to_all x2, blocking collectives: 50.4 us -> 45.8 us  [shards(): got = lax.all_to_all(message, 'ctx', 0, 0)]
    all_to_all x1, blocking collectives: 27.3 us -> 23.7 us  [shards(): got = lax.all_to_all(grad, 'dp', 0, 0, axis_index_groups=FAR)]
    all_to_all x1, blocking collectives: 10.5 us -> 13.5 us  [shards(): got = lax.all_to_all(mixed, 'ctx', 0, 0)]
    pallas_call x8 -> x9, Pallas kernels: 9.72 us -> 10.6 us  [call(): pl.pallas_call(kernel, out_shape=[jax.ShapeDtypeStruct(shape, dtype) for...]
  transfers between devices with their start and end apart: 3 -> 2, of which waited for: 2 -> 1; matrix products, arithmetic and copies ran while one was open for 0% -> 0% of each run, Pallas kernels for 0% -> 0%
where the time goes in v3:
time: 128 us
  blocking collectives  106 us (83%)
  Pallas kernels  10.6 us (8%)
  starting transfers between devices  9.22 us (7%)
  waiting for transfers between devices  1.6 us (1%)
    all_to_all x2, blocking collectives, shards(): got = lax.all_to_all(message, 'ctx', 0, 0)  45.8 us
    all_to_all x1, blocking collectives, shards(): got = lax.all_to_all(grad, 'dp', 0, 0, axis_index_groups=FAR)  23.7 us
    all_to_all x1, blocking collectives, shards(): got = lax.all_to_all(mixed, 'ctx', 0, 0)  13.5 us
    all_to_all x1, blocking collectives, shards(): got = lax.all_to_all(grad, 'dp', 0, 0, axis_index_groups=CLOSE)  12.8 us
    pallas_call x9, Pallas kernels, call(): pl.pallas_call(kernel, out_shape=[jax.ShapeDtypeStruct(shape, dtype) for...  10.6 us
    all_to_all x1, blocking collectives, shards(): got = lax.all_to_all(grad, 'dp', 0, 0, axis_index_groups=NEAR)  9.86 us
    ppermute x2, starting transfers between devices, other_core(): lax.ppermute(value, 'dp', [(source, source ^ 1) for source in range(32)])  9.22 us
  transfers between devices with their start and end apart: 2, of which 1 were waited for; matrix products, arithmetic and copies ran while one was open for 0% of the time, Pallas kernels for 0%

profile of v3, /device:TPU:1, one launch (start us, length us, event | category | flops | bytes accessed | tf_op | source)
XLA Modules:
  0.0 127.7 jit_solution(12814627462296758749)
XLA Ops:
  0.6 4.7 %shard_map.104 = (bf16[16,360,128]{2,1,0:T(8,128)(2,1)}, bf16[16,8,1152]{2,1,0:T(8,128)(2,1)}) custom-call(s32[1]{0:T(128)} %bitcast.core, bf16[128,768]{1,0:T(8,128)(2,1)} %bitcast.4, bf16[48,1152]{1,0:T(8,128)(2,1)} %wd.1, bf16[128,768]{1,0:T(8,128)(2,1)} %bitcast.5, bf16[384,768]{1,0:T(8,128)(2,1)} %mix.3, bf16[768,256]{1,0:T(8,128)(2,1)} %wq.1, ...), custom_call_target="tpu_custom_call" | custom-call | tf_op jit(solution)/shard_map/pallas_call | solution.py:249
  5.3 0.0 copy-start.3
  5.3 26.4 %all_to_all.30.got = bf16[16,360,128]{2,1,0:T(8,128)(2,1)S(1)} all-to-all(bf16[16,360,128]{2,1,0:T(8,128)(2,1)} %get-tuple-element.12), channel_id=1, replica_groups=mesh['dp'=32,'ctx'=16] {'ctx'}, dimensions={0} | all-to-all | bytes 2949120 | tf_op jit(solution)/shard_map/all_to_all | solution.py:298
  31.7 0.0 copy-done.3
  31.7 0.0 copy-start.1
  31.7 0.0 copy-start.2
  31.7 1.1 shard_map.105
  32.8 6.0 %collective-permute-start = (bf16[384,1152]{1,0:T(8,128)(2,1)S(1)}, bf16[384,1152]{1,0:T(8,128)(2,1)S(1)}, u32[]{:S(2)}, u32[]{:S(2)}) collective-permute-start(bf16[384,1152]{1,0:T(8,128)(2,1)S(1)} %get-tuple-element.15.filters), channel_id=1, source_target_pairs={{0,16},{16,0},{32,48},{48,32},{64,80},{80,64},{96,112},{112,96},{1... | collective-permute-start | bytes 2654216 | tf_op jit(solution)/shard_map/ppermute | solution.py:263
  38.8 13.5 %all_to_all.31.got = bf16[16,120,128]{2,1,0:T(8,128)(2,1)S(1)} all-to-all(bf16[16,120,128]{2,1,0:T(8,128)(2,1)S(1)} %get-tuple-element.14), channel_id=1, replica_groups=mesh['dp'=32,'ctx'=16] {'ctx'}, dimensions={0} | all-to-all | bytes 983040 | tf_op jit(solution)/shard_map/all_to_all | solution.py:301
  52.3 0.0 copy-start
  52.3 0.0 collective-permute-done.others
  52.3 0.0 copy-done.1
  52.3 0.0 copy-done.2
  52.3 2.5 %shard_map.106 = (bf16[128,768]{1,0:T(8,128)(2,1)S(1)}, bf16[128,384]{1,0:T(8,128)(2,1)S(1)}, bf16[16,216,128]{2,1,0:T(8,128)(2,1)S(1)}, bf16[16,216,128]{2,1,0:T(8,128)(2,1)S(1)}) custom-call(s32[1]{0:T(128)} %bitcast.core, bf16[16,120,128]{2,1,0:T(8,128)(2,1)S(1)} %all_to_all.31.got, bf16[768,768]{1,0:T(8,128)(2,1)S(1)} %copy-done.1, ...), custom_call_target="tpu_custom_call" | custom-call | tf_op jit(solution)/shard_map/pallas_call | solution.py:249
  54.8 3.2 %collective-permute-start.1 = (bf16[16,216,128]{2,1,0:T(8,128)(2,1)S(1)}, bf16[16,216,128]{2,1,0:T(8,128)(2,1)S(1)}, u32[]{:S(2)}, u32[]{:S(2)}) collective-permute-start(bf16[16,216,128]{2,1,0:T(8,128)(2,1)S(1)} %get-tuple-element.17), channel_id=1, source_target_pairs={{0,16},{16,0},{32,48},{48,32},{64,80},{80,64},{96,112},{112,96},{1... | collective-permute-start | bytes 2654216 | tf_op jit(solution)/shard_map/ppermute | solution.py:263
  58.0 0.0 copy-done
  58.0 0.4 shard_map.107.track
  58.5 1.6 %collective-permute-done.1.came = bf16[16,216,128]{2,1,0:T(8,128)(2,1)S(1)} collective-permute-done((bf16[16,216,128]{2,1,0:T(8,128)(2,1)S(1)}, bf16[16,216,128]{2,1,0:T(8,128)(2,1)S(1)}, u32[]{:S(2)}, u32[]{:S(2)}) %collective-permute-start.1) | collective-permute-done | bytes 884768 | tf_op jit(solution)/shard_map/ppermute | solution.py:263
  60.1 0.2 shard_map.108
  60.3 19.4 %all_to_all.32.got = bf16[16,264,128]{2,1,0:T(8,128)(2,1)S(1)} all-to-all(bf16[16,264,128]{2,1,0:T(8,128)(2,1)S(1)} %shard_map.108), channel_id=1, replica_groups=mesh['dp'=32,'ctx'=16] {'ctx'}, dimensions={0} | all-to-all | bytes 2162688 | tf_op jit(solution)/shard_map/all_to_all | solution.py:315
  79.7 1.0 shard_map.109
  80.7 9.9 %all_to_all.33.got = bf16[4,56,128]{2,1,0:T(8,128)(2,1)S(1)} all-to-all(bf16[4,56,128]{2,1,0:T(8,128)(2,1)S(1)} %get-tuple-element.21), channel_id=1, replica_groups={{0,32,64,96},{128,160,192,224},{256,288,320,352},{384,416,448,480},{16,..., dimensions={0} | all-to-all | bytes 114688 | tf_op jit(solution)/shard_map/all_to_all | solution.py:317
  90.5 23.7 %all_to_all.34.got = bf16[4,56,128]{2,1,0:T(8,128)(2,1)S(1)} all-to-all(bf16[4,56,128]{2,1,0:T(8,128)(2,1)S(1)} %shard_map.110), channel_id=1, replica_groups={{0,128,256,384},{32,160,288,416},{64,192,320,448},{96,224,352,480},{16,..., dimensions={0} | all-to-all | bytes 114688 | tf_op jit(solution)/shard_map/all_to_all | solution.py:319
  114.3 12.8 %all_to_all.35.got = bf16[8,56,128]{2,1,0:T(8,128)(2,1)S(1)} all-to-all(bf16[8,56,128]{2,1,0:T(8,128)(2,1)S(1)} %shard_map.111), channel_id=1, replica_groups={{0,16,32,48,64,80,96,112},{128,144,160,176,192,208,224,240},{256,272,28..., dimensions={0} | all-to-all | bytes 229376 | tf_op jit(solution)/shard_map/all_to_all | solution.py:321
  127.0 0.7 shard_map.112
  (2 shorter events, 0.0 us)
Async XLA Ops:
  5.3 26.4 %copy-start.3 = (bf16[16,8,1152]{2,1,0:T(8,128)(2,1)S(1)}, bf16[16,8,1152]{2,1,0:T(8,128)(2,1)}, u32[]{:S(2)}) copy-start(bf16[16,8,1152]{2,1,0:T(8,128)(2,1)} %get-tuple-element.13.carry) | copy-start | bytes 884740
  31.7 20.6 %copy-start.1 = (bf16[768,768]{1,0:T(8,128)(2,1)S(1)}, bf16[768,768]{1,0:T(8,128)(2,1)}, u32[]{:S(2)}) copy-start(bf16[768,768]{1,0:T(8,128)(2,1)} %wo.1) | copy-start | bytes 3538948
  31.7 20.6 %copy-start.2 = (bf16[768,768]{1,0:T(8,128)(2,1)S(1)}, bf16[768,768]{1,0:T(8,128)(2,1)}, u32[]{:S(2)}) copy-start(bf16[768,768]{1,0:T(8,128)(2,1)} %constant.21.clone.order) | copy-start | bytes 3538948
  32.8 19.5 %collective-permute-start = (bf16[384,1152]{1,0:T(8,128)(2,1)S(1)}, bf16[384,1152]{1,0:T(8,128)(2,1)S(1)}, u32[]{:S(2)}, u32[]{:S(2)}) collective-permute-start(bf16[384,1152]{1,0:T(8,128)(2,1)S(1)} %get-tuple-element.15.filters), channel_id=1, source_target_pairs={{0,16},{16,0},{32,48},{48,32},{64,80},{80,64},{96,112},{112,96},{1... | collective-permute-start | bytes 2654216 | tf_op jit(solution)/shard_map/ppermute | solution.py:263
  52.3 5.7 %copy-start = (bf16[384,768]{1,0:T(8,128)(2,1)S(1)}, bf16[384,768]{1,0:T(8,128)(2,1)}, u32[]{:S(2)}) copy-start(bf16[384,768]{1,0:T(8,128)(2,1)} %mix.3) | copy-start | bytes 1769476
  54.8 5.2 %collective-permute-start.1 = (bf16[16,216,128]{2,1,0:T(8,128)(2,1)S(1)}, bf16[16,216,128]{2,1,0:T(8,128)(2,1)S(1)}, u32[]{:S(2)}, u32[]{:S(2)}) collective-permute-start(bf16[16,216,128]{2,1,0:T(8,128)(2,1)S(1)} %get-tuple-element.17), channel_id=1, source_target_pairs={{0,16},{16,0},{32,48},{48,32},{64,80},{80,64},{96,112},{112,96},{1... | collective-permute-start | bytes 2654216 | tf_op jit(solution)/shard_map/ppermute | solution.py:263

commit v4 on v3

--- a/solution.py
+++ b/solution.py
@@ -11,7 +11,7 @@
 
 NEAR = [[2 * (4 * far + near) + core for near in range(4)] for core in range(2) for far in range(4)]
 FAR = [[2 * (4 * far + near) + core for far in range(4)] for core in range(2) for near in range(4)]
-CLOSE = [[8 * far + member for member in range(8)] for far in range(4)]
+CLOSE = [[4 * pair + member for member in range(4)] for pair in range(8)]
 F32, BF16 = jnp.float32, jnp.bfloat16
 VMEM = pl.BlockSpec(memory_space=pltpu.VMEM)
 SMEM = pl.BlockSpec(memory_space=pltpu.SMEM)
@@ -36,14 +36,10 @@
 def head_norm(values):
     row = lax.broadcasted_iota(jnp.int32, (256, 256), 0)
     column = lax.broadcasted_iota(jnp.int32, (256, 256), 1)
-    same = jnp.where((row >> 6) == (column >> 6), 1.0 / 64.0, 0.0).astype(F32)
-    mean = lax.dot_general(
-        values * values,
-        same,
-        (((1,), (0,)), ((), ())),
-        precision=lax.Precision.HIGHEST,
-        preferred_element_type=F32,
-    )
+    same = jnp.where((row >> 6) == (column >> 6), 1.0 / 64.0, 0.0).astype(BF16)
+    square = values * values
+    high = square.astype(BF16)
+    mean = dot(high, same) + dot((square - high.astype(F32)).astype(BF16), same)
     return values * lax.rsqrt(mean + 1e-06)
 
 
@@ -66,17 +62,15 @@
     return copies
 
 
-def front(core, x, wd, cot, mix, wq, wk, wv, message, carry, x_here, wd_here, cot_here, mix_here, wq_here, wk_here, wv_here, semaphores):
-    pieces = [(x, x_here), (wd, wd_here), (cot, cot_here)]
-    for weight, here in ((wq, wq_here), (wk, wk_here), (mix, mix_here), (wv, wv_here)):
-        step = weight.shape[0] // 4
-        pieces += [(weight.at[pl.ds(step * n, step)], here.at[pl.ds(step * n, step)]) for n in range(4)]
+def front(core, x, wd, wq, wk, wv, message, x_here, wd_here, wq_here, wk_here, wv_here, semaphores):
+    pieces = [(x, x_here), (wd, wd_here)]
+    for weight, here in ((wq, wq_here), (wk, wk_here), (wv, wv_here)):
+        step = weight.shape[0] // 2
+        pieces += [(weight.at[pl.ds(step * n, step)], here.at[pl.ds(step * n, step)]) for n in range(2)]
     copies = fetch(pieces, semaphores)
     to_queries = moves(128, lambda r, c: c == ((r >> 6) * 64 + ((r >> 1) & 15) * 4 + ((r >> 5) & 1) * 2 + (r & 1)))
-    to_bins = moves(128, lambda r, c: c == (((r >> 2) & 1) * 64 + (r >> 3) * 4 + (r & 3)))
     copies[0].wait()
     normed = layer_norm(x_here[...].astype(F32)).astype(BF16)
-    sent = dot(to_bins, x_here[...])
     copies[1].wait()
     filters = wd_here[...].astype(F32)
     filters = jnp.where(core[0] == 0, filters[0:24], filters[24:48]).astype(BF16)
@@ -84,21 +78,14 @@
         tile = filters[:, 128 * t : 128 * t + 128]
         for j in range(16):
             message[j, 144 + 24 * t : 168 + 24 * t, :] = tile
-    for copy in copies[2:7]:
+    for copy in copies[2:4]:
         copy.wait()
-    moved = dot(to_bins, cot_here[...]).astype(BF16)
     q = head_norm(dot(normed, wq_here[...]))
     q = dot(to_queries, q.astype(BF16))
-    for copy in copies[7:11]:
+    for copy in copies[4:6]:
         copy.wait()
     k = head_norm(dot(normed, wk_here[...]))
-    for copy in copies[11:15]:
-        copy.wait()
-    back = dot(moved, mix_here[...], ((1,), (1,)))
-    for j in range(16):
-        rows = slice(8 * j, 8 * j + 8)
-        carry[j] = jnp.concatenate([sent[rows], back[rows]], axis=1).astype(BF16)
-    for copy in copies[15:19]:
+    for copy in copies[6:8]:
         copy.wait()
     v = dot(normed, wv_here[...])
     low16, low64 = lower_lanes(16), lower_lanes(64)
@@ -120,7 +107,7 @@
                 message[8 * s + 4 * pair + 2 + half, 128:144, :] = jnp.where(low16, swap(a), b).astype(BF16)
 
 
-def attention(got, carry, out, filters):
+def attention(got, x, cot, mix, out, filters):
     low = got[:, 0:64, :].reshape(1024, 128)
     high = got[:, 64:128, :].reshape(1024, 128)
     value = jnp.concatenate([low, high], axis=1)
@@ -143,11 +130,16 @@
         lanes = slice(128 * t, 128 * t + 128)
         pieces = [got[i, 144 + 24 * t : 168 + 24 * t, :].astype(F32) for i in range(16)]
         filters[:, lanes] = jnp.concatenate(pieces, axis=0).astype(BF16)
+    to_bins = moves(128, lambda r, c: c == (((r >> 2) & 1) * 64 + (r >> 3) * 4 + (r & 3)))
+    sent = dot(to_bins, x[...]).astype(BF16)
+    back = dot(dot(to_bins, cot[...]).astype(BF16), mix[...], ((1,), (1,))).astype(BF16)
+    for t in range(9):
+        rows = sent[:, 128 * t : 128 * t + 128] if t < 6 else back[:, 128 * t - 768 : 128 * t - 640]
         for j in range(16):
-            out[j, 48 + 8 * t : 56 + 8 * t, :] = carry[j, :, lanes]
-
-
-def middle(core, got, wo, filters, others, order, attended, gated, mine, theirs):
+            out[j, 48 + 8 * t : 56 + 8 * t, :] = rows[8 * j : 8 * j + 8]
+
+
+def middle(core, got, wo, filters, others, order, attended, gated, own, slopes, theirs):
     to_groups = moves(128, lambda r, c: c == (((r >> 1) & 15) * 8 + (r >> 5) * 2 + (r & 1)))
     sent = []
     for t in range(9):
@@ -190,21 +182,28 @@
     gated[...] = (hidden * cdf).astype(BF16)
     pdf = jnp.exp(-0.5 * hidden * hidden) * (1.0 / math.sqrt(2.0 * math.pi))
     slope = (sent[:, 768:1152] * (cdf + hidden * pdf)).astype(BF16)
-    slopes = (dot(from_above, slope).astype(BF16), slope, dot(from_below, slope).astype(BF16))
-    for part, target in ((1, theirs), (0, mine)):
-        for tap in range(3):
-            grad = dot(lifted[part], slopes[tap], ((0,), (0,)))
-            for d in range(16):
-                for t in range(3):
-                    start = 24 * (3 * tap + t)
-                    tile = grad[24 * d : 24 * d + 24, 128 * t : 128 * t + 128]
-                    target[d, start : start + 24, :] = tile.astype(BF16)
-
-
-def mixing(attended, gated, mix, track):
+    own[...] = lifted[0]
+    slopes[:, 0:384] = dot(from_above, slope).astype(BF16)
+    slopes[:, 384:768] = slope
+    slopes[:, 768:1152] = dot(from_below, slope).astype(BF16)
+    gradient(lifted[1], slopes, theirs)
+
+
+def gradient(lifted, slopes, target):
+    for tap in range(3):
+        grad = dot(lifted, slopes[:, 384 * tap : 384 * tap + 384], ((0,), (0,)))
+        for d in range(16):
+            for t in range(3):
+                start = 24 * (3 * tap + t)
+                tile = grad[24 * d : 24 * d + 24, 128 * t : 128 * t + 128]
+                target[d, start : start + 24, :] = tile.astype(BF16)
+
+
+def rest(attended, gated, mix, lifted, slopes, track, mine):
     result = (attended[...].astype(F32) + dot(gated[...], mix[...])).astype(BF16)
     by_block = moves(128, lambda r, c: c == (((r >> 1) & 3) * 32 + (r >> 3) * 2 + (r & 1)))
     track[...] = dot(by_block, result).astype(BF16)
+    gradient(lifted[...], slopes, mine)
 
 
 def joined(mine, came, track, message):
@@ -220,7 +219,8 @@
         total = total + got[d, 48:264, :].astype(F32)
     total = jnp.concatenate([total, jnp.zeros((8, 128), F32)], axis=0)
     for near in range(4):
-        grad[near] = total[56 * near : 56 * near + 56].astype(BF16)
+        half = 112 * (near % 2)
+        grad[near] = total[half : half + 112].astype(BF16)
     natural = moves(128, lambda r, c: c == (((r >> 2) & 15) * 8 + (r >> 6) * 4 + (r & 3)))
     for t in range(6):
         rows = [got[d, 8 * t : 8 * t + 8, :].astype(F32) for d in range(16)]
@@ -237,7 +237,7 @@
 
 def ordered(got, grad):
     for core in range(2):
-        rows = jnp.concatenate([got[2 * near + core].astype(F32) for near in range(4)], axis=0)
+        rows = jnp.concatenate([got[2 * half + core].astype(F32) for half in range(2)], axis=0)
         for t in range(9):
             grad[24 * core : 24 * core + 24, 128 * t : 128 * t + 128] = rows[24 * t : 24 * t + 24]
 
@@ -245,7 +245,7 @@
 def call(kernel, outs, *args, dtype=BF16, fetched=()):
     scratch = [pltpu.VMEM(shape, BF16) for shape in fetched]
     if fetched:
-        scratch.append(pltpu.SemaphoreType.DMA((19,)))
+        scratch.append(pltpu.SemaphoreType.DMA((8,)))
     return pl.pallas_call(
         kernel,
         out_shape=[jax.ShapeDtypeStruct(shape, dtype) for shape in outs],
@@ -282,26 +282,25 @@
 ):
     core = lax.axis_index("dp") % 2
     flag = core.astype(jnp.int32).reshape(1)
-    message, carry = call(
+    rows, slope = features.reshape(128, 768), cotangent.reshape(128, 768)
+    (message,) = call(
         front,
-        [(16, 360, 128), (16, 8, 1152)],
+        [(16, 360, 128)],
         flag,
-        features.reshape(128, 768),
+        rows,
         dilated_weight,
-        cotangent.reshape(128, 768),
-        mixing_weight,
         query_weight,
         key_weight,
         value_weight,
-        fetched=((128, 768), (48, 1152), (128, 768), (384, 768), (768, 256), (768, 256), (768, 768)),
+        fetched=((128, 768), (48, 1152), (768, 256), (768, 256), (768, 768)),
     )
     got = lax.all_to_all(message, "ctx", 0, 0)
-    mixed, filters = call(attention, [(16, 120, 128), (384, 1152)], got, carry)
+    mixed, filters = call(attention, [(16, 120, 128), (384, 1152)], got, rows, slope, mixing_weight)
     others = other_core(filters)
     got = lax.all_to_all(mixed, "ctx", 0, 0)
-    attended, gated, mine, theirs = call(
+    attended, gated, lifted, slopes, theirs = call(
         middle,
-        [(128, 768), (128, 384), (16, 216, 128), (16, 216, 128)],
+        [(128, 768), (128, 384), (128, 384), (128, 1152), (16, 216, 128)],
         flag,
         got,
         output_weight,
@@ -310,14 +309,16 @@
         column_order(),
     )
     came = other_core(theirs)
-    (track,) = call(mixing, [(128, 768)], attended, gated, mixing_weight)
+    track, mine = call(
+        rest, [(128, 768), (16, 216, 128)], attended, gated, mixing_weight, lifted, slopes
+    )
     (message,) = call(joined, [(16, 264, 128)], mine, came, track)
     got = lax.all_to_all(message, "ctx", 0, 0)
-    grad, track = call(summed, [(4, 56, 128), (128, 768)], got)
+    grad, track = call(summed, [(4, 112, 128), (128, 768)], got)
     got = lax.all_to_all(grad, "dp", 0, 0, axis_index_groups=NEAR)
-    (grad,) = call(summed_again, [(4, 56, 128)], got)
+    (grad,) = call(summed_again, [(4, 112, 128)], got)
     got = lax.all_to_all(grad, "dp", 0, 0, axis_index_groups=FAR)
-    (grad,) = call(summed_again, [(8, 56, 128)], got)
+    (grad,) = call(summed_again, [(4, 112, 128)], got)
     got = lax.all_to_all(grad, "dp", 0, 0, axis_index_groups=CLOSE)
     (dilated_grad,) = call(ordered, [(48, 1152)], got, dtype=F32)
     return (track.reshape(2, 64, 768), dilated_grad)

time: 128 us -> 126 us (0.984)
  blocking collectives: 106 us -> 104 us
    all_to_all x1, blocking collectives: 12.8 us -> 11.1 us  [shards(): got = lax.all_to_all(grad, 'dp', 0, 0, axis_index_groups=CLOSE)]
  transfers between devices with their start and end apart: 2 -> 2, of which waited for: 1 -> 1; matrix products, arithmetic and copies ran while one was open for 0% -> 0% of each run, Pallas kernels for 0% -> 1%
where the time goes in v4:
time: 126 us
  blocking collectives  104 us (83%)
  Pallas kernels  10.1 us (8%)
  starting transfers between devices  9.25 us (7%)
  waiting for transfers between devices  1.35 us (1%)
    all_to_all x2, blocking collectives, shards(): got = lax.all_to_all(message, 'ctx', 0, 0)  45.8 us
    all_to_all x1, blocking collectives, shards(): got = lax.all_to_all(grad, 'dp', 0, 0, axis_index_groups=FAR)  23.9 us
    all_to_all x1, blocking collectives, shards(): got = lax.all_to_all(mixed, 'ctx', 0, 0)  13.5 us
    all_to_all x1, blocking collectives, shards(): got = lax.all_to_all(grad, 'dp', 0, 0, axis_index_groups=CLOSE)  11.1 us
    pallas_call x9, Pallas kernels, call(): pl.pallas_call(kernel, out_shape=[jax.ShapeDtypeStruct(shape, dtype) for...  10.1 us
    all_to_all x1, blocking collectives, shards(): got = lax.all_to_all(grad, 'dp', 0, 0, axis_index_groups=NEAR)  10 us
    ppermute x2, starting transfers between devices, other_core(): lax.ppermute(value, 'dp', [(source, source ^ 1) for source in range(32)])  9.25 us
  transfers between devices with their start and end apart: 2, of which 1 were waited for; matrix products, arithmetic and copies ran while one was open for 0% of the time, Pallas kernels for 1%

profile of v4, /device:TPU:1, one launch (start us, length us, event | category | flops | bytes accessed | tf_op | source)
XLA Modules:
  0.0 125.7 jit_solution(8189032295239748081)
XLA Ops:
  0.6 3.8 %shard_map.104 = bf16[16,360,128]{2,1,0:T(8,128)(2,1)} custom-call(s32[1]{0:T(128)} %bitcast.core, bf16[128,768]{1,0:T(8,128)(2,1)} %bitcast.4, bf16[48,1152]{1,0:T(8,128)(2,1)} %wd.1, bf16[768,256]{1,0:T(8,128)(2,1)} %wq.1, bf16[768,256]{1,0:T(8,128)(2,1)} %wk.1, bf16[768,768]{1,0:T(8,128)(2,1)} %wv.1), custom_call_target="tpu_custom_call" | custom-call | tf_op jit(solution)/shard_map/pallas_call | solution.py:249
  4.5 0.0 copy-start
  4.5 0.0 copy-start.3
  4.5 0.0 copy-start.4
  4.5 26.3 %all_to_all.30.got = bf16[16,360,128]{2,1,0:T(8,128)(2,1)S(1)} all-to-all(bf16[16,360,128]{2,1,0:T(8,128)(2,1)} %shard_map.104), channel_id=1, replica_groups=mesh['dp'=32,'ctx'=16] {'ctx'}, dimensions={0} | all-to-all | bytes 2949120 | tf_op jit(solution)/shard_map/all_to_all | solution.py:297
  30.9 0.0 copy-done
  30.9 0.0 copy-done.3
  30.9 0.0 copy-done.4
  30.9 0.0 copy-start.1
  30.9 0.0 copy-start.2
  30.9 1.3 %shard_map.105 = (bf16[16,120,128]{2,1,0:T(8,128)(2,1)S(1)}, bf16[384,1152]{1,0:T(8,128)(2,1)S(1)}) custom-call(bf16[16,360,128]{2,1,0:T(8,128)(2,1)S(1)} %all_to_all.30.got, bf16[128,768]{1,0:T(8,128)(2,1)S(1)} %bitcast.5, bf16[128,768]{1,0:T(8,128)(2,1)S(1)} %bitcast.6, bf16[384,768]{1,0:T(8,128)(2,1)S(1)} %copy-done), custom_call_target="tpu_custom_call" | custom-call | tf_op jit(solution)/shard_map/pallas_call | solution.py:249
  32.3 6.0 %collective-permute-start = (bf16[384,1152]{1,0:T(8,128)(2,1)S(1)}, bf16[384,1152]{1,0:T(8,128)(2,1)S(1)}, u32[]{:S(2)}, u32[]{:S(2)}) collective-permute-start(bf16[384,1152]{1,0:T(8,128)(2,1)S(1)} %get-tuple-element.14.filters), channel_id=1, source_target_pairs={{0,16},{16,0},{32,48},{48,32},{64,80},{80,64},{96,112},{112,96},{1... | collective-permute-start | bytes 2654216 | tf_op jit(solution)/shard_map/ppermute | solution.py:263
  38.3 13.5 %all_to_all.31.got = bf16[16,120,128]{2,1,0:T(8,128)(2,1)S(1)} all-to-all(bf16[16,120,128]{2,1,0:T(8,128)(2,1)S(1)} %get-tuple-element.13), channel_id=1, replica_groups=mesh['dp'=32,'ctx'=16] {'ctx'}, dimensions={0} | all-to-all | bytes 983040 | tf_op jit(solution)/shard_map/all_to_all | solution.py:300
  51.8 0.0 collective-permute-done.others
  51.8 0.0 copy-done.1
  51.8 0.0 copy-done.2
  51.8 2.3 %shard_map.106 = (bf16[128,768]{1,0:T(8,128)(2,1)S(1)}, bf16[128,384]{1,0:T(8,128)(2,1)S(1)}, bf16[128,384]{1,0:T(8,128)(2,1)S(1)}, bf16[128,1152]{1,0:T(8,128)(2,1)S(1)}, bf16[16,216,128]{2,1,0:T(8,128)(2,1)S(1)}) custom-call(s32[1]{0:T(128)} %bitcast.core, bf16[16,120,128]{2,1,0:T(8,128)(2,1)S(1)} %all_to_all.31.got, bf16[768,768]{1,0:T(8,128)(2,1)S(1)} %copy-done.1, ...), custom_call_target="tpu_custom_call" | custom-call | tf_op jit(solution)/shard_map/pallas_call | solution.py:249
  54.1 3.2 %collective-permute-start.1 = (bf16[16,216,128]{2,1,0:T(8,128)(2,1)S(1)}, bf16[16,216,128]{2,1,0:T(8,128)(2,1)S(1)}, u32[]{:S(2)}, u32[]{:S(2)}) collective-permute-start(bf16[16,216,128]{2,1,0:T(8,128)(2,1)S(1)} %get-tuple-element.20), channel_id=1, source_target_pairs={{0,16},{16,0},{32,48},{48,32},{64,80},{80,64},{96,112},{112,96},{1... | collective-permute-start | bytes 2654216 | tf_op jit(solution)/shard_map/ppermute | solution.py:263
  57.3 0.7 shard_map.107
  58.0 1.3 %collective-permute-done.1.came = bf16[16,216,128]{2,1,0:T(8,128)(2,1)S(1)} collective-permute-done((bf16[16,216,128]{2,1,0:T(8,128)(2,1)S(1)}, bf16[16,216,128]{2,1,0:T(8,128)(2,1)S(1)}, u32[]{:S(2)}, u32[]{:S(2)}) %collective-permute-start.1) | collective-permute-done | bytes 884768 | tf_op jit(solution)/shard_map/ppermute | solution.py:263
  59.3 0.2 shard_map.108
  59.5 19.4 %all_to_all.32.got = bf16[16,264,128]{2,1,0:T(8,128)(2,1)S(1)} all-to-all(bf16[16,264,128]{2,1,0:T(8,128)(2,1)S(1)} %shard_map.108), channel_id=1, replica_groups=mesh['dp'=32,'ctx'=16] {'ctx'}, dimensions={0} | all-to-all | bytes 2162688 | tf_op jit(solution)/shard_map/all_to_all | solution.py:316
  78.9 1.0 shard_map.109
  79.9 10.0 %all_to_all.33.got = bf16[4,112,128]{2,1,0:T(8,128)(2,1)S(1)} all-to-all(bf16[4,112,128]{2,1,0:T(8,128)(2,1)S(1)} %get-tuple-element.23), channel_id=1, replica_groups={{0,32,64,96},{128,160,192,224},{256,288,320,352},{384,416,448,480},{16,..., dimensions={0} | all-to-all | bytes 229376 | tf_op jit(solution)/shard_map/all_to_all | solution.py:318
  90.0 23.9 %all_to_all.34.got = bf16[4,112,128]{2,1,0:T(8,128)(2,1)S(1)} all-to-all(bf16[4,112,128]{2,1,0:T(8,128)(2,1)S(1)} %shard_map.110), channel_id=1, replica_groups={{0,128,256,384},{32,160,288,416},{64,192,320,448},{96,224,352,480},{16,..., dimensions={0} | all-to-all | bytes 229376 | tf_op jit(solution)/shard_map/all_to_all | solution.py:320
  113.9 11.1 %all_to_all.35.got = bf16[4,112,128]{2,1,0:T(8,128)(2,1)S(1)} all-to-all(bf16[4,112,128]{2,1,0:T(8,128)(2,1)S(1)} %shard_map.111), channel_id=1, replica_groups={{0,16,32,48},{64,80,96,112},{128,144,160,176},{192,208,224,240},{256,27..., dimensions={0} | all-to-all | bytes 229376 | tf_op jit(solution)/shard_map/all_to_all | solution.py:322
  125.0 0.7 shard_map.112
  (2 shorter events, 0.0 us)
Async XLA Ops:
  4.5 26.4 %copy-start = (bf16[384,768]{1,0:T(8,128)(2,1)S(1)}, bf16[384,768]{1,0:T(8,128)(2,1)}, u32[]{:S(2)}) copy-start(bf16[384,768]{1,0:T(8,128)(2,1)} %mix.3) | copy-start | bytes 1769476
  4.5 26.4 %copy-start.3 = (bf16[2,64,768]{2,1,0:T(8,128)(2,1)S(1)}, bf16[2,64,768]{2,1,0:T(8,128)(2,1)}, u32[]{:S(2)}) copy-start(bf16[2,64,768]{2,1,0:T(8,128)(2,1)} %param.9) | copy-start | bytes 589828
  4.5 26.4 %copy-start.4 = (bf16[2,64,768]{2,1,0:T(8,128)(2,1)S(1)}, bf16[2,64,768]{2,1,0:T(8,128)(2,1)}, u32[]{:S(2)}) copy-start(bf16[2,64,768]{2,1,0:T(8,128)(2,1)} %param.16) | copy-start | bytes 589828
  30.9 20.9 %copy-start.1 = (bf16[768,768]{1,0:T(8,128)(2,1)S(1)}, bf16[768,768]{1,0:T(8,128)(2,1)}, u32[]{:S(2)}) copy-start(bf16[768,768]{1,0:T(8,128)(2,1)} %wo.1) | copy-start | bytes 3538948
  30.9 20.9 %copy-start.2 = (bf16[768,768]{1,0:T(8,128)(2,1)S(1)}, bf16[768,768]{1,0:T(8,128)(2,1)}, u32[]{:S(2)}) copy-start(bf16[768,768]{1,0:T(8,128)(2,1)} %constant.21.clone.order) | copy-start | bytes 3538948
  32.3 19.5 %collective-permute-start = (bf16[384,1152]{1,0:T(8,128)(2,1)S(1)}, bf16[384,1152]{1,0:T(8,128)(2,1)S(1)}, u32[]{:S(2)}, u32[]{:S(2)}) collective-permute-start(bf16[384,1152]{1,0:T(8,128)(2,1)S(1)} %get-tuple-element.14.filters), channel_id=1, source_target_pairs={{0,16},{16,0},{32,48},{48,32},{64,80},{80,64},{96,112},{112,96},{1... | collective-permute-start | bytes 2654216 | tf_op jit(solution)/shard_map/ppermute | solution.py:263
  54.1 5.2 %collective-permute-start.1 = (bf16[16,216,128]{2,1,0:T(8,128)(2,1)S(1)}, bf16[16,216,128]{2,1,0:T(8,128)(2,1)S(1)}, u32[]{:S(2)}, u32[]{:S(2)}) collective-permute-start(bf16[16,216,128]{2,1,0:T(8,128)(2,1)S(1)} %get-tuple-element.20), channel_id=1, source_target_pairs={{0,16},{16,0},{32,48},{48,32},{64,80},{80,64},{96,112},{112,96},{1... | collective-permute-start | bytes 2654216 | tf_op jit(solution)/shard_map/ppermute | solution.py:263

commit v5 on v4

--- a/solution.py
+++ b/solution.py
@@ -2,7 +2,6 @@
 
 import jax
 import jax.numpy as jnp
-import numpy as np
 from jax import lax
 from jax.experimental import pallas as pl
 from jax.experimental.pallas import tpu as pltpu
@@ -12,6 +11,7 @@
 NEAR = [[2 * (4 * far + near) + core for near in range(4)] for core in range(2) for far in range(4)]
 FAR = [[2 * (4 * far + near) + core for far in range(4)] for core in range(2) for near in range(4)]
 CLOSE = [[4 * pair + member for member in range(4)] for pair in range(8)]
+ACROSS = [[4 * y + x for x in range(4)] for y in range(4)]
 F32, BF16 = jnp.float32, jnp.bfloat16
 VMEM = pl.BlockSpec(memory_space=pltpu.VMEM)
 SMEM = pl.BlockSpec(memory_space=pltpu.SMEM)
@@ -49,6 +49,16 @@
 
 def swap(tile):
     return pltpu.roll(tile, 64, 1)
+
+
+def strips(rows, parts):
+    lane = lax.broadcasted_iota(jnp.int32, (rows, 128), 1)
+    result = jnp.zeros((rows, 128), F32)
+    for tile, start, target, count in parts:
+        if start != target:
+            tile = pltpu.roll(tile, (target - start) % 128, 1)
+        result = jnp.where((lane >= target) & (lane < target + count), tile, result)
+    return result
 
 
 def lower_lanes(rows):
@@ -72,12 +82,15 @@
     copies[0].wait()
     normed = layer_norm(x_here[...].astype(F32)).astype(BF16)
     copies[1].wait()
-    filters = wd_here[...].astype(F32)
-    filters = jnp.where(core[0] == 0, filters[0:24], filters[24:48]).astype(BF16)
-    for t in range(9):
-        tile = filters[:, 128 * t : 128 * t + 128]
-        for j in range(16):
-            message[j, 144 + 24 * t : 168 + 24 * t, :] = tile
+    tiles = [wd_here[:, 128 * k : 128 * k + 128].astype(F32) for k in range(9)]
+    for x in range(4):
+        block = [
+            strips(48, [(tiles[4 * n + k], 32 * x, 32 * k, 32) for k in range(4)]) for n in range(2)
+        ]
+        block.append(strips(16, [(tiles[8][16 * m : 16 * m + 16], 32 * x, 32 * m, 32) for m in range(3)]))
+        block = jnp.concatenate(block, axis=0).astype(BF16)
+        for y in range(4):
+            message[4 * y + x, 144:256, :] = block
     for copy in copies[2:4]:
         copy.wait()
     q = head_norm(dot(normed, wq_here[...]))
@@ -126,26 +139,41 @@
             part = mixed[32 * j : 32 * j + 32]
             first = jnp.where(low16, swap(part[16:32, 0:128]), part[0:16, 0:128])
             out[4 * block + j, 0:48, :] = jnp.concatenate([first, part[:, 128:256]], axis=0).astype(BF16)
-    for t in range(9):
-        lanes = slice(128 * t, 128 * t + 128)
-        pieces = [got[i, 144 + 24 * t : 168 + 24 * t, :].astype(F32) for i in range(16)]
-        filters[:, lanes] = jnp.concatenate(pieces, axis=0).astype(BF16)
+    first = got[:, 144:192, :].reshape(768, 128).astype(F32)
+    second = got[:, 192:240, :].reshape(768, 128).astype(F32)
+    last = got[:, 240:256, :].reshape(256, 128).astype(F32)
+    thirds = [last, pltpu.roll(last, 96, 1), pltpu.roll(last, 64, 1)]
+    last = jnp.concatenate([t[16 * i : 16 * i + 16] for i in range(16) for t in thirds], axis=0)
+    filters[:, 0:128] = strips(768, [(first, 0, 0, 96)]).astype(BF16)
+    filters[:, 128:256] = strips(768, [(first, 96, 0, 32), (second, 0, 32, 64)]).astype(BF16)
+    filters[:, 256:384] = strips(768, [(second, 64, 0, 64), (last, 0, 64, 32)]).astype(BF16)
     to_bins = moves(128, lambda r, c: c == (((r >> 2) & 1) * 64 + (r >> 3) * 4 + (r & 3)))
     sent = dot(to_bins, x[...]).astype(BF16)
-    back = dot(dot(to_bins, cot[...]).astype(BF16), mix[...], ((1,), (1,))).astype(BF16)
-    for t in range(9):
-        rows = sent[:, 128 * t : 128 * t + 128] if t < 6 else back[:, 128 * t - 768 : 128 * t - 640]
+    for t in range(6):
         for j in range(16):
-            out[j, 48 + 8 * t : 56 + 8 * t, :] = rows[8 * j : 8 * j + 8]
-
-
-def middle(core, got, wo, filters, others, order, attended, gated, own, slopes, theirs):
-    to_groups = moves(128, lambda r, c: c == (((r >> 1) & 15) * 8 + (r >> 5) * 2 + (r & 1)))
+            out[j, 48 + 8 * t : 56 + 8 * t, :] = sent[8 * j : 8 * j + 8, 128 * t : 128 * t + 128]
+    back = dot(dot(to_bins, cot[...]).astype(BF16), mix[...], ((1,), (1,)))
+    for quarter in range(4):
+        part = strips(128, [(back[:, 128 * t : 128 * t + 128], 32 * quarter, 32 * t, 32) for t in range(3)])
+        part = part.astype(BF16)
+        for y in range(4):
+            out[4 * y + quarter, 96:128, :] = part[32 * y : 32 * y + 32]
+
+
+def to_groups():
+    return moves(128, lambda r, c: c == (((r >> 1) & 15) * 8 + (r >> 5) * 2 + (r & 1)))
+
+
+def to_blocks():
+    return moves(128, lambda r, c: c == (((r >> 1) & 3) * 32 + (r >> 3) * 2 + (r & 1)))
+
+
+def attend(got, wo):
     sent = []
-    for t in range(9):
+    for t in range(6):
         rows = [got[i, 48 + 8 * t : 56 + 8 * t, :].astype(F32) for i in range(16)]
         sent.append(jnp.concatenate(rows, axis=0).astype(BF16))
-    sent = dot(to_groups, jnp.concatenate(sent, axis=1))
+    sent = dot(to_groups(), jnp.concatenate(sent, axis=1))
     low16 = lower_lanes(16)
     tiles = []
     for pair in range(2):
@@ -159,73 +187,101 @@
                 groups[2].append(odd[16:48])
         tiles += [jnp.concatenate(g, axis=0) for g in groups]
     mixed = jnp.concatenate(tiles, axis=1).astype(BF16)
-    result = (sent[:, 0:768] + dot(mixed, wo[...])).astype(BF16)
-    attended[...] = result
-    normed = layer_norm(result.astype(F32))
-    lifted = (normed * normal_cdf(normed)).astype(BF16)
-    lifted = dot(lifted, order[...])
-    first, second = lifted[:, 0:384], lifted[:, 384:768]
-    lifted = (
-        jnp.where(core[0] == 0, first, second).astype(BF16),
-        jnp.where(core[0] == 0, second, first).astype(BF16),
-    )
-    from_below = moves(128, lambda r, c: (c == r - 4) & ((r & 31) >= 4))
-    from_above = moves(128, lambda r, c: (c == r + 4) & ((r & 31) < 28))
-    weights = (filters, others)
-    hidden = jnp.zeros((128, 384), F32)
-    for part in range(2):
-        below = dot(from_below, lifted[part]).astype(BF16)
-        above = dot(from_above, lifted[part]).astype(BF16)
-        for tap, rows in enumerate((below, lifted[part], above)):
-            hidden = hidden + dot(rows, weights[part][:, 384 * tap : 384 * tap + 384])
+    return (sent + dot(mixed, wo[...])).astype(BF16)
+
+
+def middle(got, wo, lifted):
+    normed = layer_norm(attend(got, wo).astype(F32))
+    result = (normed * normal_cdf(normed)).astype(BF16)
+    for x in range(4):
+        lifted[x] = result
+
+
+def filtered(core, lifted, got, filters, gated, mine, theirs):
+    rows = lifted[...].reshape(512, 768)
+    taps = dot(rows, filters[...])
+    place = lax.broadcasted_iota(jnp.int32, (512, 128), 0) & 31
+
+    def from_below(tile):
+        return jnp.where(place >= 4, pltpu.roll(tile, 4, 0), 0.0)
+
+    def from_above(tile):
+        return jnp.where(place < 28, pltpu.roll(tile, 508, 0), 0.0)
+
+    hidden = from_below(taps[:, 0:128]) + taps[:, 128:256] + from_above(taps[:, 256:384])
     cdf = normal_cdf(hidden)
     gated[...] = (hidden * cdf).astype(BF16)
     pdf = jnp.exp(-0.5 * hidden * hidden) * (1.0 / math.sqrt(2.0 * math.pi))
-    slope = (sent[:, 768:1152] * (cdf + hidden * pdf)).astype(BF16)
-    own[...] = lifted[0]
-    slopes[:, 0:384] = dot(from_above, slope).astype(BF16)
-    slopes[:, 384:768] = slope
-    slopes[:, 768:1152] = dot(from_below, slope).astype(BF16)
-    gradient(lifted[1], slopes, theirs)
-
-
-def gradient(lifted, slopes, target):
-    for tap in range(3):
-        grad = dot(lifted, slopes[:, 384 * tap : 384 * tap + 384], ((0,), (0,)))
-        for d in range(16):
-            for t in range(3):
-                start = 24 * (3 * tap + t)
-                tile = grad[24 * d : 24 * d + 24, 128 * t : 128 * t + 128]
-                target[d, start : start + 24, :] = tile.astype(BF16)
-
-
-def rest(attended, gated, mix, lifted, slopes, track, mine):
-    result = (attended[...].astype(F32) + dot(gated[...], mix[...])).astype(BF16)
-    by_block = moves(128, lambda r, c: c == (((r >> 1) & 3) * 32 + (r >> 3) * 2 + (r & 1)))
-    track[...] = dot(by_block, result).astype(BF16)
-    gradient(lifted[...], slopes, mine)
-
-
-def joined(mine, came, track, message):
+    back = []
+    for x in range(4):
+        part = [got[i, 96 + 8 * x : 104 + 8 * x, :].astype(F32) for i in range(16)]
+        back.append(dot(to_groups(), jnp.concatenate(part, axis=0).astype(BF16)))
+    slope = jnp.concatenate(back, axis=0) * (cdf + hidden * pdf)
+    slope = slope.astype(BF16).astype(F32)
+    below, above = from_above(slope), from_below(slope)
+    packed = [
+        strips(512, [(below, 0, 0, 96), (slope, 0, 96, 32)]),
+        strips(512, [(slope, 32, 0, 64), (above, 0, 64, 64)]),
+        strips(512, [(above, 64, 0, 32)]),
+    ]
+    packed = jnp.concatenate(packed, axis=1).astype(BF16)
+    grad = dot(rows, packed, ((0,), (0,)))
     for d in range(16):
-        for t in range(6):
-            message[d, 8 * t : 8 * t + 8, :] = track[8 * d : 8 * d + 8, 128 * t : 128 * t + 128]
-        message[d, 48:264, :] = (mine[d].astype(F32) + came[d].astype(F32)).astype(BF16)
-
-
-def summed(got, grad, track):
-    total = got[0, 48:264, :].astype(F32)
-    for d in range(1, 16):
-        total = total + got[d, 48:264, :].astype(F32)
-    total = jnp.concatenate([total, jnp.zeros((8, 128), F32)], axis=0)
+        halves = []
+        for half in range(2):
+            start = 48 * d + 24 * half
+            part = grad[start : start + 24]
+            last = strips(8, [(part[8 * m : 8 * m + 8, 256:384], 0, 32 * m, 32) for m in range(3)])
+            halves.append(jnp.concatenate([part[:, 0:128], part[:, 128:256], last], axis=0))
+        theirs[d] = jnp.where(core[0] == 0, halves[1], halves[0]).astype(BF16)
+        mine[d] = jnp.where(core[0] == 0, halves[0], halves[1]).astype(BF16)
+
+
+def rest(got, wo, gated, head):
+    rows = dot(to_blocks(), attend(got, wo))
+    gated = [dot(to_blocks(), gated[128 * x : 128 * x + 128, :]) for x in range(4)]
+    gated = [strips(128, [(gated[m], 0, 0, 96), (gated[3], 32 * m, 96, 32)]) for m in range(3)]
+    for i in range(16):
+        block = slice(8 * i, 8 * i + 8)
+        parts = [rows[block, 128 * t : 128 * t + 128] for t in range(6)] + [g[block] for g in gated]
+        head[i] = jnp.concatenate(parts, axis=0).astype(BF16)
+
+
+def joined(mine, came, head, message):
+    for d in range(16):
+        grad = mine[d].astype(F32) + came[d].astype(F32)
+        message[d] = jnp.concatenate([grad, head[d].astype(F32)], axis=0).astype(BF16)
+
+
+def summed(got, mix, grad, track):
+    total = []
+    for x in range(4):
+        part = got[x, 0:56, :].astype(F32)
+        for y in range(1, 4):
+            part = part + got[4 * y + x, 0:56, :].astype(F32)
+        total.append(part)
     for near in range(4):
-        half = 112 * (near % 2)
-        grad[near] = total[half : half + 112].astype(BF16)
+        half = 2 * (near % 2)
+        grad[near] = jnp.concatenate(total[half : half + 2], axis=0).astype(BF16)
     natural = moves(128, lambda r, c: c == (((r >> 2) & 15) * 8 + (r >> 6) * 4 + (r & 3)))
+    gated, weights = [], []
+    for x in range(4):
+        rows = []
+        for y in range(4):
+            part = got[4 * y + x, 104:128, :].astype(F32)
+            part = [part[8 * m : 8 * m + 8] for m in range(3)]
+            rows += [strips(8, [(p, 0, 0, 96)]) for p in part]
+            rows.append(strips(8, [(part[m], 96, 32 * m, 32) for m in range(3)]))
+        gated.append(jnp.concatenate(rows, axis=0).astype(BF16))
+        weights += [mix[128 * t + 32 * x : 128 * t + 32 * x + 32, :] for t in range(3)]
+        weights.append(jnp.zeros((32, 768), BF16))
+    attended = []
     for t in range(6):
-        rows = [got[d, 8 * t : 8 * t + 8, :].astype(F32) for d in range(16)]
-        rows = dot(natural, jnp.concatenate(rows, axis=0).astype(BF16))
-        track[:, 128 * t : 128 * t + 128] = rows.astype(BF16)
+        rows = [got[d, 56 + 8 * t : 64 + 8 * t, :].astype(F32) for d in range(16)]
+        attended.append(jnp.concatenate(rows, axis=0).astype(BF16))
+    gated = dot(natural, jnp.concatenate(gated, axis=1)).astype(BF16)
+    attended = dot(natural, jnp.concatenate(attended, axis=1))
+    track[...] = (attended + dot(gated, jnp.concatenate(weights, axis=0))).astype(BF16)
 
 
 def summed_again(got, grad):
@@ -237,9 +293,15 @@
 
 def ordered(got, grad):
     for core in range(2):
-        rows = jnp.concatenate([got[2 * half + core].astype(F32) for half in range(2)], axis=0)
-        for t in range(9):
-            grad[24 * core : 24 * core + 24, 128 * t : 128 * t + 128] = rows[24 * t : 24 * t + 24]
+        sources = []
+        for x in range(4):
+            part = got[2 * (x // 2) + core, 56 * (x % 2) : 56 * (x % 2) + 56, :].astype(F32)
+            last = part[48:56]
+            last = jnp.concatenate([last, pltpu.roll(last, 96, 1), pltpu.roll(last, 64, 1)], axis=0)
+            sources.append((part[0:24], part[24:48], last))
+        for k in range(9):
+            tile = strips(24, [(sources[x][k // 4], 32 * (k % 4), 32 * x, 32) for x in range(4)])
+            grad[24 * core : 24 * core + 24, 128 * k : 128 * k + 128] = tile
 
 
 def call(kernel, outs, *args, dtype=BF16, fetched=()):
@@ -263,13 +325,6 @@
     return lax.ppermute(value, "dp", [(source, source ^ 1) for source in range(32)])
 
 
-def column_order():
-    order = np.zeros((768, 768), np.float32)
-    target = np.arange(768)
-    order[(target % 384) // 24 * 48 + target // 384 * 24 + target % 24, target] = 1.0
-    return jnp.asarray(order, BF16)
-
-
 def shards(
     features,
     query_weight,
@@ -285,7 +340,7 @@
     rows, slope = features.reshape(128, 768), cotangent.reshape(128, 768)
     (message,) = call(
         front,
-        [(16, 360, 128)],
+        [(16, 256, 128)],
         flag,
         rows,
         dilated_weight,
@@ -295,26 +350,18 @@
         fetched=((128, 768), (48, 1152), (768, 256), (768, 256), (768, 768)),
     )
     got = lax.all_to_all(message, "ctx", 0, 0)
-    mixed, filters = call(attention, [(16, 120, 128), (384, 1152)], got, rows, slope, mixing_weight)
-    others = other_core(filters)
+    mixed, filters = call(attention, [(16, 128, 128), (768, 384)], got, rows, slope, mixing_weight)
     got = lax.all_to_all(mixed, "ctx", 0, 0)
-    attended, gated, lifted, slopes, theirs = call(
-        middle,
-        [(128, 768), (128, 384), (128, 384), (128, 1152), (16, 216, 128)],
-        flag,
-        got,
-        output_weight,
-        filters,
-        others,
-        column_order(),
+    (lifted,) = call(middle, [(4, 128, 768)], got, output_weight)
+    lifted = lax.all_to_all(lifted, "ctx", 0, 0, axis_index_groups=ACROSS)
+    gated, mine, theirs = call(
+        filtered, [(512, 128), (16, 56, 128), (16, 56, 128)], flag, lifted, got, filters
     )
     came = other_core(theirs)
-    track, mine = call(
-        rest, [(128, 768), (16, 216, 128)], attended, gated, mixing_weight, lifted, slopes
-    )
-    (message,) = call(joined, [(16, 264, 128)], mine, came, track)
+    (head,) = call(rest, [(16, 72, 128)], got, output_weight, gated)
+    (message,) = call(joined, [(16, 128, 128)], mine, came, head)
     got = lax.all_to_all(message, "ctx", 0, 0)
-    grad, track = call(summed, [(4, 112, 128), (128, 768)], got)
+    grad, track = call(summed, [(4, 112, 128), (128, 768)], got, mixing_weight)
     got = lax.all_to_all(grad, "dp", 0, 0, axis_index_groups=NEAR)
     (grad,) = call(summed_again, [(4, 112, 128)], got)
     got = lax.all_to_all(grad, "dp", 0, 0, axis_index_groups=FAR)

time: 126 us -> 125 us (level)
    all_to_all x0 -> x1, blocking collectives: none -> 10.7 us  [shards(): lifted = lax.all_to_all(lifted, 'ctx', 0, 0, axis_index_groups=ACROSS)]
    all_to_all x2, blocking collectives: 45.8 us -> 35.3 us  [shards(): got = lax.all_to_all(message, 'ctx', 0, 0)]
    all_to_all x1, blocking collectives: 10 us -> 11.8 us  [shards(): got = lax.all_to_all(grad, 'dp', 0, 0, axis_index_groups=NEAR)]
    all_to_all x1, blocking collectives: 13.5 us -> 12 us  [shards(): got = lax.all_to_all(mixed, 'ctx', 0, 0)]
    ppermute x2 -> x1, starting transfers between devices: 9.25 us -> 8.14 us  [other_core(): lax.ppermute(value, 'dp', [(source, source ^ 1) for source in range(32)])]
    pallas_call x9 -> x10, Pallas kernels: 10.1 us -> 10.1 us  [call(): pl.pallas_call(kernel, out_shape=[jax.ShapeDtypeStruct(shape, dtype) for...]
  transfers between devices with their start and end apart: 2 -> 1, of which waited for: 1 -> 1; matrix products, arithmetic and copies ran while one was open for 0% -> 0% of each run, Pallas kernels for 1% -> 1%
where the time goes in v5:
time: 125 us; the launch traced here: 124 us
  blocking collectives  105 us (84%)
  Pallas kernels  10.1 us (8%)
  starting transfers between devices  8.14 us (7%)
    all_to_all x2, blocking collectives, shards(): got = lax.all_to_all(message, 'ctx', 0, 0)  35.3 us
    all_to_all x1, blocking collectives, shards(): got = lax.all_to_all(grad, 'dp', 0, 0, axis_index_groups=FAR)  24 us
    all_to_all x1, blocking collectives, shards(): got = lax.all_to_all(mixed, 'ctx', 0, 0)  12 us
    all_to_all x1, blocking collectives, shards(): got = lax.all_to_all(grad, 'dp', 0, 0, axis_index_groups=NEAR)  11.8 us
    all_to_all x1, blocking collectives, shards(): got = lax.all_to_all(grad, 'dp', 0, 0, axis_index_groups=CLOSE)  11 us
    all_to_all x1, blocking collectives, shards(): lifted = lax.all_to_all(lifted, 'ctx', 0, 0, axis_index_groups=ACROSS)  10.7 us
    pallas_call x10, Pallas kernels, call(): pl.pallas_call(kernel, out_shape=[jax.ShapeDtypeStruct(shape, dtype) for...  10.1 us
    ppermute x1, starting transfers between devices, other_core(): lax.ppermute(value, 'dp', [(source, source ^ 1) for source in range(32)])  8.14 us
  transfers between devices with their start and end apart: 1, of which 1 were waited for; matrix products, arithmetic and copies ran while one was open for 0% of the time, Pallas kernels for 1%

profile of v5, /device:TPU:1, one launch (start us, length us, event | category | flops | bytes accessed | tf_op | source)
XLA Modules:
  0.0 124.1 jit_solution(13496421014299456043)
XLA Ops:
  0.6 3.7 %shard_map.95 = bf16[16,256,128]{2,1,0:T(8,128)(2,1)} custom-call(s32[1]{0:T(128)} %bitcast.core, bf16[128,768]{1,0:T(8,128)(2,1)} %bitcast.4, bf16[48,1152]{1,0:T(8,128)(2,1)} %wd.1, bf16[768,256]{1,0:T(8,128)(2,1)} %wq.1, bf16[768,256]{1,0:T(8,128)(2,1)} %wk.1, bf16[768,768]{1,0:T(8,128)(2,1)} %wv.1), custom_call_target="tpu_custom_call" | custom-call | tf_op jit(solution)/shard_map/pallas_call | solution.py:311
  4.4 0.0 copy-start.1
  4.4 0.0 copy-start.2
  4.4 0.0 copy-start.3
  4.4 21.8 %all_to_all.35.got = bf16[16,256,128]{2,1,0:T(8,128)(2,1)S(1)} all-to-all(bf16[16,256,128]{2,1,0:T(8,128)(2,1)} %shard_map.95), channel_id=1, replica_groups=mesh['dp'=32,'ctx'=16] {'ctx'}, dimensions={0} | all-to-all | bytes 2097152 | tf_op jit(solution)/shard_map/all_to_all | solution.py:352
  26.2 0.0 copy-done.1
  26.2 0.0 copy-done.2
  26.2 0.0 copy-done.3
  26.2 0.0 copy-start
  26.3 1.4 %shard_map.96 = (bf16[16,128,128]{2,1,0:T(8,128)(2,1)S(1)}, bf16[768,384]{1,0:T(8,128)(2,1)S(1)}) custom-call(bf16[16,256,128]{2,1,0:T(8,128)(2,1)S(1)} %all_to_all.35.got, bf16[128,768]{1,0:T(8,128)(2,1)S(1)} %bitcast.5, bf16[128,768]{1,0:T(8,128)(2,1)S(1)} %bitcast.6, bf16[384,768]{1,0:T(8,128)(2,1)S(1)} %copy-done.1), custom_call_target="tpu_custom_call" | custom-call | tf_op jit(solution)/shard_map/pallas_call | solution.py:311
  27.6 12.0 %all_to_all.36.got = bf16[16,128,128]{2,1,0:T(8,128)(2,1)S(1)} all-to-all(bf16[16,128,128]{2,1,0:T(8,128)(2,1)S(1)} %get-tuple-element.9), channel_id=1, replica_groups=mesh['dp'=32,'ctx'=16] {'ctx'}, dimensions={0} | all-to-all | bytes 1048576 | tf_op jit(solution)/shard_map/all_to_all | solution.py:354
  39.6 0.0 copy-done
  39.7 0.7 shard_map.97
  40.3 10.7 %all_to_all.37.lifted = bf16[4,128,768]{2,1,0:T(8,128)(2,1)S(1)} all-to-all(bf16[4,128,768]{2,1,0:T(8,128)(2,1)S(1)} %shard_map.97), channel_id=1, replica_groups={{0,1,2,3},{4,5,6,7},{8,9,10,11},{12,13,14,15},{16,17,18,19},{20,21,22,2..., dimensions={0} | all-to-all | bytes 1572864 | tf_op jit(solution)/shard_map/all_to_all | solution.py:356
  51.1 1.4 %shard_map.98 = (bf16[512,128]{1,0:T(8,128)(2,1)S(1)}, bf16[16,56,128]{2,1,0:T(8,128)(2,1)S(1)}, bf16[16,56,128]{2,1,0:T(8,128)(2,1)S(1)}) custom-call(s32[1]{0:T(128)} %bitcast.core, bf16[4,128,768]{2,1,0:T(8,128)(2,1)S(1)} %all_to_all.37.lifted, bf16[16,128,128]{2,1,0:T(8,128)(2,1)S(1)} %all_to_all.36.got, bf16[768,384]{1,0:T(8,128)(2,1)S(1)} %get-tuple-element.10.filters), custom_call_target="tpu_custom_call" | custom-call | tf_op jit(solution)/shard_map/pallas_call | solution.py:311
  52.4 8.1 %collective-permute-start = (bf16[16,56,128]{2,1,0:T(8,128)(2,1)S(1)}, bf16[16,56,128]{2,1,0:T(8,128)(2,1)S(1)}, u32[]{:S(2)}, u32[]{:S(2)}) collective-permute-start(bf16[16,56,128]{2,1,0:T(8,128)(2,1)S(1)} %get-tuple-element.12), channel_id=1, source_target_pairs={{0,16},{16,0},{32,48},{48,32},{64,80},{80,64},{96,112},{112,96},{1... | collective-permute-start | bytes 688136 | tf_op jit(solution)/shard_map/ppermute | solution.py:325
  60.6 0.8 shard_map.99.head
  61.4 0.3 collective-permute-done.came
  61.7 0.1 shard_map.100
  61.7 13.5 %all_to_all.38.got = bf16[16,128,128]{2,1,0:T(8,128)(2,1)S(1)} all-to-all(bf16[16,128,128]{2,1,0:T(8,128)(2,1)S(1)} %shard_map.100), channel_id=1, replica_groups=mesh['dp'=32,'ctx'=16] {'ctx'}, dimensions={0} | all-to-all | bytes 1048576 | tf_op jit(solution)/shard_map/all_to_all | solution.py:363
  75.2 1.2 shard_map.101
  76.4 11.8 %all_to_all.39.got = bf16[4,112,128]{2,1,0:T(8,128)(2,1)S(1)} all-to-all(bf16[4,112,128]{2,1,0:T(8,128)(2,1)S(1)} %get-tuple-element.15), channel_id=1, replica_groups={{0,32,64,96},{128,160,192,224},{256,288,320,352},{384,416,448,480},{16,..., dimensions={0} | all-to-all | bytes 229376 | tf_op jit(solution)/shard_map/all_to_all | solution.py:365
  88.2 24.0 %all_to_all.40.got = bf16[4,112,128]{2,1,0:T(8,128)(2,1)S(1)} all-to-all(bf16[4,112,128]{2,1,0:T(8,128)(2,1)S(1)} %shard_map.102), channel_id=1, replica_groups={{0,128,256,384},{32,160,288,416},{64,192,320,448},{96,224,352,480},{16,..., dimensions={0} | all-to-all | bytes 229376 | tf_op jit(solution)/shard_map/all_to_all | solution.py:367
  112.2 11.0 %all_to_all.41.got = bf16[4,112,128]{2,1,0:T(8,128)(2,1)S(1)} all-to-all(bf16[4,112,128]{2,1,0:T(8,128)(2,1)S(1)} %shard_map.103), channel_id=1, replica_groups={{0,16,32,48},{64,80,96,112},{128,144,160,176},{192,208,224,240},{256,27..., dimensions={0} | all-to-all | bytes 229376 | tf_op jit(solution)/shard_map/all_to_all | solution.py:369
  123.3 0.9 shard_map.104
  (2 shorter events, 0.0 us)
Async XLA Ops:
  4.4 21.8 %copy-start.1 = (bf16[384,768]{1,0:T(8,128)(2,1)S(1)}, bf16[384,768]{1,0:T(8,128)(2,1)}, u32[]{:S(2)}) copy-start(bf16[384,768]{1,0:T(8,128)(2,1)} %mix.3) | copy-start | bytes 1769476
  4.4 21.8 %copy-start.2 = (bf16[2,64,768]{2,1,0:T(8,128)(2,1)S(1)}, bf16[2,64,768]{2,1,0:T(8,128)(2,1)}, u32[]{:S(2)}) copy-start(bf16[2,64,768]{2,1,0:T(8,128)(2,1)} %param.8) | copy-start | bytes 589828
  4.4 21.8 %copy-start.3 = (bf16[2,64,768]{2,1,0:T(8,128)(2,1)S(1)}, bf16[2,64,768]{2,1,0:T(8,128)(2,1)}, u32[]{:S(2)}) copy-start(bf16[2,64,768]{2,1,0:T(8,128)(2,1)} %param.15) | copy-start | bytes 589828
  26.2 13.4 %copy-start = (bf16[768,768]{1,0:T(8,128)(2,1)S(1)}, bf16[768,768]{1,0:T(8,128)(2,1)}, u32[]{:S(2)}) copy-start(bf16[768,768]{1,0:T(8,128)(2,1)} %wo.3) | copy-start | bytes 3538948
  52.4 9.2 %collective-permute-start = (bf16[16,56,128]{2,1,0:T(8,128)(2,1)S(1)}, bf16[16,56,128]{2,1,0:T(8,128)(2,1)S(1)}, u32[]{:S(2)}, u32[]{:S(2)}) collective-permute-start(bf16[16,56,128]{2,1,0:T(8,128)(2,1)S(1)} %get-tuple-element.12), channel_id=1, source_target_pairs={{0,16},{16,0},{32,48},{48,32},{64,80},{80,64},{96,112},{112,96},{1... | collective-permute-start | bytes 688136 | tf_op jit(solution)/shard_map/ppermute | solution.py:325

commit v6 on v5

--- a/solution.py
+++ b/solution.py
@@ -155,9 +155,12 @@
     back = dot(dot(to_bins, cot[...]).astype(BF16), mix[...], ((1,), (1,)))
     for quarter in range(4):
         part = strips(128, [(back[:, 128 * t : 128 * t + 128], 32 * quarter, 32 * t, 32) for t in range(3)])
-        part = part.astype(BF16)
         for y in range(4):
-            out[4 * y + quarter, 96:128, :] = part[32 * y : 32 * y + 32]
+            rows = part[32 * y : 32 * y + 32]
+            rows = [
+                strips(8, [(rows[8 * m : 8 * m + 8], 0, 0, 96), (rows[24:32], 32 * m, 96, 32)]) for m in range(3)
+            ]
+            out[4 * y + quarter, 96:120, :] = jnp.concatenate(rows, axis=0).astype(BF16)
 
 
 def to_groups():
@@ -213,9 +216,10 @@
     gated[...] = (hidden * cdf).astype(BF16)
     pdf = jnp.exp(-0.5 * hidden * hidden) * (1.0 / math.sqrt(2.0 * math.pi))
     back = []
+    came = [jnp.concatenate([got[i, 96 + 8 * m : 104 + 8 * m, :].astype(F32) for i in range(16)], axis=0) for m in range(3)]
     for x in range(4):
-        part = [got[i, 96 + 8 * x : 104 + 8 * x, :].astype(F32) for i in range(16)]
-        back.append(dot(to_groups(), jnp.concatenate(part, axis=0).astype(BF16)))
+        part = [(came[x], 0, 0, 96)] if x < 3 else [(came[m], 96, 32 * m, 32) for m in range(3)]
+        back.append(dot(to_groups(), strips(128, part).astype(BF16)))
     slope = jnp.concatenate(back, axis=0) * (cdf + hidden * pdf)
     slope = slope.astype(BF16).astype(F32)
     below, above = from_above(slope), from_below(slope)
@@ -237,20 +241,19 @@
         mine[d] = jnp.where(core[0] == 0, halves[0], halves[1]).astype(BF16)
 
 
-def rest(got, wo, gated, head):
+def rest(got, wo, gated, message):
     rows = dot(to_blocks(), attend(got, wo))
     gated = [dot(to_blocks(), gated[128 * x : 128 * x + 128, :]) for x in range(4)]
     gated = [strips(128, [(gated[m], 0, 0, 96), (gated[3], 32 * m, 96, 32)]) for m in range(3)]
     for i in range(16):
         block = slice(8 * i, 8 * i + 8)
         parts = [rows[block, 128 * t : 128 * t + 128] for t in range(6)] + [g[block] for g in gated]
-        head[i] = jnp.concatenate(parts, axis=0).astype(BF16)
-
-
-def joined(mine, came, head, message):
+        message[i, 56:128, :] = jnp.concatenate(parts, axis=0).astype(BF16)
+
+
+def joined(mine, came, begun, message):
     for d in range(16):
-        grad = mine[d].astype(F32) + came[d].astype(F32)
-        message[d] = jnp.concatenate([grad, head[d].astype(F32)], axis=0).astype(BF16)
+        message[d, 0:56, :] = (mine[d].astype(F32) + came[d].astype(F32)).astype(BF16)
 
 
 def summed(got, mix, grad, track):
@@ -291,7 +294,12 @@
         grad[copy] = total
 
 
-def ordered(got, grad):
+def ordered(got, rows, target, track, grad, semaphores):
+    copies = [
+        pltpu.make_async_copy(rows, track, semaphores.at[0]),
+        pltpu.make_async_copy(grad, target, semaphores.at[1]),
+    ]
+    copies[0].start()
     for core in range(2):
         sources = []
         for x in range(4):
@@ -302,22 +310,26 @@
         for k in range(9):
             tile = strips(24, [(sources[x][k // 4], 32 * (k % 4), 32 * x, 32) for x in range(4)])
             grad[24 * core : 24 * core + 24, 128 * k : 128 * k + 128] = tile
-
-
-def call(kernel, outs, *args, dtype=BF16, fetched=()):
-    scratch = [pltpu.VMEM(shape, BF16) for shape in fetched]
-    if fetched:
-        scratch.append(pltpu.SemaphoreType.DMA((8,)))
+    copies[1].start()
+    for copy in copies:
+        copy.wait()
+
+
+def call(kernel, outs, *args, fetched=(), copies=0, in_hbm=(), out_hbm=(), limit=32, alias={}):
+    hbm = pl.BlockSpec(memory_space=pl.ANY)
     return pl.pallas_call(
         kernel,
-        out_shape=[jax.ShapeDtypeStruct(shape, dtype) for shape in outs],
+        out_shape=[jax.ShapeDtypeStruct(out[1:], F32) if out[0] == F32 else jax.ShapeDtypeStruct(out, BF16) for out in outs],
         in_specs=[
-            SMEM if a.dtype == jnp.int32 else pl.BlockSpec(memory_space=pl.ANY) if fetched else VMEM
-            for a in args
+            SMEM if a.dtype == jnp.int32 else hbm if n in in_hbm else VMEM for n, a in enumerate(args)
         ],
-        out_specs=[VMEM] * len(outs),
-        scratch_shapes=scratch,
-        compiler_params=pltpu.CompilerParams(vmem_limit_bytes=(56 if fetched else 32) * 1024 * 1024),
+        out_specs=[hbm if n in out_hbm else VMEM for n in range(len(outs))],
+        scratch_shapes=[
+            pltpu.VMEM(shape[1:], F32) if shape[0] == F32 else pltpu.VMEM(shape, BF16) for shape in fetched
+        ]
+        + ([pltpu.SemaphoreType.DMA((copies,))] if copies else []),
+        input_output_aliases=alias,
+        compiler_params=pltpu.CompilerParams(vmem_limit_bytes=limit * 1024 * 1024),
     )(*args)
 
 
@@ -348,9 +360,12 @@
         key_weight,
         value_weight,
         fetched=((128, 768), (48, 1152), (768, 256), (768, 256), (768, 768)),
+        copies=8,
+        in_hbm=(1, 2, 3, 4, 5),
+        limit=56,
     )
     got = lax.all_to_all(message, "ctx", 0, 0)
-    mixed, filters = call(attention, [(16, 128, 128), (768, 384)], got, rows, slope, mixing_weight)
+    mixed, filters = call(attention, [(16, 120, 128), (768, 384)], got, rows, slope, mixing_weight)
     got = lax.all_to_all(mixed, "ctx", 0, 0)
     (lifted,) = call(middle, [(4, 128, 768)], got, output_weight)
     lifted = lax.all_to_all(lifted, "ctx", 0, 0, axis_index_groups=ACROSS)
@@ -358,8 +373,8 @@
         filtered, [(512, 128), (16, 56, 128), (16, 56, 128)], flag, lifted, got, filters
     )
     came = other_core(theirs)
-    (head,) = call(rest, [(16, 72, 128)], got, output_weight, gated)
-    (message,) = call(joined, [(16, 128, 128)], mine, came, head)
+    (message,) = call(rest, [(16, 128, 128)], got, output_weight, gated)
+    (message,) = call(joined, [(16, 128, 128)], mine, came, message, alias={2: 0})
     got = lax.all_to_all(message, "ctx", 0, 0)
     grad, track = call(summed, [(4, 112, 128), (128, 768)], got, mixing_weight)
     got = lax.all_to_all(grad, "dp", 0, 0, axis_index_groups=NEAR)
@@ -367,7 +382,9 @@
     got = lax.all_to_all(grad, "dp", 0, 0, axis_index_groups=FAR)
     (grad,) = call(summed_again, [(4, 112, 128)], got)
     got = lax.all_to_all(grad, "dp", 0, 0, axis_index_groups=CLOSE)
-    (dilated_grad,) = call(ordered, [(48, 1152)], got, dtype=F32)
+    dilated_grad, track = call(
+        ordered, [(F32, 48, 1152), (128, 768)], got, track, fetched=((F32, 48, 1152),), copies=2, out_hbm=(0, 1)
+    )
     return (track.reshape(2, 64, 768), dilated_grad)
 
 

time: 125 us -> 124 us (level)
  no operation moved by 1% of the time
where the time goes in v6:
time: 124 us; the launch traced here: 123 us
  blocking collectives  104 us (84%)
  Pallas kernels  9.53 us (8%)
  starting transfers between devices  8.17 us (7%)
    all_to_all x2, blocking collectives, shards(): got = lax.all_to_all(message, 'ctx', 0, 0)  35.3 us
    all_to_all x1, blocking collectives, shards(): got = lax.all_to_all(grad, 'dp', 0, 0, axis_index_groups=FAR)  23.9 us
    all_to_all x1, blocking collectives, shards(): got = lax.all_to_all(mixed, 'ctx', 0, 0)  11.8 us
    all_to_all x1, blocking collectives, shards(): got = lax.all_to_all(grad, 'dp', 0, 0, axis_index_groups=NEAR)  11.7 us
    all_to_all x1, blocking collectives, shards(): got = lax.all_to_all(grad, 'dp', 0, 0, axis_index_groups=CLOSE)  11 us
    all_to_all x1, blocking collectives, shards(): lifted = lax.all_to_all(lifted, 'ctx', 0, 0, axis_index_groups=ACROSS)  10.7 us
    pallas_call x10, Pallas kernels, call(): pl.pallas_call(kernel, out_shape=[jax.ShapeDtypeStruct(out[1:], F32) if o...  9.53 us
    ppermute x1, starting transfers between devices, other_core(): lax.ppermute(value, 'dp', [(source, source ^ 1) for source in range(32)])  8.17 us
  transfers between devices with their start and end apart: 1, of which 1 were waited for; matrix products, arithmetic and copies ran while one was open for 0% of the time, Pallas kernels for 1%

profile of v6, /device:TPU:1, one launch (start us, length us, event | category | flops | bytes accessed | tf_op | source)
XLA Modules:
  0.0 123.2 jit_solution(7719595216163134634)
XLA Ops:
  0.6 3.7 %shard_map.95 = bf16[16,256,128]{2,1,0:T(8,128)(2,1)} custom-call(s32[1]{0:T(128)} %bitcast.core, bf16[128,768]{1,0:T(8,128)(2,1)} %bitcast.4, bf16[48,1152]{1,0:T(8,128)(2,1)} %wd.1, bf16[768,256]{1,0:T(8,128)(2,1)} %wq.1, bf16[768,256]{1,0:T(8,128)(2,1)} %wk.1, bf16[768,768]{1,0:T(8,128)(2,1)} %wv.1), custom_call_target="tpu_custom_call" | custom-call | tf_op jit(solution)/shard_map/pallas_call | solution.py:320
  4.4 0.0 copy-start.1
  4.4 0.0 copy-start.2
  4.4 0.0 copy-start.3
  4.4 21.8 %all_to_all.35.got = bf16[16,256,128]{2,1,0:T(8,128)(2,1)S(1)} all-to-all(bf16[16,256,128]{2,1,0:T(8,128)(2,1)} %shard_map.95), channel_id=1, replica_groups=mesh['dp'=32,'ctx'=16] {'ctx'}, dimensions={0} | all-to-all | bytes 2097152 | tf_op jit(solution)/shard_map/all_to_all | solution.py:367
  26.2 0.0 copy-done.1
  26.2 0.0 copy-done.2
  26.2 0.0 copy-done.3
  26.2 0.0 copy-start
  26.3 1.5 %shard_map.96 = (bf16[16,120,128]{2,1,0:T(8,128)(2,1)S(1)}, bf16[768,384]{1,0:T(8,128)(2,1)S(1)}) custom-call(bf16[16,256,128]{2,1,0:T(8,128)(2,1)S(1)} %all_to_all.35.got, bf16[128,768]{1,0:T(8,128)(2,1)S(1)} %bitcast.5, bf16[128,768]{1,0:T(8,128)(2,1)S(1)} %bitcast.6, bf16[384,768]{1,0:T(8,128)(2,1)S(1)} %copy-done.1), custom_call_target="tpu_custom_call" | custom-call | tf_op jit(solution)/shard_map/pallas_call | solution.py:320
  27.7 11.8 %all_to_all.36.got = bf16[16,120,128]{2,1,0:T(8,128)(2,1)S(1)} all-to-all(bf16[16,120,128]{2,1,0:T(8,128)(2,1)S(1)} %get-tuple-element.11), channel_id=1, replica_groups=mesh['dp'=32,'ctx'=16] {'ctx'}, dimensions={0} | all-to-all | bytes 983040 | tf_op jit(solution)/shard_map/all_to_all | solution.py:369
  39.6 0.0 copy-done
  39.6 0.6 shard_map.97
  40.2 10.7 %all_to_all.37.lifted = bf16[4,128,768]{2,1,0:T(8,128)(2,1)S(1)} all-to-all(bf16[4,128,768]{2,1,0:T(8,128)(2,1)S(1)} %shard_map.97), channel_id=1, replica_groups={{0,1,2,3},{4,5,6,7},{8,9,10,11},{12,13,14,15},{16,17,18,19},{20,21,22,2..., dimensions={0} | all-to-all | bytes 1572864 | tf_op jit(solution)/shard_map/all_to_all | solution.py:371
  51.0 1.4 %shard_map.98 = (bf16[512,128]{1,0:T(8,128)(2,1)S(1)}, bf16[16,56,128]{2,1,0:T(8,128)(2,1)S(1)}, bf16[16,56,128]{2,1,0:T(8,128)(2,1)S(1)}) custom-call(s32[1]{0:T(128)} %bitcast.core, bf16[4,128,768]{2,1,0:T(8,128)(2,1)S(1)} %all_to_all.37.lifted, bf16[16,120,128]{2,1,0:T(8,128)(2,1)S(1)} %all_to_all.36.got, bf16[768,384]{1,0:T(8,128)(2,1)S(1)} %get-tuple-element.12.filters), custom_call_target="tpu_custom_call" | custom-call | tf_op jit(solution)/shard_map/pallas_call | solution.py:320
  52.3 8.2 %collective-permute-start = (bf16[16,56,128]{2,1,0:T(8,128)(2,1)S(1)}, bf16[16,56,128]{2,1,0:T(8,128)(2,1)S(1)}, u32[]{:S(2)}, u32[]{:S(2)}) collective-permute-start(bf16[16,56,128]{2,1,0:T(8,128)(2,1)S(1)} %get-tuple-element.14), channel_id=1, source_target_pairs={{0,16},{16,0},{32,48},{48,32},{64,80},{80,64},{96,112},{112,96},{1... | collective-permute-start | bytes 688136 | tf_op jit(solution)/shard_map/ppermute | solution.py:337
  60.5 0.8 shard_map.99.begun
  61.3 0.3 collective-permute-done.came
  61.6 0.1 shard_map.100
  61.7 13.5 %all_to_all.38.got = bf16[16,128,128]{2,1,0:T(8,128)(2,1)S(1)} all-to-all(bf16[16,128,128]{2,1,0:T(8,128)(2,1)S(1)} %shard_map.100), channel_id=1, replica_groups=mesh['dp'=32,'ctx'=16] {'ctx'}, dimensions={0} | all-to-all | bytes 1048576 | tf_op jit(solution)/shard_map/all_to_all | solution.py:378
  75.1 0.5 shard_map.101
  75.6 11.7 %all_to_all.39.got = bf16[4,112,128]{2,1,0:T(8,128)(2,1)S(1)} all-to-all(bf16[4,112,128]{2,1,0:T(8,128)(2,1)S(1)} %get-tuple-element.16), channel_id=1, replica_groups={{0,32,64,96},{128,160,192,224},{256,288,320,352},{384,416,448,480},{16,..., dimensions={0} | all-to-all | bytes 229376 | tf_op jit(solution)/shard_map/all_to_all | solution.py:380
  87.3 23.9 %all_to_all.40.got = bf16[4,112,128]{2,1,0:T(8,128)(2,1)S(1)} all-to-all(bf16[4,112,128]{2,1,0:T(8,128)(2,1)S(1)} %shard_map.102), channel_id=1, replica_groups={{0,128,256,384},{32,160,288,416},{64,192,320,448},{96,224,352,480},{16,..., dimensions={0} | all-to-all | bytes 229376 | tf_op jit(solution)/shard_map/all_to_all | solution.py:382
  111.2 11.0 %all_to_all.41.got = bf16[4,112,128]{2,1,0:T(8,128)(2,1)S(1)} all-to-all(bf16[4,112,128]{2,1,0:T(8,128)(2,1)S(1)} %shard_map.103), channel_id=1, replica_groups={{0,16,32,48},{64,80,96,112},{128,144,160,176},{192,208,224,240},{256,27..., dimensions={0} | all-to-all | bytes 229376 | tf_op jit(solution)/shard_map/all_to_all | solution.py:384
  122.3 0.9 shard_map.104
  (2 shorter events, 0.0 us)
Async XLA Ops:
  4.4 21.8 %copy-start.1 = (bf16[384,768]{1,0:T(8,128)(2,1)S(1)}, bf16[384,768]{1,0:T(8,128)(2,1)}, u32[]{:S(2)}) copy-start(bf16[384,768]{1,0:T(8,128)(2,1)} %mix.3) | copy-start | bytes 1769476
  4.4 21.8 %copy-start.2 = (bf16[2,64,768]{2,1,0:T(8,128)(2,1)S(1)}, bf16[2,64,768]{2,1,0:T(8,128)(2,1)}, u32[]{:S(2)}) copy-start(bf16[2,64,768]{2,1,0:T(8,128)(2,1)} %param.8) | copy-start | bytes 589828
  4.4 21.8 %copy-start.3 = (bf16[2,64,768]{2,1,0:T(8,128)(2,1)S(1)}, bf16[2,64,768]{2,1,0:T(8,128)(2,1)}, u32[]{:S(2)}) copy-start(bf16[2,64,768]{2,1,0:T(8,128)(2,1)} %param.15) | copy-start | bytes 589828
  26.2 13.3 %copy-start = (bf16[768,768]{1,0:T(8,128)(2,1)S(1)}, bf16[768,768]{1,0:T(8,128)(2,1)}, u32[]{:S(2)}) copy-start(bf16[768,768]{1,0:T(8,128)(2,1)} %wo.3) | copy-start | bytes 3538948
  52.3 9.3 %collective-permute-start = (bf16[16,56,128]{2,1,0:T(8,128)(2,1)S(1)}, bf16[16,56,128]{2,1,0:T(8,128)(2,1)S(1)}, u32[]{:S(2)}, u32[]{:S(2)}) collective-permute-start(bf16[16,56,128]{2,1,0:T(8,128)(2,1)S(1)} %get-tuple-element.14), channel_id=1, source_target_pairs={{0,16},{16,0},{32,48},{48,32},{64,80},{80,64},{96,112},{112,96},{1... | collective-permute-start | bytes 688136 | tf_op jit(solution)/shard_map/ppermute | solution.py:337

commit v7 on v6

--- a/solution.py
+++ b/solution.py
@@ -11,7 +11,8 @@
 NEAR = [[2 * (4 * far + near) + core for near in range(4)] for core in range(2) for far in range(4)]
 FAR = [[2 * (4 * far + near) + core for far in range(4)] for core in range(2) for near in range(4)]
 CLOSE = [[4 * pair + member for member in range(4)] for pair in range(8)]
-ACROSS = [[4 * y + x for x in range(4)] for y in range(4)]
+CTX = [[16 * d + (k if d % 2 == 0 else 4 * (k % 4) + k // 4) for k in range(16)] for d in range(32)]
+ACROSS = [[member for member in group[4 * a : 4 * a + 4]] for group in CTX for a in range(4)]
 F32, BF16 = jnp.float32, jnp.bfloat16
 VMEM = pl.BlockSpec(memory_space=pltpu.VMEM)
 SMEM = pl.BlockSpec(memory_space=pltpu.SMEM)
@@ -59,6 +60,11 @@
             tile = pltpu.roll(tile, (target - start) % 128, 1)
         result = jnp.where((lane >= target) & (lane < target + count), tile, result)
     return result
+
+
+def slot(core, i):
+    turned = 4 * (i % 4) + i // 4
+    return i if turned == i else jnp.where(core[0] == 0, i, turned)
 
 
 def lower_lanes(rows):
@@ -90,7 +96,7 @@
         block.append(strips(16, [(tiles[8][16 * m : 16 * m + 16], 32 * x, 32 * m, 32) for m in range(3)]))
         block = jnp.concatenate(block, axis=0).astype(BF16)
         for y in range(4):
-            message[4 * y + x, 144:256, :] = block
+            message[4 * y + (x - y) % 4, 144:256, :] = block
     for copy in copies[2:4]:
         copy.wait()
     q = head_norm(dot(normed, wq_here[...]))
@@ -120,11 +126,12 @@
                 message[8 * s + 4 * pair + 2 + half, 128:144, :] = jnp.where(low16, swap(a), b).astype(BF16)
 
 
-def attention(got, x, cot, mix, out, filters):
+def attention(core, got, x, cot, mix, out, filters):
     low = got[:, 0:64, :].reshape(1024, 128)
     high = got[:, 64:128, :].reshape(1024, 128)
     value = jnp.concatenate([low, high], axis=1)
-    query = got[:, 128:144, :].reshape(256, 128)
+    slots = [slot(core, i) for i in range(16)]
+    query = jnp.concatenate([got[i, 128:144, :] for i in slots], axis=0)
     by_bins = moves(256, lambda r, c: c == (((r >> 1) & 15) * 16 + (r >> 5) * 2 + (r & 1)))
     query = dot(by_bins, query) * 0.25
     is_low = lower_lanes(256)
@@ -139,9 +146,10 @@
             part = mixed[32 * j : 32 * j + 32]
             first = jnp.where(low16, swap(part[16:32, 0:128]), part[0:16, 0:128])
             out[4 * block + j, 0:48, :] = jnp.concatenate([first, part[:, 128:256]], axis=0).astype(BF16)
-    first = got[:, 144:192, :].reshape(768, 128).astype(F32)
-    second = got[:, 192:240, :].reshape(768, 128).astype(F32)
-    last = got[:, 240:256, :].reshape(256, 128).astype(F32)
+    first, second, last = (
+        jnp.concatenate([got[i, start:stop, :].astype(F32) for i in slots], axis=0)
+        for start, stop in ((144, 192), (192, 240), (240, 256))
+    )
     thirds = [last, pltpu.roll(last, 96, 1), pltpu.roll(last, 64, 1)]
     last = jnp.concatenate([t[16 * i : 16 * i + 16] for i in range(16) for t in thirds], axis=0)
     filters[:, 0:128] = strips(768, [(first, 0, 0, 96)]).astype(BF16)
@@ -160,7 +168,7 @@
             rows = [
                 strips(8, [(rows[8 * m : 8 * m + 8], 0, 0, 96), (rows[24:32], 32 * m, 96, 32)]) for m in range(3)
             ]
-            out[4 * y + quarter, 96:120, :] = jnp.concatenate(rows, axis=0).astype(BF16)
+            out[4 * y + (quarter - y) % 4, 96:120, :] = jnp.concatenate(rows, axis=0).astype(BF16)
 
 
 def to_groups():
@@ -171,10 +179,10 @@
     return moves(128, lambda r, c: c == (((r >> 1) & 3) * 32 + (r >> 3) * 2 + (r & 1)))
 
 
-def attend(got, wo):
+def attend(core, got, wo):
     sent = []
     for t in range(6):
-        rows = [got[i, 48 + 8 * t : 56 + 8 * t, :].astype(F32) for i in range(16)]
+        rows = [got[slot(core, i), 48 + 8 * t : 56 + 8 * t, :].astype(F32) for i in range(16)]
         sent.append(jnp.concatenate(rows, axis=0).astype(BF16))
     sent = dot(to_groups(), jnp.concatenate(sent, axis=1))
     low16 = lower_lanes(16)
@@ -193,8 +201,8 @@
     return (sent + dot(mixed, wo[...])).astype(BF16)
 
 
-def middle(got, wo, lifted):
-    normed = layer_norm(attend(got, wo).astype(F32))
+def middle(core, got, wo, lifted):
+    normed = layer_norm(attend(core, got, wo).astype(F32))
     result = (normed * normal_cdf(normed)).astype(BF16)
     for x in range(4):
         lifted[x] = result
@@ -216,7 +224,7 @@
     gated[...] = (hidden * cdf).astype(BF16)
     pdf = jnp.exp(-0.5 * hidden * hidden) * (1.0 / math.sqrt(2.0 * math.pi))
     back = []
-    came = [jnp.concatenate([got[i, 96 + 8 * m : 104 + 8 * m, :].astype(F32) for i in range(16)], axis=0) for m in range(3)]
+    came = [jnp.concatenate([got[slot(core, i), 96 + 8 * m : 104 + 8 * m, :].astype(F32) for i in range(16)], axis=0) for m in range(3)]
     for x in range(4):
         part = [(came[x], 0, 0, 96)] if x < 3 else [(came[m], 96, 32 * m, 32) for m in range(3)]
         back.append(dot(to_groups(), strips(128, part).astype(BF16)))
@@ -241,19 +249,19 @@
         mine[d] = jnp.where(core[0] == 0, halves[0], halves[1]).astype(BF16)
 
 
-def rest(got, wo, gated, message):
-    rows = dot(to_blocks(), attend(got, wo))
+def rest(core, got, wo, gated, message):
+    rows = dot(to_blocks(), attend(core, got, wo))
     gated = [dot(to_blocks(), gated[128 * x : 128 * x + 128, :]) for x in range(4)]
     gated = [strips(128, [(gated[m], 0, 0, 96), (gated[3], 32 * m, 96, 32)]) for m in range(3)]
     for i in range(16):
         block = slice(8 * i, 8 * i + 8)
         parts = [rows[block, 128 * t : 128 * t + 128] for t in range(6)] + [g[block] for g in gated]
-        message[i, 56:128, :] = jnp.concatenate(parts, axis=0).astype(BF16)
-
-
-def joined(mine, came, begun, message):
+        message[slot(core, i), 56:128, :] = jnp.concatenate(parts, axis=0).astype(BF16)
+
+
+def joined(core, mine, came, begun, message):
     for d in range(16):
-        message[d, 0:56, :] = (mine[d].astype(F32) + came[d].astype(F32)).astype(BF16)
+        message[slot(core, d), 0:56, :] = (mine[d].astype(F32) + came[d].astype(F32)).astype(BF16)
 
 
 def summed(got, mix, grad, track):
@@ -261,7 +269,7 @@
     for x in range(4):
         part = got[x, 0:56, :].astype(F32)
         for y in range(1, 4):
-            part = part + got[4 * y + x, 0:56, :].astype(F32)
+            part = part + got[4 * y + (x - y) % 4, 0:56, :].astype(F32)
         total.append(part)
     for near in range(4):
         half = 2 * (near % 2)
@@ -271,7 +279,7 @@
     for x in range(4):
         rows = []
         for y in range(4):
-            part = got[4 * y + x, 104:128, :].astype(F32)
+            part = got[4 * y + (x - y) % 4, 104:128, :].astype(F32)
             part = [part[8 * m : 8 * m + 8] for m in range(3)]
             rows += [strips(8, [(p, 0, 0, 96)]) for p in part]
             rows.append(strips(8, [(part[m], 96, 32 * m, 32) for m in range(3)]))
@@ -364,18 +372,18 @@
         in_hbm=(1, 2, 3, 4, 5),
         limit=56,
     )
-    got = lax.all_to_all(message, "ctx", 0, 0)
-    mixed, filters = call(attention, [(16, 120, 128), (768, 384)], got, rows, slope, mixing_weight)
-    got = lax.all_to_all(mixed, "ctx", 0, 0)
-    (lifted,) = call(middle, [(4, 128, 768)], got, output_weight)
-    lifted = lax.all_to_all(lifted, "ctx", 0, 0, axis_index_groups=ACROSS)
+    got = lax.all_to_all(message, ("dp", "ctx"), 0, 0, axis_index_groups=CTX)
+    mixed, filters = call(attention, [(16, 120, 128), (768, 384)], flag, got, rows, slope, mixing_weight)
+    got = lax.all_to_all(mixed, ("dp", "ctx"), 0, 0, axis_index_groups=CTX)
+    (lifted,) = call(middle, [(4, 128, 768)], flag, got, output_weight)
+    lifted = lax.all_to_all(lifted, ("dp", "ctx"), 0, 0, axis_index_groups=ACROSS)
     gated, mine, theirs = call(
         filtered, [(512, 128), (16, 56, 128), (16, 56, 128)], flag, lifted, got, filters
     )
     came = other_core(theirs)
-    (message,) = call(rest, [(16, 128, 128)], got, output_weight, gated)
-    (message,) = call(joined, [(16, 128, 128)], mine, came, message, alias={2: 0})
-    got = lax.all_to_all(message, "ctx", 0, 0)
+    (message,) = call(rest, [(16, 128, 128)], flag, got, output_weight, gated)
+    (message,) = call(joined, [(16, 128, 128)], flag, mine, came, message, alias={3: 0})
+    got = lax.all_to_all(message, ("dp", "ctx"), 0, 0, axis_index_groups=CTX)
     grad, track = call(summed, [(4, 112, 128), (128, 768)], got, mixing_weight)
     got = lax.all_to_all(grad, "dp", 0, 0, axis_index_groups=NEAR)
     (grad,) = call(summed_again, [(4, 112, 128)], got)

time: 124 us -> 122 us (0.984)
  no operation moved by 1% of the time
where the time goes in v7:
time: 122 us
  blocking collectives  104 us (85%)
  Pallas kernels  9.55 us (8%)
  starting transfers between devices  7.7 us (6%)
    all_to_all x2, blocking collectives, shards(): got = lax.all_to_all(message, ('dp', 'ctx'), 0, 0, axis_index_groups=CTX)  34.9 us
    all_to_all x1, blocking collectives, shards(): got = lax.all_to_all(grad, 'dp', 0, 0, axis_index_groups=FAR)  23.9 us
    all_to_all x1, blocking collectives, shards(): got = lax.all_to_all(mixed, ('dp', 'ctx'), 0, 0, axis_index_groups=CTX)  12.7 us
    all_to_all x1, blocking collectives, shards(): got = lax.all_to_all(grad, 'dp', 0, 0, axis_index_groups=CLOSE)  10.9 us
    all_to_all x1, blocking collectives, shards(): lax.all_to_all(lifted, ('dp', 'ctx'), 0, 0, axis_index_groups=ACROSS)  10.7 us
    all_to_all x1, blocking collectives, shards(): got = lax.all_to_all(grad, 'dp', 0, 0, axis_index_groups=NEAR)  10.5 us
    pallas_call x10, Pallas kernels, call(): pl.pallas_call(kernel, out_shape=[jax.ShapeDtypeStruct(out[1:], F32) if o...  9.55 us
    ppermute x1, starting transfers between devices, other_core(): lax.ppermute(value, 'dp', [(source, source ^ 1) for source in range(32)])  7.7 us
  transfers between devices with their start and end apart: 1, of which 1 were waited for; matrix products, arithmetic and copies ran while one was open for 0% of the time, Pallas kernels for 1%

profile of v7, /device:TPU:1, one launch (start us, length us, event | category | flops | bytes accessed | tf_op | source)
XLA Modules:
  0.0 121.9 jit_solution(6768261556916412081)
XLA Ops:
  0.6 3.7 %shard_map.95 = bf16[16,256,128]{2,1,0:T(8,128)(2,1)} custom-call(s32[1]{0:T(128)} %bitcast.core, bf16[128,768]{1,0:T(8,128)(2,1)} %bitcast.4, bf16[48,1152]{1,0:T(8,128)(2,1)} %wd.1, bf16[768,256]{1,0:T(8,128)(2,1)} %wq.1, bf16[768,256]{1,0:T(8,128)(2,1)} %wk.1, bf16[768,768]{1,0:T(8,128)(2,1)} %wv.1), custom_call_target="tpu_custom_call" | custom-call | tf_op jit(solution)/shard_map/pallas_call | solution.py:328
  4.4 0.0 copy-start.1
  4.4 0.0 copy-start.2
  4.4 0.0 copy-start.3
  4.4 21.3 %all_to_all.35.got = bf16[16,256,128]{2,1,0:T(8,128)(2,1)S(1)} all-to-all(bf16[16,256,128]{2,1,0:T(8,128)(2,1)} %shard_map.95), channel_id=1, replica_groups={{0,1,2,3,4,5,6,7,8,9,10,11,12,13,14,15},{16,20,24,28,17,21,25,29,18,22,..., dimensions={0} | all-to-all | bytes 2097152 | tf_op jit(solution)/shard_map/all_to_all | solution.py:375
  25.8 0.0 copy-done.1
  25.8 0.0 copy-done.2
  25.8 0.0 copy-done.3
  25.8 0.0 copy-start
  25.8 1.5 %shard_map.96 = (bf16[16,120,128]{2,1,0:T(8,128)(2,1)S(1)}, bf16[768,384]{1,0:T(8,128)(2,1)S(1)}) custom-call(s32[1]{0:T(128)} %bitcast.core, bf16[16,256,128]{2,1,0:T(8,128)(2,1)S(1)} %all_to_all.35.got, bf16[128,768]{1,0:T(8,128)(2,1)S(1)} %bitcast.5, bf16[128,768]{1,0:T(8,128)(2,1)S(1)} %bitcast.6, bf16[384,768]{1,0:T(8,128)(2,1)S(1)} %copy-done.1), custom_call_target="tpu_custom_call" | custom-call | tf_op jit(solution)/shard_map/pallas_call | solution.py:328
  27.3 12.7 %all_to_all.36.got = bf16[16,120,128]{2,1,0:T(8,128)(2,1)S(1)} all-to-all(bf16[16,120,128]{2,1,0:T(8,128)(2,1)S(1)} %get-tuple-element.11), channel_id=1, replica_groups={{0,1,2,3,4,5,6,7,8,9,10,11,12,13,14,15},{16,20,24,28,17,21,25,29,18,22,..., dimensions={0} | all-to-all | bytes 983040 | tf_op jit(solution)/shard_map/all_to_all | solution.py:377
  40.0 0.0 copy-done
  40.0 0.7 shard_map.97
  40.7 10.7 %all_to_all.37.lifted = bf16[4,128,768]{2,1,0:T(8,128)(2,1)S(1)} all-to-all(bf16[4,128,768]{2,1,0:T(8,128)(2,1)S(1)} %shard_map.97), channel_id=1, replica_groups={{0,1,2,3},{4,5,6,7},{8,9,10,11},{12,13,14,15},{16,20,24,28},{17,21,25,2..., dimensions={0} | all-to-all | bytes 1572864 | tf_op jit(solution)/shard_map/all_to_all | solution.py:379
  51.4 1.4 %shard_map.98 = (bf16[512,128]{1,0:T(8,128)(2,1)S(1)}, bf16[16,56,128]{2,1,0:T(8,128)(2,1)S(1)}, bf16[16,56,128]{2,1,0:T(8,128)(2,1)S(1)}) custom-call(s32[1]{0:T(128)} %bitcast.core, bf16[4,128,768]{2,1,0:T(8,128)(2,1)S(1)} %all_to_all.37.lifted, bf16[16,120,128]{2,1,0:T(8,128)(2,1)S(1)} %all_to_all.36.got, bf16[768,384]{1,0:T(8,128)(2,1)S(1)} %get-tuple-element.12.filters), custom_call_target="tpu_custom_call" | custom-call | tf_op jit(solution)/shard_map/pallas_call | solution.py:328
  52.8 7.7 %collective-permute-start = (bf16[16,56,128]{2,1,0:T(8,128)(2,1)S(1)}, bf16[16,56,128]{2,1,0:T(8,128)(2,1)S(1)}, u32[]{:S(2)}, u32[]{:S(2)}) collective-permute-start(bf16[16,56,128]{2,1,0:T(8,128)(2,1)S(1)} %get-tuple-element.14), channel_id=1, source_target_pairs={{0,16},{16,0},{32,48},{48,32},{64,80},{80,64},{96,112},{112,96},{1... | collective-permute-start | bytes 688136 | tf_op jit(solution)/shard_map/ppermute | solution.py:345
  60.5 0.8 shard_map.99.begun
  61.3 0.3 collective-permute-done.came
  61.6 0.1 shard_map.100
  61.7 13.6 %all_to_all.38.got = bf16[16,128,128]{2,1,0:T(8,128)(2,1)S(1)} all-to-all(bf16[16,128,128]{2,1,0:T(8,128)(2,1)S(1)} %shard_map.100), channel_id=1, replica_groups={{0,1,2,3,4,5,6,7,8,9,10,11,12,13,14,15},{16,20,24,28,17,21,25,29,18,22,..., dimensions={0} | all-to-all | bytes 1048576 | tf_op jit(solution)/shard_map/all_to_all | solution.py:386
  75.3 0.5 shard_map.101
  75.8 10.5 %all_to_all.39.got = bf16[4,112,128]{2,1,0:T(8,128)(2,1)S(1)} all-to-all(bf16[4,112,128]{2,1,0:T(8,128)(2,1)S(1)} %get-tuple-element.16), channel_id=1, replica_groups={{0,32,64,96},{128,160,192,224},{256,288,320,352},{384,416,448,480},{16,..., dimensions={0} | all-to-all | bytes 229376 | tf_op jit(solution)/shard_map/all_to_all | solution.py:388
  86.3 23.9 %all_to_all.40.got = bf16[4,112,128]{2,1,0:T(8,128)(2,1)S(1)} all-to-all(bf16[4,112,128]{2,1,0:T(8,128)(2,1)S(1)} %shard_map.102), channel_id=1, replica_groups={{0,128,256,384},{32,160,288,416},{64,192,320,448},{96,224,352,480},{16,..., dimensions={0} | all-to-all | bytes 229376 | tf_op jit(solution)/shard_map/all_to_all | solution.py:390
  110.2 10.9 %all_to_all.41.got = bf16[4,112,128]{2,1,0:T(8,128)(2,1)S(1)} all-to-all(bf16[4,112,128]{2,1,0:T(8,128)(2,1)S(1)} %shard_map.103), channel_id=1, replica_groups={{0,16,32,48},{64,80,96,112},{128,144,160,176},{192,208,224,240},{256,27..., dimensions={0} | all-to-all | bytes 229376 | tf_op jit(solution)/shard_map/all_to_all | solution.py:392
  121.0 0.9 shard_map.104
  (2 shorter events, 0.0 us)
Async XLA Ops:
  4.4 21.4 %copy-start.1 = (bf16[384,768]{1,0:T(8,128)(2,1)S(1)}, bf16[384,768]{1,0:T(8,128)(2,1)}, u32[]{:S(2)}) copy-start(bf16[384,768]{1,0:T(8,128)(2,1)} %mix.3) | copy-start | bytes 1769476
  4.4 21.4 %copy-start.2 = (bf16[2,64,768]{2,1,0:T(8,128)(2,1)S(1)}, bf16[2,64,768]{2,1,0:T(8,128)(2,1)}, u32[]{:S(2)}) copy-start(bf16[2,64,768]{2,1,0:T(8,128)(2,1)} %param.8) | copy-start | bytes 589828
  4.4 21.4 %copy-start.3 = (bf16[2,64,768]{2,1,0:T(8,128)(2,1)S(1)}, bf16[2,64,768]{2,1,0:T(8,128)(2,1)}, u32[]{:S(2)}) copy-start(bf16[2,64,768]{2,1,0:T(8,128)(2,1)} %param.15) | copy-start | bytes 589828
  25.8 14.2 %copy-start = (bf16[768,768]{1,0:T(8,128)(2,1)S(1)}, bf16[768,768]{1,0:T(8,128)(2,1)}, u32[]{:S(2)}) copy-start(bf16[768,768]{1,0:T(8,128)(2,1)} %wo.3) | copy-start | bytes 3538948
  52.8 8.8 %collective-permute-start = (bf16[16,56,128]{2,1,0:T(8,128)(2,1)S(1)}, bf16[16,56,128]{2,1,0:T(8,128)(2,1)S(1)}, u32[]{:S(2)}, u32[]{:S(2)}) collective-permute-start(bf16[16,56,128]{2,1,0:T(8,128)(2,1)S(1)} %get-tuple-element.14), channel_id=1, source_target_pairs={{0,16},{16,0},{32,48},{48,32},{64,80},{80,64},{96,112},{112,96},{1... | collective-permute-start | bytes 688136 | tf_op jit(solution)/shard_map/ppermute | solution.py:345

commit v8 on v7

--- a/solution.py
+++ b/solution.py
@@ -208,7 +208,7 @@
         lifted[x] = result
 
 
-def filtered(core, lifted, got, filters, gated, mine, theirs):
+def filtered(core, lifted, got, filters, gated, slopes, theirs):
     rows = lifted[...].reshape(512, 768)
     taps = dot(rows, filters[...])
     place = lax.broadcasted_iota(jnp.int32, (512, 128), 0) & 31
@@ -236,20 +236,20 @@
         strips(512, [(slope, 32, 0, 64), (above, 0, 64, 64)]),
         strips(512, [(above, 64, 0, 32)]),
     ]
-    packed = jnp.concatenate(packed, axis=1).astype(BF16)
-    grad = dot(rows, packed, ((0,), (0,)))
+    slopes[...] = jnp.concatenate(packed, axis=1).astype(BF16)
+    gradient(core, 1, rows, slopes, theirs)
+
+
+def gradient(core, other, rows, slopes, target):
+    grad = dot(rows, slopes[...], ((0,), (0,)))
     for d in range(16):
-        halves = []
-        for half in range(2):
-            start = 48 * d + 24 * half
-            part = grad[start : start + 24]
-            last = strips(8, [(part[8 * m : 8 * m + 8, 256:384], 0, 32 * m, 32) for m in range(3)])
-            halves.append(jnp.concatenate([part[:, 0:128], part[:, 128:256], last], axis=0))
-        theirs[d] = jnp.where(core[0] == 0, halves[1], halves[0]).astype(BF16)
-        mine[d] = jnp.where(core[0] == 0, halves[0], halves[1]).astype(BF16)
-
-
-def rest(core, got, wo, gated, message):
+        low, high = grad[48 * d : 48 * d + 24], grad[48 * d + 24 : 48 * d + 48]
+        part = jnp.where(core[0] == other, low, high)
+        last = strips(8, [(part[8 * m : 8 * m + 8, 256:384], 0, 32 * m, 32) for m in range(3)])
+        target[d] = jnp.concatenate([part[:, 0:128], part[:, 128:256], last], axis=0).astype(BF16)
+
+
+def rest(core, got, wo, gated, lifted, slopes, message, mine):
     rows = dot(to_blocks(), attend(core, got, wo))
     gated = [dot(to_blocks(), gated[128 * x : 128 * x + 128, :]) for x in range(4)]
     gated = [strips(128, [(gated[m], 0, 0, 96), (gated[3], 32 * m, 96, 32)]) for m in range(3)]
@@ -257,6 +257,7 @@
         block = slice(8 * i, 8 * i + 8)
         parts = [rows[block, 128 * t : 128 * t + 128] for t in range(6)] + [g[block] for g in gated]
         message[slot(core, i), 56:128, :] = jnp.concatenate(parts, axis=0).astype(BF16)
+    gradient(core, 0, lifted[...].reshape(512, 768), slopes, mine)
 
 
 def joined(core, mine, came, begun, message):
@@ -377,11 +378,13 @@
     got = lax.all_to_all(mixed, ("dp", "ctx"), 0, 0, axis_index_groups=CTX)
     (lifted,) = call(middle, [(4, 128, 768)], flag, got, output_weight)
     lifted = lax.all_to_all(lifted, ("dp", "ctx"), 0, 0, axis_index_groups=ACROSS)
-    gated, mine, theirs = call(
-        filtered, [(512, 128), (16, 56, 128), (16, 56, 128)], flag, lifted, got, filters
+    gated, slopes, theirs = call(
+        filtered, [(512, 128), (512, 384), (16, 56, 128)], flag, lifted, got, filters
     )
     came = other_core(theirs)
-    (message,) = call(rest, [(16, 128, 128)], flag, got, output_weight, gated)
+    message, mine = call(
+        rest, [(16, 128, 128), (16, 56, 128)], flag, got, output_weight, gated, lifted, slopes
+    )
     (message,) = call(joined, [(16, 128, 128)], flag, mine, came, message, alias={3: 0})
     got = lax.all_to_all(message, ("dp", "ctx"), 0, 0, axis_index_groups=CTX)
     grad, track = call(summed, [(4, 112, 128), (128, 768)], got, mixing_weight)

time: 122 us -> 123 us (level)
  transfers between devices with their start and end apart: 1 -> 1, of which waited for: 1 -> 0; matrix products, arithmetic and copies ran while one was open for 0% -> 0% of each run, Pallas kernels for 1% -> 1%
where the time goes in v8:
time: 123 us; the launch traced here: 122 us
  blocking collectives  104 us (85%)
  Pallas kernels  9.99 us (8%)
  starting transfers between devices  7.7 us (6%)
    all_to_all x2, blocking collectives, shards(): got = lax.all_to_all(message, ('dp', 'ctx'), 0, 0, axis_index_groups=CTX)  34.9 us
    all_to_all x1, blocking collectives, shards(): got = lax.all_to_all(grad, 'dp', 0, 0, axis_index_groups=FAR)  23.9 us
    all_to_all x1, blocking collectives, shards(): got = lax.all_to_all(mixed, ('dp', 'ctx'), 0, 0, axis_index_groups=CTX)  12.7 us
    all_to_all x1, blocking collectives, shards(): got = lax.all_to_all(grad, 'dp', 0, 0, axis_index_groups=CLOSE)  10.9 us
    all_to_all x1, blocking collectives, shards(): lax.all_to_all(lifted, ('dp', 'ctx'), 0, 0, axis_index_groups=ACROSS)  10.7 us
    all_to_all x1, blocking collectives, shards(): got = lax.all_to_all(grad, 'dp', 0, 0, axis_index_groups=NEAR)  10.5 us
    pallas_call x10, Pallas kernels, call(): pl.pallas_call(kernel, out_shape=[jax.ShapeDtypeStruct(out[1:], F32) if o...  9.99 us
    ppermute x1, starting transfers between devices, other_core(): lax.ppermute(value, 'dp', [(source, source ^ 1) for source in range(32)])  7.7 us
  transfers between devices with their start and end apart: 1, of which 0 were waited for; matrix products, arithmetic and copies ran while one was open for 0% of the time, Pallas kernels for 1%

profile of v8, /device:TPU:1, one launch (start us, length us, event | category | flops | bytes accessed | tf_op | source)
XLA Modules:
  0.0 122.1 jit_solution(6514389139022674651)
XLA Ops:
  0.6 3.7 %shard_map.95 = bf16[16,256,128]{2,1,0:T(8,128)(2,1)} custom-call(s32[1]{0:T(128)} %bitcast.core, bf16[128,768]{1,0:T(8,128)(2,1)} %bitcast.4, bf16[48,1152]{1,0:T(8,128)(2,1)} %wd.1, bf16[768,256]{1,0:T(8,128)(2,1)} %wq.1, bf16[768,256]{1,0:T(8,128)(2,1)} %wk.1, bf16[768,768]{1,0:T(8,128)(2,1)} %wv.1), custom_call_target="tpu_custom_call" | custom-call | tf_op jit(solution)/shard_map/pallas_call | solution.py:329
  4.4 0.0 copy-start.1
  4.4 0.0 copy-start.2
  4.4 0.0 copy-start.3
  4.4 21.3 %all_to_all.35.got = bf16[16,256,128]{2,1,0:T(8,128)(2,1)S(1)} all-to-all(bf16[16,256,128]{2,1,0:T(8,128)(2,1)} %shard_map.95), channel_id=1, replica_groups={{0,1,2,3,4,5,6,7,8,9,10,11,12,13,14,15},{16,20,24,28,17,21,25,29,18,22,..., dimensions={0} | all-to-all | bytes 2097152 | tf_op jit(solution)/shard_map/all_to_all | solution.py:376
  25.8 0.0 copy-done.1
  25.8 0.0 copy-done.2
  25.8 0.0 copy-done.3
  25.8 0.0 copy-start
  25.8 1.5 %shard_map.96 = (bf16[16,120,128]{2,1,0:T(8,128)(2,1)S(1)}, bf16[768,384]{1,0:T(8,128)(2,1)S(1)}) custom-call(s32[1]{0:T(128)} %bitcast.core, bf16[16,256,128]{2,1,0:T(8,128)(2,1)S(1)} %all_to_all.35.got, bf16[128,768]{1,0:T(8,128)(2,1)S(1)} %bitcast.5, bf16[128,768]{1,0:T(8,128)(2,1)S(1)} %bitcast.6, bf16[384,768]{1,0:T(8,128)(2,1)S(1)} %copy-done.1), custom_call_target="tpu_custom_call" | custom-call | tf_op jit(solution)/shard_map/pallas_call | solution.py:329
  27.3 12.7 %all_to_all.36.got = bf16[16,120,128]{2,1,0:T(8,128)(2,1)S(1)} all-to-all(bf16[16,120,128]{2,1,0:T(8,128)(2,1)S(1)} %get-tuple-element.13), channel_id=1, replica_groups={{0,1,2,3,4,5,6,7,8,9,10,11,12,13,14,15},{16,20,24,28,17,21,25,29,18,22,..., dimensions={0} | all-to-all | bytes 983040 | tf_op jit(solution)/shard_map/all_to_all | solution.py:378
  40.0 0.0 copy-done
  40.0 0.7 shard_map.97
  40.7 10.7 %all_to_all.37.lifted = bf16[4,128,768]{2,1,0:T(8,128)(2,1)S(1)} all-to-all(bf16[4,128,768]{2,1,0:T(8,128)(2,1)S(1)} %shard_map.97), channel_id=1, replica_groups={{0,1,2,3},{4,5,6,7},{8,9,10,11},{12,13,14,15},{16,20,24,28},{17,21,25,2..., dimensions={0} | all-to-all | bytes 1572864 | tf_op jit(solution)/shard_map/all_to_all | solution.py:380
  51.4 1.4 %shard_map.98 = (bf16[512,128]{1,0:T(8,128)(2,1)S(1)}, bf16[512,384]{1,0:T(8,128)(2,1)S(1)}, bf16[16,56,128]{2,1,0:T(8,128)(2,1)S(1)}) custom-call(s32[1]{0:T(128)} %bitcast.core, bf16[4,128,768]{2,1,0:T(8,128)(2,1)S(1)} %all_to_all.37.lifted, bf16[16,120,128]{2,1,0:T(8,128)(2,1)S(1)} %all_to_all.36.got, bf16[768,384]{1,0:T(8,128)(2,1)S(1)} %get-tuple-element.14.filters), custom_call_target="tpu_custom_call" | custom-call | tf_op jit(solution)/shard_map/pallas_call | solution.py:329
  52.8 7.7 %collective-permute-start = (bf16[16,56,128]{2,1,0:T(8,128)(2,1)S(1)}, bf16[16,56,128]{2,1,0:T(8,128)(2,1)S(1)}, u32[]{:S(2)}, u32[]{:S(2)}) collective-permute-start(bf16[16,56,128]{2,1,0:T(8,128)(2,1)S(1)} %get-tuple-element.18), channel_id=1, source_target_pairs={{0,16},{16,0},{32,48},{48,32},{64,80},{80,64},{96,112},{112,96},{1... | collective-permute-start | bytes 688136 | tf_op jit(solution)/shard_map/ppermute | solution.py:346
  60.5 1.2 %shard_map.99 = (bf16[16,128,128]{2,1,0:T(8,128)(2,1)S(1)}, bf16[16,56,128]{2,1,0:T(8,128)(2,1)S(1)}) custom-call(s32[1]{0:T(128)} %bitcast.core, bf16[16,120,128]{2,1,0:T(8,128)(2,1)S(1)} %all_to_all.36.got, bf16[768,768]{1,0:T(8,128)(2,1)S(1)} %copy-done, bf16[512,128]{1,0:T(8,128)(2,1)S(1)} %get-tuple-element.15.gated, ...), custom_call_target="tpu_custom_call" | custom-call | tf_op jit(solution)/shard_map/pallas_call | solution.py:329
  61.8 0.0 collective-permute-done.came
  61.8 0.1 shard_map.100
  61.8 13.6 %all_to_all.38.got = bf16[16,128,128]{2,1,0:T(8,128)(2,1)S(1)} all-to-all(bf16[16,128,128]{2,1,0:T(8,128)(2,1)S(1)} %shard_map.100), channel_id=1, replica_groups={{0,1,2,3,4,5,6,7,8,9,10,11,12,13,14,15},{16,20,24,28,17,21,25,29,18,22,..., dimensions={0} | all-to-all | bytes 1048576 | tf_op jit(solution)/shard_map/all_to_all | solution.py:389
  75.4 0.5 shard_map.101
  75.9 10.5 %all_to_all.39.got = bf16[4,112,128]{2,1,0:T(8,128)(2,1)S(1)} all-to-all(bf16[4,112,128]{2,1,0:T(8,128)(2,1)S(1)} %get-tuple-element.20), channel_id=1, replica_groups={{0,32,64,96},{128,160,192,224},{256,288,320,352},{384,416,448,480},{16,..., dimensions={0} | all-to-all | bytes 229376 | tf_op jit(solution)/shard_map/all_to_all | solution.py:391
  86.5 23.9 %all_to_all.40.got = bf16[4,112,128]{2,1,0:T(8,128)(2,1)S(1)} all-to-all(bf16[4,112,128]{2,1,0:T(8,128)(2,1)S(1)} %shard_map.102), channel_id=1, replica_groups={{0,128,256,384},{32,160,288,416},{64,192,320,448},{96,224,352,480},{16,..., dimensions={0} | all-to-all | bytes 229376 | tf_op jit(solution)/shard_map/all_to_all | solution.py:393
  110.4 10.9 %all_to_all.41.got = bf16[4,112,128]{2,1,0:T(8,128)(2,1)S(1)} all-to-all(bf16[4,112,128]{2,1,0:T(8,128)(2,1)S(1)} %shard_map.103), channel_id=1, replica_groups={{0,16,32,48},{64,80,96,112},{128,144,160,176},{192,208,224,240},{256,27..., dimensions={0} | all-to-all | bytes 229376 | tf_op jit(solution)/shard_map/all_to_all | solution.py:395
  121.2 0.9 shard_map.104
  (2 shorter events, 0.0 us)
Async XLA Ops:
  4.4 21.4 %copy-start.1 = (bf16[384,768]{1,0:T(8,128)(2,1)S(1)}, bf16[384,768]{1,0:T(8,128)(2,1)}, u32[]{:S(2)}) copy-start(bf16[384,768]{1,0:T(8,128)(2,1)} %mix.3) | copy-start | bytes 1769476
  4.4 21.4 %copy-start.2 = (bf16[2,64,768]{2,1,0:T(8,128)(2,1)S(1)}, bf16[2,64,768]{2,1,0:T(8,128)(2,1)}, u32[]{:S(2)}) copy-start(bf16[2,64,768]{2,1,0:T(8,128)(2,1)} %param.8) | copy-start | bytes 589828
  4.4 21.4 %copy-start.3 = (bf16[2,64,768]{2,1,0:T(8,128)(2,1)S(1)}, bf16[2,64,768]{2,1,0:T(8,128)(2,1)}, u32[]{:S(2)}) copy-start(bf16[2,64,768]{2,1,0:T(8,128)(2,1)} %param.15) | copy-start | bytes 589828
  25.8 14.2 %copy-start = (bf16[768,768]{1,0:T(8,128)(2,1)S(1)}, bf16[768,768]{1,0:T(8,128)(2,1)}, u32[]{:S(2)}) copy-start(bf16[768,768]{1,0:T(8,128)(2,1)} %wo.3) | copy-start | bytes 3538948
  52.8 8.9 %collective-permute-start = (bf16[16,56,128]{2,1,0:T(8,128)(2,1)S(1)}, bf16[16,56,128]{2,1,0:T(8,128)(2,1)S(1)}, u32[]{:S(2)}, u32[]{:S(2)}) collective-permute-start(bf16[16,56,128]{2,1,0:T(8,128)(2,1)S(1)} %get-tuple-element.18), channel_id=1, source_target_pairs={{0,16},{16,0},{32,48},{48,32},{64,80},{80,64},{96,112},{112,96},{1... | collective-permute-start | bytes 688136 | tf_op jit(solution)/shard_map/ppermute | solution.py:346

commit v9 on v7

--- a/solution.py
+++ b/solution.py
@@ -79,11 +79,7 @@
 
 
 def front(core, x, wd, wq, wk, wv, message, x_here, wd_here, wq_here, wk_here, wv_here, semaphores):
-    pieces = [(x, x_here), (wd, wd_here)]
-    for weight, here in ((wq, wq_here), (wk, wk_here), (wv, wv_here)):
-        step = weight.shape[0] // 2
-        pieces += [(weight.at[pl.ds(step * n, step)], here.at[pl.ds(step * n, step)]) for n in range(2)]
-    copies = fetch(pieces, semaphores)
+    copies = fetch([(x, x_here), (wd, wd_here), (wq, wq_here), (wk, wk_here), (wv, wv_here)], semaphores)
     to_queries = moves(128, lambda r, c: c == ((r >> 6) * 64 + ((r >> 1) & 15) * 4 + ((r >> 5) & 1) * 2 + (r & 1)))
     copies[0].wait()
     normed = layer_norm(x_here[...].astype(F32)).astype(BF16)
@@ -97,15 +93,12 @@
         block = jnp.concatenate(block, axis=0).astype(BF16)
         for y in range(4):
             message[4 * y + (x - y) % 4, 144:256, :] = block
-    for copy in copies[2:4]:
-        copy.wait()
+    copies[2].wait()
     q = head_norm(dot(normed, wq_here[...]))
     q = dot(to_queries, q.astype(BF16))
-    for copy in copies[4:6]:
-        copy.wait()
+    copies[3].wait()
     k = head_norm(dot(normed, wk_here[...]))
-    for copy in copies[6:8]:
-        copy.wait()
+    copies[4].wait()
     v = dot(normed, wv_here[...])
     low16, low64 = lower_lanes(16), lower_lanes(64)
     for s in range(2):
@@ -368,7 +361,7 @@
         key_weight,
         value_weight,
         fetched=((128, 768), (48, 1152), (768, 256), (768, 256), (768, 768)),
-        copies=8,
+        copies=5,
         in_hbm=(1, 2, 3, 4, 5),
         limit=56,
     )

time: 122 us -> 122 us (level)
  no operation moved by 1% of the time
where the time goes in v9:
time: 122 us
  blocking collectives  104 us (85%)
  Pallas kernels  9.5 us (8%)
  starting transfers between devices  7.71 us (6%)
    all_to_all x2, blocking collectives, shards(): got = lax.all_to_all(message, ('dp', 'ctx'), 0, 0, axis_index_groups=CTX)  34.9 us
    all_to_all x1, blocking collectives, shards(): got = lax.all_to_all(grad, 'dp', 0, 0, axis_index_groups=FAR)  23.9 us
    all_to_all x1, blocking collectives, shards(): got = lax.all_to_all(mixed, ('dp', 'ctx'), 0, 0, axis_index_groups=CTX)  12.7 us
    all_to_all x1, blocking collectives, shards(): got = lax.all_to_all(grad, 'dp', 0, 0, axis_index_groups=CLOSE)  10.9 us
    all_to_all x1, blocking collectives, shards(): lax.all_to_all(lifted, ('dp', 'ctx'), 0, 0, axis_index_groups=ACROSS)  10.7 us
    all_to_all x1, blocking collectives, shards(): got = lax.all_to_all(grad, 'dp', 0, 0, axis_index_groups=NEAR)  10.5 us
    pallas_call x10, Pallas kernels, call(): pl.pallas_call(kernel, out_shape=[jax.ShapeDtypeStruct(out[1:], F32) if o...  9.5 us
    ppermute x1, starting transfers between devices, other_core(): lax.ppermute(value, 'dp', [(source, source ^ 1) for source in range(32)])  7.71 us
  transfers between devices with their start and end apart: 1, of which 1 were waited for; matrix products, arithmetic and copies ran while one was open for 0% of the time, Pallas kernels for 1%

profile of v9, /device:TPU:1, one launch (start us, length us, event | category | flops | bytes accessed | tf_op | source)
XLA Modules:
  0.0 121.9 jit_solution(12991318090961862998)
XLA Ops:
  0.6 3.7 %shard_map.95 = bf16[16,256,128]{2,1,0:T(8,128)(2,1)} custom-call(s32[1]{0:T(128)} %bitcast.core, bf16[128,768]{1,0:T(8,128)(2,1)} %bitcast.4, bf16[48,1152]{1,0:T(8,128)(2,1)} %wd.1, bf16[768,256]{1,0:T(8,128)(2,1)} %wq.1, bf16[768,256]{1,0:T(8,128)(2,1)} %wk.1, bf16[768,768]{1,0:T(8,128)(2,1)} %wv.1), custom_call_target="tpu_custom_call" | custom-call | tf_op jit(solution)/shard_map/pallas_call | solution.py:321
  4.4 0.0 copy-start.1
  4.4 0.0 copy-start.2
  4.4 0.0 copy-start.3
  4.4 21.3 %all_to_all.35.got = bf16[16,256,128]{2,1,0:T(8,128)(2,1)S(1)} all-to-all(bf16[16,256,128]{2,1,0:T(8,128)(2,1)} %shard_map.95), channel_id=1, replica_groups={{0,1,2,3,4,5,6,7,8,9,10,11,12,13,14,15},{16,20,24,28,17,21,25,29,18,22,..., dimensions={0} | all-to-all | bytes 2097152 | tf_op jit(solution)/shard_map/all_to_all | solution.py:368
  25.7 0.0 copy-done.1
  25.7 0.0 copy-done.2
  25.7 0.0 copy-done.3
  25.8 0.0 copy-start
  25.8 1.5 %shard_map.96 = (bf16[16,120,128]{2,1,0:T(8,128)(2,1)S(1)}, bf16[768,384]{1,0:T(8,128)(2,1)S(1)}) custom-call(s32[1]{0:T(128)} %bitcast.core, bf16[16,256,128]{2,1,0:T(8,128)(2,1)S(1)} %all_to_all.35.got, bf16[128,768]{1,0:T(8,128)(2,1)S(1)} %bitcast.5, bf16[128,768]{1,0:T(8,128)(2,1)S(1)} %bitcast.6, bf16[384,768]{1,0:T(8,128)(2,1)S(1)} %copy-done.1), custom_call_target="tpu_custom_call" | custom-call | tf_op jit(solution)/shard_map/pallas_call | solution.py:321
  27.2 12.7 %all_to_all.36.got = bf16[16,120,128]{2,1,0:T(8,128)(2,1)S(1)} all-to-all(bf16[16,120,128]{2,1,0:T(8,128)(2,1)S(1)} %get-tuple-element.11), channel_id=1, replica_groups={{0,1,2,3,4,5,6,7,8,9,10,11,12,13,14,15},{16,20,24,28,17,21,25,29,18,22,..., dimensions={0} | all-to-all | bytes 983040 | tf_op jit(solution)/shard_map/all_to_all | solution.py:370
  40.0 0.0 copy-done
  40.0 0.6 shard_map.97
  40.7 10.7 %all_to_all.37.lifted = bf16[4,128,768]{2,1,0:T(8,128)(2,1)S(1)} all-to-all(bf16[4,128,768]{2,1,0:T(8,128)(2,1)S(1)} %shard_map.97), channel_id=1, replica_groups={{0,1,2,3},{4,5,6,7},{8,9,10,11},{12,13,14,15},{16,20,24,28},{17,21,25,2..., dimensions={0} | all-to-all | bytes 1572864 | tf_op jit(solution)/shard_map/all_to_all | solution.py:372
  51.4 1.4 %shard_map.98 = (bf16[512,128]{1,0:T(8,128)(2,1)S(1)}, bf16[16,56,128]{2,1,0:T(8,128)(2,1)S(1)}, bf16[16,56,128]{2,1,0:T(8,128)(2,1)S(1)}) custom-call(s32[1]{0:T(128)} %bitcast.core, bf16[4,128,768]{2,1,0:T(8,128)(2,1)S(1)} %all_to_all.37.lifted, bf16[16,120,128]{2,1,0:T(8,128)(2,1)S(1)} %all_to_all.36.got, bf16[768,384]{1,0:T(8,128)(2,1)S(1)} %get-tuple-element.12.filters), custom_call_target="tpu_custom_call" | custom-call | tf_op jit(solution)/shard_map/pallas_call | solution.py:321
  52.8 7.7 %collective-permute-start = (bf16[16,56,128]{2,1,0:T(8,128)(2,1)S(1)}, bf16[16,56,128]{2,1,0:T(8,128)(2,1)S(1)}, u32[]{:S(2)}, u32[]{:S(2)}) collective-permute-start(bf16[16,56,128]{2,1,0:T(8,128)(2,1)S(1)} %get-tuple-element.14), channel_id=1, source_target_pairs={{0,16},{16,0},{32,48},{48,32},{64,80},{80,64},{96,112},{112,96},{1... | collective-permute-start | bytes 688136 | tf_op jit(solution)/shard_map/ppermute | solution.py:338
  60.5 0.8 shard_map.99.begun
  61.3 0.3 collective-permute-done.came
  61.6 0.1 shard_map.100
  61.6 13.6 %all_to_all.38.got = bf16[16,128,128]{2,1,0:T(8,128)(2,1)S(1)} all-to-all(bf16[16,128,128]{2,1,0:T(8,128)(2,1)S(1)} %shard_map.100), channel_id=1, replica_groups={{0,1,2,3,4,5,6,7,8,9,10,11,12,13,14,15},{16,20,24,28,17,21,25,29,18,22,..., dimensions={0} | all-to-all | bytes 1048576 | tf_op jit(solution)/shard_map/all_to_all | solution.py:379
  75.2 0.5 shard_map.101
  75.7 10.5 %all_to_all.39.got = bf16[4,112,128]{2,1,0:T(8,128)(2,1)S(1)} all-to-all(bf16[4,112,128]{2,1,0:T(8,128)(2,1)S(1)} %get-tuple-element.16), channel_id=1, replica_groups={{0,32,64,96},{128,160,192,224},{256,288,320,352},{384,416,448,480},{16,..., dimensions={0} | all-to-all | bytes 229376 | tf_op jit(solution)/shard_map/all_to_all | solution.py:381
  86.2 23.9 %all_to_all.40.got = bf16[4,112,128]{2,1,0:T(8,128)(2,1)S(1)} all-to-all(bf16[4,112,128]{2,1,0:T(8,128)(2,1)S(1)} %shard_map.102), channel_id=1, replica_groups={{0,128,256,384},{32,160,288,416},{64,192,320,448},{96,224,352,480},{16,..., dimensions={0} | all-to-all | bytes 229376 | tf_op jit(solution)/shard_map/all_to_all | solution.py:383
  110.2 10.9 %all_to_all.41.got = bf16[4,112,128]{2,1,0:T(8,128)(2,1)S(1)} all-to-all(bf16[4,112,128]{2,1,0:T(8,128)(2,1)S(1)} %shard_map.103), channel_id=1, replica_groups={{0,16,32,48},{64,80,96,112},{128,144,160,176},{192,208,224,240},{256,27..., dimensions={0} | all-to-all | bytes 229376 | tf_op jit(solution)/shard_map/all_to_all | solution.py:385
  121.0 0.9 shard_map.104
  (2 shorter events, 0.0 us)
Async XLA Ops:
  4.4 21.4 %copy-start.1 = (bf16[384,768]{1,0:T(8,128)(2,1)S(1)}, bf16[384,768]{1,0:T(8,128)(2,1)}, u32[]{:S(2)}) copy-start(bf16[384,768]{1,0:T(8,128)(2,1)} %mix.3) | copy-start | bytes 1769476
  4.4 21.4 %copy-start.2 = (bf16[2,64,768]{2,1,0:T(8,128)(2,1)S(1)}, bf16[2,64,768]{2,1,0:T(8,128)(2,1)}, u32[]{:S(2)}) copy-start(bf16[2,64,768]{2,1,0:T(8,128)(2,1)} %param.8) | copy-start | bytes 589828
  4.4 21.4 %copy-start.3 = (bf16[2,64,768]{2,1,0:T(8,128)(2,1)S(1)}, bf16[2,64,768]{2,1,0:T(8,128)(2,1)}, u32[]{:S(2)}) copy-start(bf16[2,64,768]{2,1,0:T(8,128)(2,1)} %param.15) | copy-start | bytes 589828
  25.8 14.2 %copy-start = (bf16[768,768]{1,0:T(8,128)(2,1)S(1)}, bf16[768,768]{1,0:T(8,128)(2,1)}, u32[]{:S(2)}) copy-start(bf16[768,768]{1,0:T(8,128)(2,1)} %wo.3) | copy-start | bytes 3538948
  52.8 8.8 %collective-permute-start = (bf16[16,56,128]{2,1,0:T(8,128)(2,1)S(1)}, bf16[16,56,128]{2,1,0:T(8,128)(2,1)S(1)}, u32[]{:S(2)}, u32[]{:S(2)}) collective-permute-start(bf16[16,56,128]{2,1,0:T(8,128)(2,1)S(1)} %get-tuple-element.14), channel_id=1, source_target_pairs={{0,16},{16,0},{32,48},{48,32},{64,80},{80,64},{96,112},{112,96},{1... | collective-permute-start | bytes 688136 | tf_op jit(solution)/shard_map/ppermute | solution.py:338

commit v10 on v7

--- a/solution.py
+++ b/solution.py
@@ -99,11 +99,11 @@
             message[4 * y + (x - y) % 4, 144:256, :] = block
     for copy in copies[2:4]:
         copy.wait()
-    q = head_norm(dot(normed, wq_here[...]))
-    q = dot(to_queries, q.astype(BF16))
     for copy in copies[4:6]:
         copy.wait()
-    k = head_norm(dot(normed, wk_here[...]))
+    both = jnp.concatenate([dot(normed, wq_here[...]), dot(normed, wk_here[...])], axis=0)
+    both = head_norm(both)
+    q, k = dot(to_queries, both[0:128].astype(BF16)), both[128:256]
     for copy in copies[6:8]:
         copy.wait()
     v = dot(normed, wv_here[...])

time: 122 us -> 122 us (level)
  no operation moved by 1% of the time
where the time goes in v10:
time: 122 us
  blocking collectives  104 us (85%)
  Pallas kernels  9.24 us (8%)
  starting transfers between devices  7.71 us (6%)
    all_to_all x2, blocking collectives, shards(): got = lax.all_to_all(message, ('dp', 'ctx'), 0, 0, axis_index_groups=CTX)  34.9 us
    all_to_all x1, blocking collectives, shards(): got = lax.all_to_all(grad, 'dp', 0, 0, axis_index_groups=FAR)  23.9 us
    all_to_all x1, blocking collectives, shards(): got = lax.all_to_all(mixed, ('dp', 'ctx'), 0, 0, axis_index_groups=CTX)  12.7 us
    all_to_all x1, blocking collectives, shards(): got = lax.all_to_all(grad, 'dp', 0, 0, axis_index_groups=CLOSE)  10.9 us
    all_to_all x1, blocking collectives, shards(): lax.all_to_all(lifted, ('dp', 'ctx'), 0, 0, axis_index_groups=ACROSS)  10.7 us
    all_to_all x1, blocking collectives, shards(): got = lax.all_to_all(grad, 'dp', 0, 0, axis_index_groups=NEAR)  10.5 us
    pallas_call x10, Pallas kernels, call(): pl.pallas_call(kernel, out_shape=[jax.ShapeDtypeStruct(out[1:], F32) if o...  9.24 us
    ppermute x1, starting transfers between devices, other_core(): lax.ppermute(value, 'dp', [(source, source ^ 1) for source in range(32)])  7.71 us
  transfers between devices with their start and end apart: 1, of which 1 were waited for; matrix products, arithmetic and copies ran while one was open for 0% of the time, Pallas kernels for 1%

profile of v10, /device:TPU:1, one launch (start us, length us, event | category | flops | bytes accessed | tf_op | source)
XLA Modules:
  0.0 121.6 jit_solution(16822555557496058039)
XLA Ops:
  0.6 3.4 %shard_map.95 = bf16[16,256,128]{2,1,0:T(8,128)(2,1)} custom-call(s32[1]{0:T(128)} %bitcast.core, bf16[128,768]{1,0:T(8,128)(2,1)} %bitcast.4, bf16[48,1152]{1,0:T(8,128)(2,1)} %wd.1, bf16[768,256]{1,0:T(8,128)(2,1)} %wq.1, bf16[768,256]{1,0:T(8,128)(2,1)} %wk.1, bf16[768,768]{1,0:T(8,128)(2,1)} %wv.1), custom_call_target="tpu_custom_call" | custom-call | tf_op jit(solution)/shard_map/pallas_call | solution.py:328
  4.1 0.0 copy-start.1
  4.1 0.0 copy-start.2
  4.1 0.0 copy-start.3
  4.1 21.3 %all_to_all.35.got = bf16[16,256,128]{2,1,0:T(8,128)(2,1)S(1)} all-to-all(bf16[16,256,128]{2,1,0:T(8,128)(2,1)} %shard_map.95), channel_id=1, replica_groups={{0,1,2,3,4,5,6,7,8,9,10,11,12,13,14,15},{16,20,24,28,17,21,25,29,18,22,..., dimensions={0} | all-to-all | bytes 2097152 | tf_op jit(solution)/shard_map/all_to_all | solution.py:375
  25.5 0.0 copy-done.1
  25.5 0.0 copy-done.2
  25.5 0.0 copy-done.3
  25.5 0.0 copy-start
  25.5 1.5 %shard_map.96 = (bf16[16,120,128]{2,1,0:T(8,128)(2,1)S(1)}, bf16[768,384]{1,0:T(8,128)(2,1)S(1)}) custom-call(s32[1]{0:T(128)} %bitcast.core, bf16[16,256,128]{2,1,0:T(8,128)(2,1)S(1)} %all_to_all.35.got, bf16[128,768]{1,0:T(8,128)(2,1)S(1)} %bitcast.5, bf16[128,768]{1,0:T(8,128)(2,1)S(1)} %bitcast.6, bf16[384,768]{1,0:T(8,128)(2,1)S(1)} %copy-done.1), custom_call_target="tpu_custom_call" | custom-call | tf_op jit(solution)/shard_map/pallas_call | solution.py:328
  27.0 12.7 %all_to_all.36.got = bf16[16,120,128]{2,1,0:T(8,128)(2,1)S(1)} all-to-all(bf16[16,120,128]{2,1,0:T(8,128)(2,1)S(1)} %get-tuple-element.11), channel_id=1, replica_groups={{0,1,2,3,4,5,6,7,8,9,10,11,12,13,14,15},{16,20,24,28,17,21,25,29,18,22,..., dimensions={0} | all-to-all | bytes 983040 | tf_op jit(solution)/shard_map/all_to_all | solution.py:377
  39.7 0.0 copy-done
  39.7 0.7 shard_map.97
  40.4 10.7 %all_to_all.37.lifted = bf16[4,128,768]{2,1,0:T(8,128)(2,1)S(1)} all-to-all(bf16[4,128,768]{2,1,0:T(8,128)(2,1)S(1)} %shard_map.97), channel_id=1, replica_groups={{0,1,2,3},{4,5,6,7},{8,9,10,11},{12,13,14,15},{16,20,24,28},{17,21,25,2..., dimensions={0} | all-to-all | bytes 1572864 | tf_op jit(solution)/shard_map/all_to_all | solution.py:379
  51.1 1.4 %shard_map.98 = (bf16[512,128]{1,0:T(8,128)(2,1)S(1)}, bf16[16,56,128]{2,1,0:T(8,128)(2,1)S(1)}, bf16[16,56,128]{2,1,0:T(8,128)(2,1)S(1)}) custom-call(s32[1]{0:T(128)} %bitcast.core, bf16[4,128,768]{2,1,0:T(8,128)(2,1)S(1)} %all_to_all.37.lifted, bf16[16,120,128]{2,1,0:T(8,128)(2,1)S(1)} %all_to_all.36.got, bf16[768,384]{1,0:T(8,128)(2,1)S(1)} %get-tuple-element.12.filters), custom_call_target="tpu_custom_call" | custom-call | tf_op jit(solution)/shard_map/pallas_call | solution.py:328
  52.5 7.7 %collective-permute-start = (bf16[16,56,128]{2,1,0:T(8,128)(2,1)S(1)}, bf16[16,56,128]{2,1,0:T(8,128)(2,1)S(1)}, u32[]{:S(2)}, u32[]{:S(2)}) collective-permute-start(bf16[16,56,128]{2,1,0:T(8,128)(2,1)S(1)} %get-tuple-element.14), channel_id=1, source_target_pairs={{0,16},{16,0},{32,48},{48,32},{64,80},{80,64},{96,112},{112,96},{1... | collective-permute-start | bytes 688136 | tf_op jit(solution)/shard_map/ppermute | solution.py:345
  60.2 0.8 shard_map.99.begun
  61.0 0.3 collective-permute-done.came
  61.3 0.1 shard_map.100
  61.4 13.6 %all_to_all.38.got = bf16[16,128,128]{2,1,0:T(8,128)(2,1)S(1)} all-to-all(bf16[16,128,128]{2,1,0:T(8,128)(2,1)S(1)} %shard_map.100), channel_id=1, replica_groups={{0,1,2,3,4,5,6,7,8,9,10,11,12,13,14,15},{16,20,24,28,17,21,25,29,18,22,..., dimensions={0} | all-to-all | bytes 1048576 | tf_op jit(solution)/shard_map/all_to_all | solution.py:386
  75.0 0.5 shard_map.101
  75.5 10.5 %all_to_all.39.got = bf16[4,112,128]{2,1,0:T(8,128)(2,1)S(1)} all-to-all(bf16[4,112,128]{2,1,0:T(8,128)(2,1)S(1)} %get-tuple-element.16), channel_id=1, replica_groups={{0,32,64,96},{128,160,192,224},{256,288,320,352},{384,416,448,480},{16,..., dimensions={0} | all-to-all | bytes 229376 | tf_op jit(solution)/shard_map/all_to_all | solution.py:388
  86.0 23.9 %all_to_all.40.got = bf16[4,112,128]{2,1,0:T(8,128)(2,1)S(1)} all-to-all(bf16[4,112,128]{2,1,0:T(8,128)(2,1)S(1)} %shard_map.102), channel_id=1, replica_groups={{0,128,256,384},{32,160,288,416},{64,192,320,448},{96,224,352,480},{16,..., dimensions={0} | all-to-all | bytes 229376 | tf_op jit(solution)/shard_map/all_to_all | solution.py:390
  109.9 10.9 %all_to_all.41.got = bf16[4,112,128]{2,1,0:T(8,128)(2,1)S(1)} all-to-all(bf16[4,112,128]{2,1,0:T(8,128)(2,1)S(1)} %shard_map.103), channel_id=1, replica_groups={{0,16,32,48},{64,80,96,112},{128,144,160,176},{192,208,224,240},{256,27..., dimensions={0} | all-to-all | bytes 229376 | tf_op jit(solution)/shard_map/all_to_all | solution.py:392
  120.7 0.9 shard_map.104
  (2 shorter events, 0.0 us)
Async XLA Ops:
  4.1 21.4 %copy-start.1 = (bf16[384,768]{1,0:T(8,128)(2,1)S(1)}, bf16[384,768]{1,0:T(8,128)(2,1)}, u32[]{:S(2)}) copy-start(bf16[384,768]{1,0:T(8,128)(2,1)} %mix.3) | copy-start | bytes 1769476
  4.1 21.4 %copy-start.2 = (bf16[2,64,768]{2,1,0:T(8,128)(2,1)S(1)}, bf16[2,64,768]{2,1,0:T(8,128)(2,1)}, u32[]{:S(2)}) copy-start(bf16[2,64,768]{2,1,0:T(8,128)(2,1)} %param.8) | copy-start | bytes 589828
  4.1 21.4 %copy-start.3 = (bf16[2,64,768]{2,1,0:T(8,128)(2,1)S(1)}, bf16[2,64,768]{2,1,0:T(8,128)(2,1)}, u32[]{:S(2)}) copy-start(bf16[2,64,768]{2,1,0:T(8,128)(2,1)} %param.15) | copy-start | bytes 589828
  25.5 14.2 %copy-start = (bf16[768,768]{1,0:T(8,128)(2,1)S(1)}, bf16[768,768]{1,0:T(8,128)(2,1)}, u32[]{:S(2)}) copy-start(bf16[768,768]{1,0:T(8,128)(2,1)} %wo.3) | copy-start | bytes 3538948
  52.5 8.8 %collective-permute-start = (bf16[16,56,128]{2,1,0:T(8,128)(2,1)S(1)}, bf16[16,56,128]{2,1,0:T(8,128)(2,1)S(1)}, u32[]{:S(2)}, u32[]{:S(2)}) collective-permute-start(bf16[16,56,128]{2,1,0:T(8,128)(2,1)S(1)} %get-tuple-element.14), channel_id=1, source_target_pairs={{0,16},{16,0},{32,48},{48,32},{64,80},{80,64},{96,112},{112,96},{1... | collective-permute-start | bytes 688136 | tf_op jit(solution)/shard_map/ppermute | solution.py:345
